TPU v7x, 128 devices: a whole 4x4x4 slice. The times are simulated.
128 devices in a mesh: dp: 2 (over x_lo), label: 64 (over y, z, x_hi, core).
Axes of the slice: x: 4 (x_hi: 2, x_lo: 2; x = x_hi * 2 + x_lo), y: 4, z: 4, core: 2. Of those that a mesh axis runs over, the one named last changes fastest.
Arguments:
- hidden: bfloat16 [2048, 768], P(('dp', 'label')), may hold values from -6 to 6
- enc_weight: bfloat16 [768, 768], replicated, may hold values from -0.21875 to 0.21875
- cls_weight: bfloat16 [768, 196608], P(None, 'label'), may hold values from -0.21875 to 0.21875
- targets: int32 [2048, 196608], P('dp', 'label'), may hold values 0 or 1
Outputs:
- cls_grad: bfloat16 [768, 196608], P('dp', 'label')
- input_grad: bfloat16 [2048, 768], P(('dp', 'label'))
- enc_grad: float32 [768, 768], replicated
All inputs are finite; a program needn't handle non-finite values. No bound on the sum of `targets` on one device may be relied on, other than what follows from the above.
Results may differ from a plain program's by a relative error of at most 0.012.
Values may be sent and summed in bfloat16 or wider, within the bound.
No kernel may reach another device: no remote copies, remote signals or barrier semaphores. Data moves between devices by JAX's collectives and lax.ppermute only.
A program may use at most 128 MiB of HBM per device.

v0:
```python
import jax
import jax.numpy as jnp
from jax import lax
from jax.sharding import PartitionSpec as P


def layer_out(rows_in, enc_weight):
    pre = jnp.dot(rows_in, enc_weight, preferred_element_type=jnp.float32)
    act = jnp.tanh(pre)
    return (act, (rows_in.astype(jnp.float32) + act).astype(jnp.bfloat16))


def body(hidden, enc_weight, cls_weight, targets):
    batch = hidden.shape[0] * lax.axis_size("dp") * lax.axis_size("label")
    scale = 1.0 / jnp.sqrt(jnp.float32(batch))
    act, emb = layer_out(hidden, enc_weight)
    emb_all = lax.all_gather(emb, "label", axis=0, tiled=True)
    logits = jnp.dot(emb_all, cls_weight, preferred_element_type=jnp.float32)
    err = ((jax.nn.sigmoid(logits) - targets.astype(jnp.float32)) * scale).astype(jnp.bfloat16)
    cls_grad = lax.psum_scatter(
        lax.dot_general(
            emb_all, err, (((0,), (0,)), ((), ())), preferred_element_type=jnp.float32
        ).astype(jnp.bfloat16),
        "dp",
        scatter_dimension=0,
        tiled=True,
    )
    emb_grad = lax.psum_scatter(
        lax.dot_general(
            err, cls_weight, (((1,), (1,)), ((), ())), preferred_element_type=jnp.float32
        ),
        "label",
        scatter_dimension=0,
        tiled=True,
    )
    pre_grad = (emb_grad * (1.0 - act * act)).astype(jnp.bfloat16)
    back = lax.dot_general(
        pre_grad, enc_weight, (((1,), (1,)), ((), ())), preferred_element_type=jnp.float32
    )
    input_grad = (emb_grad + back).astype(jnp.bfloat16)
    enc_local = lax.dot_general(
        hidden, pre_grad, (((0,), (0,)), ((), ())), preferred_element_type=jnp.float32
    )
    enc_grad = lax.psum(enc_local, ("dp", "label"))
    return (cls_grad, input_grad, enc_grad)


def solution(mesh):
    placed = (P(("dp", "label"), None), P(), P(None, "label"), P("dp", "label"))
    return jax.shard_map(
        body,
        mesh=mesh,
        in_specs=placed,
        out_specs=(P("dp", "label"), P(("dp", "label"), None), P()),
        check_vma=False,
    )
```

profile of v0, /device:TPU:0, one launch (start us, length us, event | category | flops | bytes accessed | tf_op | source)
XLA Modules:
  0.0 472.5 jit_solution(11581572200503095745)
XLA Ops:
  7.2 0.0 copy-start
  7.2 0.0 all-gather.2.cloned.1.call-start
  7.2 1.2 copy-done
  8.4 1.7 add_convert_fusion
  10.2 0.0 all-gather.2.cloned.1.call-update
  10.2 0.0 reduce-scatter.5.cloned.1.call-start
  10.2 70.9 %all-gather.2.cloned.1.call-done = bf16[1024,768]{1,0:T(8,128)(2,1)} async-done(((bf16[16,768]{1,0:T(8,128)(2,1)}), bf16[1024,768]{1,0:T(8,128)(2,1)}) %all-gather.2.cloned.1.call-update) | async-done | bytes 1572880 | tf_op jit(solution)/shard_map/all_gather | solution.py:17
  81.1 10.3 %multiply_convert_fusion = bf16[1024,3072]{1,0:T(8,128)(2,1)S(1)} fusion(s32[1024,3072]{1,0:T(8,128)} %param.7, bf16[1024,768]{1,0:T(8,128)(2,1)} %all-gather.2.cloned.1.call-done, bf16[768,3072]{1,0:T(8,128)(2,1)} %param.6), kind=kOutput, calls=%fused_computation | convolution fusion | flops 4853858304 | bytes 25165824 | tf_op jit(solution)/shard_map/dot_general | solution.py:18
  91.4 0.0 copy-start.4
  91.4 2.7 copy-done.4
  94.1 0.0 copy-start.2
  94.1 9.1 %fusion.3 = f32[1024,768]{1,0:T(8,128)} fusion(bf16[1024,3072]{1,0:T(8,128)(2,1)S(1)} %multiply_convert_fusion, bf16[768,3072]{1,0:T(8,128)(2,1)} %param.6), kind=kOutput, calls=%fused_computation.10 | convolution fusion | flops 4831838208 | bytes 14155776 | tf_op jit(solution)/shard_map/dot_general | solution.py:29
  103.2 0.0 copy-start.3
  103.2 0.0 reduce-scatter.5.cloned.1.call-update
  103.2 0.0 all-reduce.2.cloned.1.call-start
  103.3 145.3 %reduce-scatter.5.cloned.1.call-done = f32[16,768]{1,0:T(8,128)} async-done(((f32[1024,768]{1,0:T(8,128)}), f32[16,768]{1,0:T(8,128)}) %reduce-scatter.5.cloned.1.call-update) | async-done | bytes 49168 | tf_op jit(solution)/shard_map/reduce_scatter | solution.py:28
  248.5 0.0 copy-done.2
  248.5 2.7 convolution_bitcast_fusion
  251.3 0.0 all-reduce.2.cloned.1.call-update
  251.3 0.0 reduce-scatter.3.cloned.1.call-start
  251.3 0.0 copy-done.3
  251.3 9.7 %convolution_convert_fusion = bf16[768,3072]{1,0:T(8,128)(2,1)} fusion(bf16[1024,768]{1,0:T(8,128)(2,1)S(1)} %copy-done.3, bf16[1024,3072]{1,0:T(8,128)(2,1)} %copy-done.4), kind=kOutput, calls=%fused_computation.1 | convolution fusion | flops 4834197504 | bytes 12582912 | tf_op jit(solution)/shard_map/dot_general | solution.py:21
  261.0 0.0 copy-start.1
  261.0 0.0 reduce-scatter.3.cloned.1.call-update
  261.0 0.8 copy-done.1
  261.8 1.1 fusion
  262.9 139.5 %all-reduce.2.cloned.1.call-done = f32[768,768]{0,1:T(8,128)} async-done(((f32[768,768]{0,1:T(8,128)}), f32[768,768]{0,1:T(8,128)}) %all-reduce.2.cloned.1.call-update) | async-done | bytes 2359312 | tf_op jit(solution)/shard_map/psum | solution.py:44
  402.4 3.0 copy.7
  405.4 60.5 %reduce-scatter.3.cloned.1.call-done = bf16[384,3072]{1,0:T(8,128)(2,1)} async-done(((bf16[768,3072]{1,0:T(8,128)(2,1)}), bf16[384,3072]{1,0:T(8,128)(2,1)}) %reduce-scatter.3.cloned.1.call-update) | async-done | bytes 2359312 | tf_op jit(solution)/shard_map/reduce_scatter | solution.py:20
Async XLA Ops:
  7.2 1.3 copy-start
  7.2 74.0 %all-gather.2.cloned.1.call-start = ((), (), s32[]{:S(2)}) async-start(), calls=%async_computation.2 | async-start | bytes 1597440 | tf_op jit(solution)/shard_map/all_gather | solution.py:17
  10.2 238.4 %reduce-scatter.5.cloned.1.call-start = ((), (), s32[]{:S(2)}) async-start(), calls=%async_computation.4 | async-start | bytes 3194880 | tf_op jit(solution)/shard_map/reduce_scatter | solution.py:28
  91.4 2.7 copy-start.4
  94.1 154.5 %copy-start.2 = (bf16[16,768]{1,0:T(8,128)(2,1)S(1)}, bf16[16,768]{1,0:T(8,128)(2,1)}, u32[]{:S(2)}) copy-start(bf16[16,768]{1,0:T(8,128)(2,1)} %param.4) | copy-start | bytes 73732
  103.2 148.1 %copy-start.3 = (bf16[1024,768]{1,0:T(8,128)(2,1)S(1)}, bf16[1024,768]{1,0:T(8,128)(2,1)}, u32[]{:S(2)}) copy-start(bf16[1024,768]{1,0:T(8,128)(2,1)} %all-gather.2.cloned.1.call-done) | copy-start | bytes 4718596
  103.2 299.1 %all-reduce.2.cloned.1.call-start = ((), (), s32[]{:S(2)}) async-start(), calls=%async_computation.5 | async-start | bytes 4718592 | tf_op jit(solution)/shard_map/psum | solution.py:44
  251.3 214.6 %reduce-scatter.3.cloned.1.call-start = ((), (), s32[]{:S(2)}) async-start(), calls=%async_computation.3 | async-start | bytes 7077888 | tf_op jit(solution)/shard_map/reduce_scatter | solution.py:20
  261.0 0.8 copy-start.1
Sparse Core Ops, SparseCore 0:
  11.8 69.3 all-gather.1
  103.3 145.1 reduce-scatter.4
  253.9 148.4 all-reduce.1
  405.3 60.5 reduce-scatter.2
where the time goes:
time: 474 us; the launch traced here: 472 us
  waiting for transfers between devices  416 us (88%)
  matrix products  34.5 us (7%)
  between operations  13.8 us (3%)
  local copies, waits for them, and re-layouts  7.7 us (2%)
    reduce_scatter x1, waiting for transfers between devices, body(): lax.psum_scatter(lax.dot_general(err, cls_weight, (((1,), (1,)), ((), ())...  145 us
    psum x1, waiting for transfers between devices, body(): enc_grad = lax.psum(enc_local, ('dp', 'label'))  139 us
    all_gather x1, waiting for transfers between devices, body(): emb_all = lax.all_gather(emb, 'label', axis=0, tiled=True)  70.9 us
    reduce_scatter x1, waiting for transfers between devices, body(): lax.psum_scatter(lax.dot_general(emb_all, err, (((0,), (0,)), ((), ())),...  60.5 us
    dot_general x1, matrix products, body(): logits = jnp.dot(emb_all, cls_weight, preferred_element_type=jnp.float32)  10.3 us
    dot_general x1, matrix products, body(): lax.dot_general(emb_all, err, (((0,), (0,)), ((), ())), preferred_element...  9.67 us
  transfers between devices with their start and end apart: 4, of which 4 were waited for; matrix products, arithmetic and copies ran while one was open for 3% of the time, Pallas kernels for 0%

commit v1 on v0

v1 whole, which is shorter than its diff:
```python
import jax
import jax.numpy as jnp
from jax import lax
from jax.sharding import Mesh, PartitionSpec as P

F32 = jnp.float32
BF16 = jnp.bfloat16
AXES = ("xl", "y", "z", "xh", "c")
N_CHUNK = 4


def dot(a, b, dims):
    return lax.dot_general(a, b, (dims, ((), ())), preferred_element_type=F32)


def swap(x, axis):
    return lax.ppermute(x, axis, [(0, 1), (1, 0)])


def body(hidden, enc_weight, cls_weight, targets):
    core = lax.axis_index("c")
    dp = lax.axis_index("xl")
    rows, width = hidden.shape
    labels = cls_weight.shape[1]
    half = width // 2
    n_peer = 32
    scale = 1.0 / jnp.sqrt(F32(2048))

    mine = lax.all_to_all(
        jnp.broadcast_to(hidden[None], (n_peer, rows, width)), ("y", "z", "xh"), 0, 0, tiled=True
    )
    other = swap(mine, "c")
    pair = jnp.where(core == 0, jnp.stack([mine, other], 1), jnp.stack([other, mine], 1))
    hid = pair.reshape(-1, width)
    act = jnp.tanh(dot(hid, enc_weight, ((1,), (0,))))
    emb = (hid.astype(F32) + act).astype(BF16)
    slope = 1.0 - act * act
    emb_send = lax.dynamic_slice(emb, (0, (1 - dp) * half), (emb.shape[0], half))
    emb_keep = lax.dynamic_slice(emb, (0, dp * half), (emb.shape[0], half))

    step = labels // N_CHUNK
    part = jnp.zeros((emb.shape[0], width), F32)
    errs, arrived = [], []
    for j in range(N_CHUNK):
        w = cls_weight[:, j * step : (j + 1) * step]
        t = targets[:, j * step : (j + 1) * step]
        logits = dot(emb, w, ((1,), (0,)))
        err = ((jax.nn.sigmoid(logits) - t.astype(F32)) * scale).astype(BF16)
        errs.append(err)
        arrived.append(swap(dot(emb_send, err, ((0,), (0,))).astype(BF16), "xl"))
        part = part + dot(err, w, ((1,), (1,)))

    enc = dot(hid, (part * slope).astype(BF16), ((0,), (0,))).astype(BF16)
    enc = enc.reshape(2, half, width)
    enc_mine = enc[core].astype(F32) + swap(enc[1 - core], "c").astype(F32)
    enc_mine = enc_mine.astype(BF16).reshape(16, half // 16, width)
    enc_mine = lax.all_to_all(enc_mine, ("y", "z"), 0, 0, tiled=True)
    enc_mine = jnp.sum(enc_mine.astype(F32), 0).astype(BF16)
    enc_x = lax.all_to_all(
        jnp.broadcast_to(enc_mine[None], (4,) + enc_mine.shape), ("xl", "xh"), 0, 0, tiled=True
    )
    enc_x = jnp.sum(enc_x.astype(F32), 0).astype(BF16)
    enc_half = lax.all_to_all(
        jnp.broadcast_to(enc_x[None], (16,) + enc_x.shape), ("y", "z"), 0, 0, tiled=True
    ).reshape(half, width)
    enc_rest = swap(enc_half, "c")
    enc_grad = jnp.where(
        core == 0, jnp.concatenate([enc_half, enc_rest]), jnp.concatenate([enc_rest, enc_half])
    ).astype(F32)

    sums = part.astype(BF16).reshape(n_peer, 2, rows, width)
    sums_mine = sums[:, core].astype(F32) + swap(sums[:, 1 - core], "c").astype(F32)
    got = lax.all_to_all(sums_mine.astype(BF16), ("y", "z", "xh"), 0, 0, tiled=True)
    emb_grad = jnp.sum(got.astype(F32), 0)
    act_own = jnp.tanh(dot(hidden, enc_weight, ((1,), (0,))))
    pre_grad = (emb_grad * (1.0 - act_own * act_own)).astype(BF16)
    input_grad = (emb_grad + dot(pre_grad, enc_weight, ((1,), (1,)))).astype(BF16)

    kept = [dot(emb_keep, e, ((0,), (0,))) for e in errs]
    cls_grad = jnp.concatenate(
        [(k + a.astype(F32)).astype(BF16) for k, a in zip(kept, arrived)], 1
    )
    return (cls_grad, input_grad, enc_grad)


def solution(mesh):
    grid = Mesh(mesh.devices.reshape(2, 4, 4, 2, 2), AXES)
    label = AXES[1:]
    placed = (P(AXES, None), P(), P(None, label), P("xl", label))
    return jax.shard_map(
        body,
        mesh=grid,
        in_specs=placed,
        out_specs=(P("xl", label), P(AXES, None), P()),
        check_vma=False,
    )
```

time: 474 us -> 155 us (0.33)
  waiting for transfers between devices: 416 us -> 47 us
  blocking collectives: 0 us -> 27.2 us
  starting transfers between devices: 0.16 us -> 19.5 us
  between operations: 13.8 us -> 1.01 us
  other arithmetic: 0 us -> 9.2 us
  matrix products: 34.5 us -> 40.7 us
    reduce_scatter x2 -> x0, waiting for transfers between devices: 206 us -> none  [the longest x1 145 us: body(): lax.psum_scatter(lax.dot_general(err, cls_weight, (((1,), (1,)), ((), ())...]
    psum x1 -> x0, waiting for transfers between devices: 139 us -> none  [body(): enc_grad = lax.psum(enc_local, ('dp', 'label'))]
    all_gather x1 -> x0, waiting for transfers between devices: 70.9 us -> none  [body(): emb_all = lax.all_gather(emb, 'label', axis=0, tiled=True)]
    all_to_all x0 -> x4, waiting for transfers between devices: none -> 44.7 us  [the longest x1 26 us: body(): lax.all_to_all(jnp.broadcast_to(enc_mine[None], (4,) + enc_mine.shape), (...]
    all_to_all x0 -> x1, blocking collectives: none -> 27.2 us  [body(): lax.all_to_all(jnp.broadcast_to(hidden[None], (n_peer, rows, width)), ('y...]
    all_to_all x0 -> x4, starting transfers between devices: none -> 15.1 us  [the longest x1 4.61 us: body(): lax.all_to_all(sums_mine.astype(BF16), ('y', 'z', 'xh'), 0, 0, tiled=True)]
    convert_element_type x0 -> x3, other arithmetic: none -> 7.12 us  [the longest x1 2.88 us: body(): enc_grad = jnp.where(core == 0, jnp.concatenate([enc_half, enc_rest]), jn...]
    dot_general x6 -> x19, matrix products: 34.5 us -> 40.7 us  [dot(): return lax.dot_general(a, b, (dims, ((), ())), preferred_element_type=F32)]
  transfers between devices with their start and end apart: 4 -> 12, of which waited for: 4 -> 5; matrix products, arithmetic and copies ran while one was open for 3% -> 21% of each run, Pallas kernels for 0% -> 0%
where the time goes in v1:
time: 155 us; the launch traced here: 154 us
  waiting for transfers between devices  47 us (30%)
  matrix products  40.7 us (26%)
  blocking collectives  27.2 us (18%)
  starting transfers between devices  19.5 us (13%)
  local copies, waits for them, and re-layouts  9.43 us (6%)
  other arithmetic  9.2 us (6%)
    dot_general x19, matrix products, dot(): return lax.dot_general(a, b, (dims, ((), ())), preferred_element_type=F32)  40.7 us
    all_to_all x1, blocking collectives, body(): lax.all_to_all(jnp.broadcast_to(hidden[None], (n_peer, rows, width)), ('y...  27.2 us
    all_to_all x1, waiting for transfers between devices, body(): lax.all_to_all(jnp.broadcast_to(enc_mine[None], (4,) + enc_mine.shape), (...  26 us
    all_to_all x1, waiting for transfers between devices, body(): lax.all_to_all(sums_mine.astype(BF16), ('y', 'z', 'xh'), 0, 0, tiled=True)  8.35 us
    unnamed x42, local copies, waits for them, and re-layouts  6.03 us
    all_to_all x1, waiting for transfers between devices, body(): lax.all_to_all(jnp.broadcast_to(enc_x[None], (16,) + enc_x.shape), ('y',...  6.03 us
    all_to_all x1, starting transfers between devices, body(): lax.all_to_all(sums_mine.astype(BF16), ('y', 'z', 'xh'), 0, 0, tiled=True)  4.61 us
    ppermute x8, starting transfers between devices, swap(): return lax.ppermute(x, axis, [(0, 1), (1, 0)])  4.35 us
  transfers between devices with their start and end apart: 12, of which 5 were waited for; matrix products, arithmetic and copies ran while one was open for 21% of the time, Pallas kernels for 0%

profile of v1, /device:TPU:0, one launch (start us, length us, event | category | flops | bytes accessed | tf_op | source)
XLA Modules:
  0.0 154.0 jit_solution(8445095013351137181)
XLA Ops:
  0.6 0.9 broadcast_in_dim.6
  1.5 27.2 %all_to_all.25 = bf16[32,16,768]{2,1,0:T(8,128)(2,1)S(1)} all-to-all(bf16[32,16,768]{2,1,0:T(8,128)(2,1)S(1)} %broadcast_in_dim.6), channel_id=1, replica_groups=mesh['xl'=2,'y'=4,'z'=4,'xh'=2,'c'=2] {'y','z','xh'}, dimensions={0} | all-to-all | bytes 1572864 | tf_op jit(solution)/shard_map/all_to_all | solution.py:29
  28.7 2.3 %collective-permute-done = bf16[32,16,768]{2,1,0:T(8,128)(2,1)S(1)} collective-permute-done((bf16[32,16,768]{2,1,0:T(8,128)(2,1)S(1)}, bf16[32,16,768]{2,1,0:T(8,128)(2,1)S(1)}, u32[]{:S(2)}, u32[]{:S(2)}) %collective-permute-start) | collective-permute-done | bytes 786464 | tf_op jit(solution)/shard_map/ppermute | solution.py:17
  31.0 0.1 maximum_select_fusion
  31.2 3.1 %add_convert_fusion = (bf16[1024,768]{1,0:T(8,128)(2,1)S(1)}, f32[1024,768]{1,0:T(8,128)}) fusion(bf16[32,2,16,768]{3,2,1,0:T(8,128)(2,1)S(1)} %maximum_select_fusion, bf16[1024,768]{1,0:T(8,128)(2,1)S(1)} %bitcast.46, bf16[768,768]{1,0:T(8,128)(2,1)S(1)} %copy-done), kind=kOutput, calls=%fused_computation.6 | convolution fusion | flops 1210318848 | bytes 9043968 | tf_op jit(solution)/shard_map/dot_general | solution.py:13
  34.3 4.5 %copy-done.17 = s32[1024,3072]{1,0:T(8,128)S(1)} copy-done((s32[1024,3072]{1,0:T(8,128)S(1)}, s32[1024,3072]{1,0:T(8,128)}, u32[]{:S(2)}) %copy-start.17) | copy-done | bytes 12582936
  38.8 1.7 %multiply_convert_fusion.1 = bf16[1024,768]{1,0:T(8,128)(2,1)S(1)} fusion(s32[1024,3072]{1,0:T(8,128)S(1)} %copy-done.17, bf16[1024,768]{1,0:T(8,128)(2,1)S(1)} %get-tuple-element.3, bf16[768,3072]{1,0:T(8,128)(2,1)S(1)} %bitcast.52), kind=kOutput, calls=%fused_computation.2 | convolution fusion | flops 1213464576 | bytes 7471104 | tf_op jit(solution)/shard_map/dot_general | solution.py:13
  40.5 1.7 %multiply_convert_fusion.2 = bf16[1024,768]{1,0:T(8,128)(2,1)S(1)} fusion(s32[1024,3072]{1,0:T(8,128)S(1)} %copy-done.17, bf16[1024,768]{1,0:T(8,128)(2,1)S(1)} %get-tuple-element.3, bf16[768,3072]{1,0:T(8,128)(2,1)S(1)} %bitcast.52), kind=kOutput, calls=%fused_computation.3 | convolution fusion | flops 1213464576 | bytes 7471104 | tf_op jit(solution)/shard_map/dot_general | solution.py:13
  42.3 1.7 %multiply_convert_fusion.3 = bf16[1024,768]{1,0:T(8,128)(2,1)S(1)} fusion(s32[1024,3072]{1,0:T(8,128)S(1)} %copy-done.17, bf16[1024,768]{1,0:T(8,128)(2,1)S(1)} %get-tuple-element.3, bf16[768,3072]{1,0:T(8,128)(2,1)S(1)} %bitcast.52), kind=kOutput, calls=%fused_computation.4 | convolution fusion | flops 1213464576 | bytes 7471104 | tf_op jit(solution)/shard_map/dot_general | solution.py:13
  44.0 1.7 %multiply_convert_fusion.4 = bf16[1024,768]{1,0:T(8,128)(2,1)S(1)} fusion(s32[1024,3072]{1,0:T(8,128)S(1)} %copy-done.17, bf16[1024,768]{1,0:T(8,128)(2,1)S(1)} %get-tuple-element.3, bf16[768,3072]{1,0:T(8,128)(2,1)S(1)} %bitcast.52), kind=kOutput, calls=%fused_computation.5 | convolution fusion | flops 1213464576 | bytes 7471104 | tf_op jit(solution)/shard_map/dot_general | solution.py:13
  45.8 1.4 fusion.13
  47.3 1.4 fusion.19
  48.7 1.4 fusion.16
  50.1 1.5 fusion.53
  51.6 0.4 copy-done.18
  52.0 1.8 %fusion.3 = bf16[768,768]{1,0:T(8,128)(2,1)S(1)} fusion(bf16[1024,768]{1,0:T(8,128)(2,1)S(1)} %bitcast.47, f32[1024,768]{1,0:T(8,128)S(1)} %get-tuple-element.6, f32[1024,768]{1,0:T(8,128)S(1)} %copy-done.18), kind=kOutput, calls=%fused_computation.14 | convolution fusion | flops 1211695104 | bytes 9043968 | tf_op jit(solution)/shard_map/dot_general | solution.py:13
  53.8 1.0 copy-done.14
  54.9 0.2 collective-permute-start.6
  55.1 3.5 %convolution_convert_fusion = bf16[384,768]{1,0:T(8,128)(2,1)} fusion(bf16[1024,768]{1,0:T(8,128)(2,1)} %copy-done.1, bf16[1024,768]{1,0:T(8,128)(2,1)} %copy-done.2, s32[]{:T(128)S(6)} %select_n.38), kind=kOutput, calls=%fused_computation.15 | convolution fusion | flops 604274688 | bytes 2949124 | tf_op jit(solution)/shard_map/dot_general | solution.py:13
  58.5 0.6 collective-permute-start.4
  59.2 1.7 %convolution_convert_fusion.1 = bf16[384,768]{1,0:T(8,128)(2,1)} fusion(bf16[1024,768]{1,0:T(8,128)(2,1)S(1)} %copy-done.13, bf16[1024,768]{1,0:T(8,128)(2,1)S(1)} %copy-done.3, s32[]{:T(128)S(6)} %select_n.38), kind=kOutput, calls=%fused_computation.16 | convolution fusion | flops 604274688 | bytes 2949124 | tf_op jit(solution)/shard_map/dot_general | solution.py:13
  60.9 1.4 collective-permute-start.3
  62.3 2.0 %fusion.5 = bf16[384,768]{1,0:T(8,128)(2,1)} fusion(bf16[384,768]{1,0:T(8,128)(2,1)} %collective-permute-done.6, bf16[2,384,768]{2,1,0:T(8,128)(2,1)S(1)} %bitcast.49, s32[]{:T(128)S(6)} %select_n.39), kind=kLoop, calls=%fused_computation.22 | loop fusion | flops 1179648 | bytes 1769476 | tf_op jit(solution)/shard_map/convert_element_type | solution.py:56
  64.3 3.6 %all-to-all-start.2 = ((bf16[16,24,768]{2,1,0:T(8,128)(2,1)}), bf16[16,24,768]{2,1,0:T(8,128)(2,1)S(1)}, u32[]{:S(2)}, u32[]{:S(2)}) async-start(bf16[16,24,768]{2,1,0:T(8,128)(2,1)} %bitcast.43), calls=%async_computation.2 | async-start | bytes 1179648 | tf_op jit(solution)/shard_map/all_to_all | solution.py:57
  67.9 3.4 %convolution_convert_fusion.2 = bf16[384,768]{1,0:T(8,128)(2,1)} fusion(bf16[1024,768]{1,0:T(8,128)(2,1)} %copy-done.11, bf16[1024,768]{1,0:T(8,128)(2,1)} %copy-done.2, s32[]{:T(128)S(6)} %select_n.38), kind=kOutput, calls=%fused_computation.17 | convolution fusion | flops 604274688 | bytes 2949124 | tf_op jit(solution)/shard_map/dot_general | solution.py:13
  71.3 0.6 collective-permute-start.2
  71.9 1.0 dynamic-slice_bitcast_fusion
  72.9 1.7 %convolution_convert_fusion.3 = bf16[384,768]{1,0:T(8,128)(2,1)} fusion(bf16[1024,768]{1,0:T(8,128)(2,1)S(1)} %copy-done.9, bf16[1024,768]{1,0:T(8,128)(2,1)S(1)} %copy-done.4, s32[]{:T(128)S(6)} %select_n.38), kind=kOutput, calls=%fused_computation.18 | convolution fusion | flops 604274688 | bytes 2949124 | tf_op jit(solution)/shard_map/dot_general | solution.py:13
  74.6 1.4 collective-permute-start.1
  76.0 4.3 %all-to-all-done.2 = bf16[16,24,768]{2,1,0:T(8,128)(2,1)S(1)} async-done(((bf16[16,24,768]{2,1,0:T(8,128)(2,1)}), bf16[16,24,768]{2,1,0:T(8,128)(2,1)S(1)}, u32[]{:S(2)}, u32[]{:S(2)}) %all-to-all-start.2) | async-done | bytes 589856 | tf_op jit(solution)/shard_map/all_to_all | solution.py:57
  80.4 0.7 broadcast_in_dim.7
  81.1 3.3 %all-to-all-start.3 = ((bf16[4,24,768]{2,1,0:T(8,128)(2,1)}), bf16[4,24,768]{2,1,0:T(8,128)(2,1)S(1)}, u32[]{:S(2)}, u32[]{:S(2)}) async-start(bf16[4,24,768]{2,1,0:T(8,128)(2,1)} %broadcast_in_dim.7), calls=%async_computation.3 | async-start | bytes 294912 | tf_op jit(solution)/shard_map/all_to_all | solution.py:59
  84.4 3.5 %add_convert_fusion.1 = bf16[384,768]{1,0:T(8,128)(2,1)} fusion(bf16[384,768]{1,0:T(8,128)(2,1)} %collective-permute-done.4, bf16[1024,768]{1,0:T(8,128)(2,1)} %copy-done.1, bf16[1024,768]{1,0:T(8,128)(2,1)} %copy-done.2, s32[]{:T(128)S(6)} %select_n.37), kind=kOutput, calls=%fused_computation.23 | convolution fusion | flops 604864512 | bytes 3538948 | tf_op jit(solution)/shard_map/dot_general | solution.py:13
  87.9 26.0 %all-to-all-done.3 = bf16[4,24,768]{2,1,0:T(8,128)(2,1)S(1)} async-done(((bf16[4,24,768]{2,1,0:T(8,128)(2,1)}), bf16[4,24,768]{2,1,0:T(8,128)(2,1)S(1)}, u32[]{:S(2)}, u32[]{:S(2)}) %all-to-all-start.3) | async-done | bytes 147488 | tf_op jit(solution)/shard_map/all_to_all | solution.py:59
  113.9 0.9 broadcast_in_dim.8
  114.8 3.6 %all-to-all-start.4 = ((bf16[16,24,768]{2,1,0:T(8,128)(2,1)}), bf16[16,24,768]{2,1,0:T(8,128)(2,1)S(1)}, u32[]{:S(2)}, u32[]{:S(2)}) async-start(bf16[16,24,768]{2,1,0:T(8,128)(2,1)} %broadcast_in_dim.8), calls=%async_computation.4 | async-start | bytes 1179648 | tf_op jit(solution)/shard_map/all_to_all | solution.py:63
  118.4 3.5 %add_convert_fusion.2 = bf16[384,768]{1,0:T(8,128)(2,1)} fusion(bf16[384,768]{1,0:T(8,128)(2,1)} %collective-permute-done.3, bf16[1024,768]{1,0:T(8,128)(2,1)} %copy-done.12, bf16[1024,768]{1,0:T(8,128)(2,1)} %copy-done.2, s32[]{:T(128)S(6)} %select_n.37), kind=kOutput, calls=%fused_computation.24 | convolution fusion | flops 604864512 | bytes 3538948 | tf_op jit(solution)/shard_map/dot_general | solution.py:13
  121.9 2.2 %fusion.1 = bf16[32,16,768]{2,1,0:T(8,128)(2,1)} fusion(bf16[32,16,768]{2,1,0:T(8,128)(2,1)} %collective-permute-done.5, bf16[32,2,16,768]{3,2,1,0:T(8,128)(2,1)S(1)} %bitcast.41, s32[]{:T(128)S(6)} %select_n.39), kind=kLoop, calls=%fused_computation.11 | loop fusion | flops 1572864 | bytes 2359300 | tf_op jit(solution)/shard_map/convert_element_type | solution.py:73
  124.1 6.0 %all-to-all-done.4 = bf16[16,24,768]{2,1,0:T(8,128)(2,1)S(1)} async-done(((bf16[16,24,768]{2,1,0:T(8,128)(2,1)}), bf16[16,24,768]{2,1,0:T(8,128)(2,1)S(1)}, u32[]{:S(2)}, u32[]{:S(2)}) %all-to-all-start.4) | async-done | bytes 589856 | tf_op jit(solution)/shard_map/all_to_all | solution.py:63
  130.1 4.6 %all-to-all-start.1 = ((bf16[32,16,768]{2,1,0:T(8,128)(2,1)}), bf16[32,16,768]{2,1,0:T(8,128)(2,1)S(1)}, u32[]{:S(2)}, u32[]{:S(2)}) async-start(bf16[32,16,768]{2,1,0:T(8,128)(2,1)} %fusion.1), calls=%async_computation.1 | async-start | bytes 1572864 | tf_op jit(solution)/shard_map/all_to_all | solution.py:73
  134.8 2.7 %add_convert_fusion.3 = bf16[384,768]{1,0:T(8,128)(2,1)S(1)} fusion(bf16[384,768]{1,0:T(8,128)(2,1)} %collective-permute-done.2, bf16[1024,768]{1,0:T(8,128)(2,1)} %copy-done.11, bf16[1024,768]{1,0:T(8,128)(2,1)} %copy-done.2, s32[]{:T(128)S(6)} %select_n.37), kind=kOutput, calls=%fused_computation.25 | convolution fusion | flops 604864512 | bytes 3538948 | tf_op jit(solution)/shard_map/dot_general | solution.py:13
  137.6 2.0 %add_convert_fusion.4 = bf16[384,768]{1,0:T(8,128)(2,1)S(1)} fusion(bf16[384,768]{1,0:T(8,128)(2,1)} %collective-permute-done.1, bf16[1024,768]{1,0:T(8,128)(2,1)S(1)} %copy-done.10, bf16[1024,768]{1,0:T(8,128)(2,1)S(1)} %copy-done.5, s32[]{:T(128)S(6)} %select_n.37), kind=kOutput, calls=%fused_computation.26 | convolution fusion | flops 604864512 | bytes 3538948 | tf_op jit(solution)/shard_map/dot_general | solution.py:13
  139.6 0.1 collective-permute-start.7
  139.7 1.7 %pad_maximum_fusion = bf16[384,3072]{1,0:T(8,128)(2,1)} fusion(bf16[384,768]{1,0:T(8,128)(2,1)S(1)} %copy-done.6, bf16[384,768]{1,0:T(8,128)(2,1)S(1)} %copy-done.7, bf16[384,768]{1,0:T(8,128)(2,1)S(1)} %add_convert_fusion.3, bf16[384,768]{1,0:T(8,128)(2,1)S(1)} %add_convert_fusion.4), kind=kLoop, calls=%fused_computation.7 | loop fusion | flops 9437184 | bytes 4718592 | tf_op jit(solution)/shard_map/concatenate | solution.py:80
  141.4 8.3 %all-to-all-done.1 = bf16[32,16,768]{2,1,0:T(8,128)(2,1)S(1)} async-done(((bf16[32,16,768]{2,1,0:T(8,128)(2,1)}), bf16[32,16,768]{2,1,0:T(8,128)(2,1)S(1)}, u32[]{:S(2)}, u32[]{:S(2)}) %all-to-all-start.1) | async-done | bytes 786464 | tf_op jit(solution)/shard_map/all_to_all | solution.py:73
  149.7 0.1 convert_reduce_fusion
  149.8 1.3 fusion.10
  151.1 2.9 %fusion.4 = f32[768,768]{1,0:T(8,128)} fusion(bf16[384,768]{1,0:T(8,128)(2,1)} %collective-permute-done.7, bf16[384,768]{1,0:T(8,128)(2,1)S(1)} %bitcast.45, pred[]{:T(512)S(6)} %eq.4), kind=kLoop, calls=%fused_computation.20 | loop fusion | flops 5898240 | bytes 3538945 | tf_op jit(solution)/shard_map/convert_element_type | solution.py:69
  (52 shorter events, 0.3 us)
Async XLA Ops:
  0.6 30.6 %copy-start = (bf16[768,768]{1,0:T(8,128)(2,1)S(1)}, bf16[768,768]{1,0:T(8,128)(2,1)}, u32[]{:S(2)}) copy-start(bf16[768,768]{1,0:T(8,128)(2,1)} %param.5) | copy-start | bytes 3538948
  28.7 2.3 %collective-permute-start = (bf16[32,16,768]{2,1,0:T(8,128)(2,1)S(1)}, bf16[32,16,768]{2,1,0:T(8,128)(2,1)S(1)}, u32[]{:S(2)}, u32[]{:S(2)}) collective-permute-start(bf16[32,16,768]{2,1,0:T(8,128)(2,1)S(1)} %all_to_all.25), channel_id=1, source_target_pairs={{0,1},{1,0},{2,3},{3,2},{4,5},{5,4},{6,7},{7,6},{8,9},{9,8},{10,11... | collective-permute-start | bytes 2359304 | tf_op jit(solution)/shard_map/ppermute | solution.py:17
  31.0 3.3 %slice-start = ((s8[4718592]{0:T(1024)(128)(4,1)}), s8[4194304]{0:T(1024)(128)(4,1)S(1)}, s32[]{:S(2)}) async-start(s8[4718592]{0:T(1024)(128)(4,1)} %bitcast.51), calls=%async_computation.5 | async-start | bytes 8388608
  31.2 3.1 %slice-start.1 = ((s8[4718592]{0:T(1024)(128)(4,1)}), s8[524288]{0:T(1024)(128)(4,1)S(1)}, s32[]{:S(2)}) async-start(s8[4718592]{0:T(1024)(128)(4,1)} %bitcast.51), calls=%async_computation.6 | async-start | bytes 1048576
  31.2 7.6 %copy-start.17 = (s32[1024,3072]{1,0:T(8,128)S(1)}, s32[1024,3072]{1,0:T(8,128)}, u32[]{:S(2)}) copy-start(s32[1024,3072]{1,0:T(8,128)} %param.7) | copy-start | bytes 37748740
  34.3 9.7 %copy-start.2 = (bf16[1024,768]{1,0:T(8,128)(2,1)}, bf16[1024,768]{1,0:T(8,128)(2,1)S(1)}, u32[]{:S(2)}) copy-start(bf16[1024,768]{1,0:T(8,128)(2,1)S(1)} %get-tuple-element.3) | copy-start | bytes 4718596
  40.5 9.6 %copy-start.1 = (bf16[1024,768]{1,0:T(8,128)(2,1)}, bf16[1024,768]{1,0:T(8,128)(2,1)S(1)}, u32[]{:S(2)}) copy-start(bf16[1024,768]{1,0:T(8,128)(2,1)S(1)} %multiply_convert_fusion.1) | copy-start | bytes 4718596
  42.3 3.5 %copy-start.12 = (bf16[1024,768]{1,0:T(8,128)(2,1)}, bf16[1024,768]{1,0:T(8,128)(2,1)S(1)}, u32[]{:S(2)}) copy-start(bf16[1024,768]{1,0:T(8,128)(2,1)S(1)} %multiply_convert_fusion.2) | copy-start | bytes 4718596
  44.0 4.6 %copy-start.11 = (bf16[1024,768]{1,0:T(8,128)(2,1)}, bf16[1024,768]{1,0:T(8,128)(2,1)S(1)}, u32[]{:S(2)}) copy-start(bf16[1024,768]{1,0:T(8,128)(2,1)S(1)} %multiply_convert_fusion.3) | copy-start | bytes 4718596
  45.8 1.5 copy-start.8
  50.1 1.9 %copy-start.18 = (f32[1024,768]{1,0:T(8,128)S(1)}, f32[1024,768]{1,0:T(8,128)}, u32[]{:S(2)}) copy-start(f32[1024,768]{1,0:T(8,128)} %get-tuple-element.4) | copy-start | bytes 9437188
  53.8 1.0 copy-start.14
  54.9 7.4 %collective-permute-start.6 = (bf16[384,768]{1,0:T(8,128)(2,1)S(1)}, bf16[384,768]{1,0:T(8,128)(2,1)}, u32[]{:S(2)}, u32[]{:S(2)}) collective-permute-start(bf16[384,768]{1,0:T(8,128)(2,1)S(1)} %dynamic-slice_bitcast_fusion.1), channel_id=1, source_target_pairs={{0,1},{1,0},{2,3},{3,2},{4,5},{5,4},{6,7},{7,6},{8,9},{9,8},{10,11... | collective-permute-start | bytes 1769480 | tf_op jit(solution)/shard_map/ppermute | solution.py:17
  55.1 4.1 %copy-start.3 = (bf16[1024,768]{1,0:T(8,128)(2,1)S(1)}, bf16[1024,768]{1,0:T(8,128)(2,1)}, u32[]{:S(2)}) copy-start(bf16[1024,768]{1,0:T(8,128)(2,1)} %copy-done.2) | copy-start | bytes 4718596
  55.1 4.1 %copy-start.13 = (bf16[1024,768]{1,0:T(8,128)(2,1)S(1)}, bf16[1024,768]{1,0:T(8,128)(2,1)}, u32[]{:S(2)}) copy-start(bf16[1024,768]{1,0:T(8,128)(2,1)} %copy-done.12) | copy-start | bytes 4718596
  58.5 3.8 %copy-start.15 = (bf16[768,768]{1,0:T(8,128)(2,1)S(1)}, bf16[768,768]{1,0:T(8,128)(2,1)}, u32[]{:S(2)}) copy-start(bf16[768,768]{1,0:T(8,128)(2,1)} %copy-done.14) | copy-start | bytes 3538948
  58.5 25.9 %collective-permute-start.4 = (bf16[384,768]{1,0:T(8,128)(2,1)}, bf16[384,768]{1,0:T(8,128)(2,1)}, u32[]{:S(2)}, u32[]{:S(2)}) collective-permute-start(bf16[384,768]{1,0:T(8,128)(2,1)} %convolution_convert_fusion), channel_id=1, source_target_pairs={{0,64},{64,0},{1,65},{65,1},{2,66},{66,2},{3,67},{67,3},{4,68},{68... | collective-permute-start | bytes 1769480 | tf_op jit(solution)/shard_map/ppermute | solution.py:17
  60.9 57.5 %collective-permute-start.3 = (bf16[384,768]{1,0:T(8,128)(2,1)}, bf16[384,768]{1,0:T(8,128)(2,1)}, u32[]{:S(2)}, u32[]{:S(2)}) collective-permute-start(bf16[384,768]{1,0:T(8,128)(2,1)} %convolution_convert_fusion.1), channel_id=1, source_target_pairs={{0,64},{64,0},{1,65},{65,1},{2,66},{66,2},{3,67},{67,3},{4,68},{68... | collective-permute-start | bytes 1769480 | tf_op jit(solution)/shard_map/ppermute | solution.py:17
  64.3 16.0 %all-to-all-start.2 = ((bf16[16,24,768]{2,1,0:T(8,128)(2,1)}), bf16[16,24,768]{2,1,0:T(8,128)(2,1)S(1)}, u32[]{:S(2)}, u32[]{:S(2)}) async-start(bf16[16,24,768]{2,1,0:T(8,128)(2,1)} %bitcast.43), calls=%async_computation.2 | async-start | bytes 1179648 | tf_op jit(solution)/shard_map/all_to_all | solution.py:57
  67.9 5.0 %copy-start.9 = (bf16[1024,768]{1,0:T(8,128)(2,1)S(1)}, bf16[1024,768]{1,0:T(8,128)(2,1)}, u32[]{:S(2)}) copy-start(bf16[1024,768]{1,0:T(8,128)(2,1)} %copy-done.8) | copy-start | bytes 4718596
  71.3 1.6 %copy-start.4 = (bf16[1024,768]{1,0:T(8,128)(2,1)S(1)}, bf16[1024,768]{1,0:T(8,128)(2,1)}, u32[]{:S(2)}) copy-start(bf16[1024,768]{1,0:T(8,128)(2,1)} %copy-done.2) | copy-start | bytes 4718596
  71.3 63.4 %collective-permute-start.2 = (bf16[384,768]{1,0:T(8,128)(2,1)}, bf16[384,768]{1,0:T(8,128)(2,1)}, u32[]{:S(2)}, u32[]{:S(2)}) collective-permute-start(bf16[384,768]{1,0:T(8,128)(2,1)} %convolution_convert_fusion.2), channel_id=1, source_target_pairs={{0,64},{64,0},{1,65},{65,1},{2,66},{66,2},{3,67},{67,3},{4,68},{68... | collective-permute-start | bytes 1769480 | tf_op jit(solution)/shard_map/ppermute | solution.py:17
  72.9 49.0 %collective-permute-start.5 = (bf16[32,16,768]{2,1,0:T(8,128)(2,1)}, bf16[32,16,768]{2,1,0:T(8,128)(2,1)}, u32[]{:S(2)}, u32[]{:S(2)}) collective-permute-start(bf16[32,16,768]{2,1,0:T(8,128)(2,1)} %dynamic-slice_bitcast_fusion), channel_id=1, source_target_pairs={{0,1},{1,0},{2,3},{3,2},{4,5},{5,4},{6,7},{7,6},{8,9},{9,8},{10,11... | collective-permute-start | bytes 2359304 | tf_op jit(solution)/shard_map/ppermute | solution.py:17
  74.6 63.0 %collective-permute-start.1 = (bf16[384,768]{1,0:T(8,128)(2,1)}, bf16[384,768]{1,0:T(8,128)(2,1)}, u32[]{:S(2)}, u32[]{:S(2)}) collective-permute-start(bf16[384,768]{1,0:T(8,128)(2,1)} %convolution_convert_fusion.3), channel_id=1, source_target_pairs={{0,64},{64,0},{1,65},{65,1},{2,66},{66,2},{3,67},{67,3},{4,68},{68... | collective-permute-start | bytes 1769480 | tf_op jit(solution)/shard_map/ppermute | solution.py:17
  81.1 32.8 %all-to-all-start.3 = ((bf16[4,24,768]{2,1,0:T(8,128)(2,1)}), bf16[4,24,768]{2,1,0:T(8,128)(2,1)S(1)}, u32[]{:S(2)}, u32[]{:S(2)}) async-start(bf16[4,24,768]{2,1,0:T(8,128)(2,1)} %broadcast_in_dim.7), calls=%async_computation.3 | async-start | bytes 294912 | tf_op jit(solution)/shard_map/all_to_all | solution.py:59
  114.8 15.3 %all-to-all-start.4 = ((bf16[16,24,768]{2,1,0:T(8,128)(2,1)}), bf16[16,24,768]{2,1,0:T(8,128)(2,1)S(1)}, u32[]{:S(2)}, u32[]{:S(2)}) async-start(bf16[16,24,768]{2,1,0:T(8,128)(2,1)} %broadcast_in_dim.8), calls=%async_computation.4 | async-start | bytes 1179648 | tf_op jit(solution)/shard_map/all_to_all | solution.py:63
  130.1 19.6 %all-to-all-start.1 = ((bf16[32,16,768]{2,1,0:T(8,128)(2,1)}), bf16[32,16,768]{2,1,0:T(8,128)(2,1)S(1)}, u32[]{:S(2)}, u32[]{:S(2)}) async-start(bf16[32,16,768]{2,1,0:T(8,128)(2,1)} %fusion.1), calls=%async_computation.1 | async-start | bytes 1572864 | tf_op jit(solution)/shard_map/all_to_all | solution.py:73
  134.7 2.8 %copy-start.5 = (bf16[1024,768]{1,0:T(8,128)(2,1)S(1)}, bf16[1024,768]{1,0:T(8,128)(2,1)}, u32[]{:S(2)}) copy-start(bf16[1024,768]{1,0:T(8,128)(2,1)} %copy-done.2) | copy-start | bytes 4718596
  134.7 2.8 %copy-start.10 = (bf16[1024,768]{1,0:T(8,128)(2,1)S(1)}, bf16[1024,768]{1,0:T(8,128)(2,1)}, u32[]{:S(2)}) copy-start(bf16[1024,768]{1,0:T(8,128)(2,1)} %copy-done.8) | copy-start | bytes 4718596
  137.5 2.1 %copy-start.6 = (bf16[384,768]{1,0:T(8,128)(2,1)S(1)}, bf16[384,768]{1,0:T(8,128)(2,1)}, u32[]{:S(2)}) copy-start(bf16[384,768]{1,0:T(8,128)(2,1)} %add_convert_fusion.1) | copy-start | bytes 1769476
  137.5 2.1 %copy-start.7 = (bf16[384,768]{1,0:T(8,128)(2,1)S(1)}, bf16[384,768]{1,0:T(8,128)(2,1)}, u32[]{:S(2)}) copy-start(bf16[384,768]{1,0:T(8,128)(2,1)} %add_convert_fusion.2) | copy-start | bytes 1769476
  139.5 10.3 %copy-start.16 = (bf16[16,768]{1,0:T(8,128)(2,1)S(1)}, bf16[16,768]{1,0:T(8,128)(2,1)}, u32[]{:S(2)}) copy-start(bf16[16,768]{1,0:T(8,128)(2,1)} %param.4) | copy-start | bytes 73732
  139.6 11.6 %collective-permute-start.7 = (bf16[384,768]{1,0:T(8,128)(2,1)S(1)}, bf16[384,768]{1,0:T(8,128)(2,1)}, u32[]{:S(2)}, u32[]{:S(2)}) collective-permute-start(bf16[384,768]{1,0:T(8,128)(2,1)S(1)} %bitcast.44), channel_id=1, source_target_pairs={{0,1},{1,0},{2,3},{3,2},{4,5},{5,4},{6,7},{7,6},{8,9},{9,8},{10,11... | collective-permute-start | bytes 1769480 | tf_op jit(solution)/shard_map/ppermute | solution.py:17

commit v2 on v1

v2 whole, which is shorter than its diff:
```python
import functools

import jax
import jax.numpy as jnp
from jax import lax
from jax.experimental import pallas as pl
from jax.experimental.pallas import tpu as pltpu
from jax.sharding import Mesh, PartitionSpec as P

F32 = jnp.float32
BF16 = jnp.bfloat16
AXES = ("xl", "y", "z", "xh", "c")
PLANE = ("y", "z")
CHUNKS = (768, 1024, 768, 512)
TILE = 256
MIB = 2**20
LIGHT = 1024
IN_VMEM = pl.BlockSpec(memory_space=pltpu.VMEM)
IN_SMEM = pl.BlockSpec(memory_space=pltpu.SMEM)
IN_HBM = pl.BlockSpec(memory_space=pl.ANY)


def dot(a, b, dims=((1,), (0,))):
    return lax.dot_general(a, b, (dims, ((), ())), preferred_element_type=F32)


def swap(x, axis):
    return lax.ppermute(x, axis, [(0, 1), (1, 0)])


def after(x, *earlier):
    return lax.optimization_barrier((x,) + earlier)[0]


def spread(x, axes, n):
    return lax.all_to_all(jnp.broadcast_to(x[None], (n,) + x.shape), axes, 0, 0, tiled=True)


def pick(x, i, dim=0):
    return lax.dynamic_index_in_dim(x, i, dim, keepdims=False)


def ring_pass(x, axis):
    me = lax.axis_index(axis)
    ring = [[(i, (i + k) % 4) for i in range(4)] for k in range(4)]
    return [pick(x, me)] + [lax.ppermute(pick(x, (me + k) % 4), axis, ring[k]) for k in (1, 2, 3)]


def add_up(blocks):
    return sum(b.astype(F32) for b in blocks)


def x_sum(x):
    there = [
        lax.ppermute(x, ("xl", "xh"), [(i, i ^ k) for i in range(4)]).astype(F32) for k in (1, 2, 3)
    ]
    return (x.astype(F32) + there[0]) + (there[1] + there[2])


def kernel_call(kernel, ins, places, outs, scratch=(), flops=0, moved=0, limit=20, **more):
    specs = {"s": IN_SMEM, "v": IN_VMEM, "h": IN_HBM}
    given = [
        pltpu.with_memory_space_constraint(x, pltpu.HBM) if p == "h" else x
        for x, p in zip(ins, places)
    ]
    return pl.pallas_call(
        kernel,
        out_shape=[o for _, o in outs],
        in_specs=[specs[p] for p in places],
        out_specs=[specs[p] for p, _ in outs],
        scratch_shapes=scratch,
        cost_estimate=pl.CostEstimate(flops=LIGHT, bytes_accessed=LIGHT, transcendentals=0),
        compiler_params=pltpu.CompilerParams(vmem_limit_bytes=limit * MIB),
        **more,
    )(*given)


def vmem(shape, dtype=BF16):
    return ("v", jax.ShapeDtypeStruct(shape, dtype))


def hbm(shape, dtype=BF16):
    return ("h", pltpu.HBM(shape, dtype))


def start_all(copies):
    for c in copies:
        c.start()
    return copies


def wait_all(copies):
    for c in copies:
        c.wait()


def cast_kernel(at, t_hbm, out, slots, done, in_sems, out_sems):
    n_slot, piece = slots.shape[0], slots.shape[1]
    per_core = t_hbm.shape[0] // piece
    steps = 2 * per_core

    def read(s):
        core = at[0] if s < per_core else 1 - at[0]
        src = t_hbm.at[pl.ds((s % per_core) * piece, piece), core]
        return pltpu.make_async_copy(src, slots.at[s % n_slot], in_sems.at[s % n_slot])

    def write(s):
        dst = out.at[pl.ds(s * piece, piece)]
        return pltpu.make_async_copy(done.at[s % n_slot], dst, out_sems.at[s % n_slot])

    for s in range(n_slot):
        read(s).start()
    for s in range(steps):
        read(s).wait()
        if s >= n_slot:
            write(s - n_slot).wait()
        done[s % n_slot] = slots[s % n_slot].astype(F32).astype(BF16)
        write(s).start()
        if s + n_slot < steps:
            read(s + n_slot).start()
    for s in range(steps - n_slot, steps):
        write(s).wait()


def cast_targets(at, targets, rows):
    labels = targets.shape[1]
    tall = targets.reshape(32, 2, rows, labels)
    (out,) = kernel_call(
        cast_kernel,
        (at, tall),
        "sh",
        [hbm((64, rows, labels))],
        scratch=[
            pltpu.VMEM((4, 4, rows, labels), jnp.int32),
            pltpu.VMEM((4, 4, rows, labels), BF16),
            pltpu.SemaphoreType.DMA((4,)),
            pltpu.SemaphoreType.DMA((4,)),
        ],
        flops=10**9,
        moved=6 * targets.size,
    )
    return out.reshape(64 * rows, labels)


def err_of(logits, t, scale):
    return ((jax.nn.sigmoid(logits) - t.astype(F32)) * scale).astype(BF16)


def front_kernel(
    scale, at, mine, other, enc_w, w_hbm, t_hbm,
    hid, emb, send_t, slope, err, w, t, keep_t, err_out, gone, keep_v, gone_v, sems,
):
    n, width = mine.shape
    half = width // 2
    first = err.shape[1]
    rest = w.shape[1] - first
    now, later = pl.ds(0, first), pl.ds(first, rest)
    halves = start_all([
        pltpu.make_async_copy(mine, hid.at[pl.ds(0, n)], sems.at[0]),
        pltpu.make_async_copy(other, hid.at[pl.ds(n, n)], sems.at[1]),
    ])
    chunk = start_all([
        pltpu.make_async_copy(w_hbm.at[:, now], w.at[:, now], sems.at[2]),
        pltpu.make_async_copy(t_hbm.at[:, now], t.at[:, now], sems.at[3]),
    ])
    others = start_all([
        pltpu.make_async_copy(w_hbm.at[:, later], w.at[:, later], sems.at[4]),
        pltpu.make_async_copy(t_hbm.at[:, later], t.at[:, later], sems.at[5]),
    ])
    for i, arrival in enumerate(halves):
        arrival.wait()
        rows = pl.ds(i * n, n)
        for d in range(0, width, TILE):
            cut = pl.ds(d, TILE)
            act = jnp.tanh(dot(hid[rows, :], enc_w[:, cut]))
            emb[rows, cut] = (hid[rows, cut].astype(F32) + act).astype(BF16)
            slope[rows, cut] = 1.0 - act * act
    first_half = emb[:, pl.ds(0, half)].T
    second_half = emb[:, pl.ds(half, half)].T
    low = at[1] == 0
    send_t[...] = jnp.where(low, second_half, first_half)
    keep_v[...] = jnp.where(low, first_half, second_half)
    leaving = start_all([pltpu.make_async_copy(keep_v, keep_t, sems.at[8])])
    wait_all(chunk)

    def tile(j, carry):
        cut = pl.ds(pl.multiple_of(j * TILE, TILE), TILE)
        e = err_of(dot(emb[...], w[:, cut]), t[:, cut], scale)
        err[:, cut] = e
        gone_v[:, cut] = dot(send_t[...], e).astype(BF16)
        return carry

    lax.fori_loop(0, first // TILE, tile, 0)
    leaving += start_all([
        pltpu.make_async_copy(gone_v, gone, sems.at[6]),
        pltpu.make_async_copy(err, err_out, sems.at[7]),
    ])
    wait_all(others + leaving)


def main_kernel(
    scale, at, hid, emb, send_t, slope, w, t, err0,
    enc_send, enc_keep, *refs,
):
    *gone, part_own, part_other, err_out, err, gone_v, parts_v, steep, sems = refs
    n_all, width = hid.shape
    half, n = width // 2, n_all // 2
    start = err0.shape[1]
    done = 0
    leaving = []
    for k, g in enumerate(gone):
        size = g.shape[1]

        def tile(j, carry):
            here = pl.multiple_of(done + j * TILE, TILE)
            cut, wide = pl.ds(here, TILE), pl.ds(here + start, TILE)
            e = err_of(dot(emb[...], w[:, wide]), t[:, wide], scale)
            err[:, cut] = e
            gone_v[:, cut] = dot(send_t[...], e).astype(BF16)
            return carry

        lax.fori_loop(0, size // TILE, tile, 0)
        leaving += start_all([pltpu.make_async_copy(gone_v.at[:, pl.ds(done, size)], g, sems.at[k])])
        done += size
    leaving += start_all([pltpu.make_async_copy(err, err_out, sems.at[len(gone) + 2])])
    transposed = ((1,), (1,))
    for i in (1, 0):
        rows = pl.ds(i * n, n)
        for d in range(0, width, TILE):
            cut = pl.ds(d, TILE)
            p = dot(err0[rows, :], w[cut, pl.ds(0, start)], transposed)
            p = p + dot(err[rows, :], w[cut, pl.ds(start, done)], transposed)
            parts_v[rows, cut] = p.astype(BF16)
            steep[rows, cut] = (p * slope[rows, cut]).astype(BF16)
        part = pltpu.make_async_copy(parts_v.at[rows], (part_own, part_other)[i], sems.at[len(gone) + i])
        leaving += start_all([part])
    low = at[0] == 0
    first, second = hid[:, pl.ds(0, half)].T, hid[:, pl.ds(half, half)].T
    for turned, out in (
        (jnp.where(low, second, first), enc_send),
        (jnp.where(low, first, second), enc_keep),
    ):
        for d in range(0, width, TILE):
            cut = pl.ds(d, TILE)
            out[:, cut] = dot(turned, steep[:, cut]).astype(out.dtype)
    wait_all(leaving)


def kept_kernel(pieces, again, keep_t, *refs):
    n = len(pieces)
    errs, come, refs = refs[:n], refs[n : 2 * n], refs[2 * n + again :]
    out, keep_v, err_v, come_v, out_v, sems = refs
    reads = [start_all([pltpu.make_async_copy(keep_t, keep_v, sems.at[0])])]
    cuts, at = [], 0
    for i, (lo, size, _) in enumerate(pieces):
        cut = pl.ds(at, size)
        reads.append(start_all([
            pltpu.make_async_copy(errs[i].at[:, pl.ds(lo, size)], err_v.at[:, cut], sems.at[3 * i + 1]),
            pltpu.make_async_copy(come[i], come_v.at[:, cut], sems.at[3 * i + 2]),
        ]))
        cuts.append(cut)
        at += size
    leaving = []
    wait_all(reads[0])
    at = 0
    for i, (_, size, start) in enumerate(pieces):
        wait_all(reads[i + 1])
        for d in range(at, at + size, TILE):
            cut = pl.ds(d, TILE)
            block = dot(keep_v[...], err_v[:, cut]) + come_v[:, cut].astype(F32)
            out_v[:, cut] = block.astype(BF16)
        at += size
        dst = out.at[:, pl.ds(start, size)]
        leaving += start_all([pltpu.make_async_copy(out_v.at[:, cuts[i]], dst, sems.at[3 * i + 3])])
    wait_all(leaving)


def keep_and_add(keep_t, pieces, labels, given=None):
    half, n_all = keep_t.shape
    size = sum(c.shape[1] for _, _, c, _ in pieces)
    n = len(pieces)
    again = given is not None
    ins = [keep_t] + [p[0] for p in pieces] + [p[2] for p in pieces] + ([given] if again else [])
    (out,) = kernel_call(
        functools.partial(kept_kernel, [(p[1], p[2].shape[1], p[3]) for p in pieces], int(again)),
        ins,
        "h" * len(ins),
        [hbm((half, labels))],
        scratch=[
            pltpu.VMEM((half, n_all), BF16),
            pltpu.VMEM((n_all, size), BF16),
            pltpu.VMEM((half, size), BF16),
            pltpu.VMEM((half, size), BF16),
            pltpu.SemaphoreType.DMA((3 * n + 1,)),
        ],
        input_output_aliases={len(ins) - 1: 0} if again else {},
    )
    return out


def body(hidden, enc_weight, cls_weight, targets):
    core = lax.axis_index("c")
    dp = lax.axis_index("xl")
    far = lax.axis_index("xh")
    at = jnp.stack([core, dp]).astype(jnp.int32)
    rows, width = hidden.shape
    labels = cls_weight.shape[1]
    half = width // 2
    n_all = 64 * rows
    n_own = n_all // 2
    scale = float(1.0 / (2048.0**0.5))

    mine = spread(hidden, ("y", "z", "xh"), 32)
    t = cast_targets(at, targets, rows)
    mine, t = lax.optimization_barrier((mine, t))
    other = swap(mine, "c").reshape(n_own, width)
    mine = mine.reshape(n_own, width)

    first, rest = CHUNKS[0], labels - CHUNKS[0]
    hid, emb, send_t, slope, err0, w_v, t_v, keep_t, err0_out, gone0 = kernel_call(
        functools.partial(front_kernel, scale),
        (at, mine, other, enc_weight, cls_weight, t),
        "shvvhh",
        [
            vmem((n_all, width)),
            vmem((n_all, width)),
            vmem((half, n_all)),
            vmem((n_all, width), F32),
            vmem((n_all, first)),
            vmem((width, labels)),
            vmem((n_all, labels)),
            hbm((half, n_all)),
            hbm((n_all, first)),
            hbm((half, first)),
        ],
        scratch=[
            pltpu.VMEM((half, n_all), BF16),
            pltpu.VMEM((half, first), BF16),
            pltpu.SemaphoreType.DMA((9,)),
        ],
        flops=2 * n_all * width * (width + first + first // 2),
        moved=4 * MIB,
    )
    gone0_in = swap(gone0, "xl")
    enc_send, enc_keep, *gone, part_own, part_other, err = kernel_call(
        functools.partial(main_kernel, scale),
        (at, hid, emb, send_t, slope, w_v, t_v, err0),
        "svvvvvvv",
        [vmem((half, width)), vmem((half, width), F32)]
        + [hbm((half, c)) for c in CHUNKS[1:]]
        + [hbm((n_own, width))] * 2
        + [hbm((n_all, rest))],
        scratch=[
            pltpu.VMEM((n_all, rest), BF16),
            pltpu.VMEM((half, rest), BF16),
            pltpu.VMEM((n_all, width), BF16),
            pltpu.VMEM((n_all, width), BF16),
            pltpu.SemaphoreType.DMA((len(CHUNKS) + 2,)),
        ],
        flops=2 * n_all * width * (rest + rest // 2 + labels + width),
        moved=8 * MIB,
    )
    enc_in = swap(after(enc_send, gone0_in), "c")
    gone1_in = swap(gone[0], "xl")

    enc = (enc_keep + enc_in.astype(F32)).astype(BF16)
    enc_sent = enc
    enc = lax.all_to_all(enc.reshape(16, half // 16, width), PLANE, 0, 0, tiled=True)
    cls_grad = keep_and_add(after(keep_t, enc_sent), [(err0_out, 0, gone0_in, 0)], labels)
    enc_part = jnp.sum(after(enc, gone1_in, cls_grad).astype(F32), 0).astype(BF16)
    enc = x_sum(enc_part).astype(BF16)
    gone2_in, gone3_in = swap(after(gone[1], enc), "xl"), swap(after(gone[2], enc), "xl")
    cls_grad = keep_and_add(after(keep_t, enc), [(err, 0, gone1_in, first)], labels, cls_grad)
    enc_half = after(spread(enc, PLANE, 16), gone2_in, cls_grad).reshape(half, width)
    enc_rest = swap(enc_half, "c")
    is_mine = (jnp.arange(2) == core)[:, None, None]
    enc_grad = jnp.where(is_mine, enc_half[None], enc_rest[None]).astype(F32).reshape(width, width)

    sums_in = swap(part_other, "c")
    sums = after((part_own.astype(F32) + sums_in.astype(F32)).astype(BF16), enc_sent)
    sums = [after(b, enc) for b in ring_pass(sums.reshape(4, 4 * 2 * rows, width), "y")]
    sums = add_up(sums).astype(BF16).reshape(4, 2 * rows, width)
    sums = [after(b, enc_half) for b in ring_pass(sums, "z")]
    sums = add_up(sums).reshape(2, rows, width)
    emb_grad = pick(sums, far) + swap(pick(sums, 1 - far).astype(BF16), "xh").astype(F32)
    act_own = jnp.tanh(dot(hidden, enc_weight))
    pre_grad = (emb_grad * (1.0 - act_own * act_own)).astype(BF16)
    input_grad = (emb_grad + dot(pre_grad, enc_weight, ((1,), (1,)))).astype(BF16)

    for come, start in ((gone2_in, sum(CHUNKS[:2])), (gone3_in, sum(CHUNKS[:3]))):
        cls_grad = keep_and_add(keep_t, [(err, start - first, come, start)], labels, cls_grad)
    return (cls_grad, input_grad, enc_grad)


def solution(mesh):
    grid = Mesh(mesh.devices.reshape(2, 4, 4, 2, 2), AXES)
    label = AXES[1:]
    placed = (P(AXES, None), P(), P(None, label), P("xl", label))
    return jax.shard_map(
        body,
        mesh=grid,
        in_specs=placed,
        out_specs=(P("xl", label), P(AXES, None), P()),
        check_vma=False,
    )
```

time: 155 us -> 120 us (0.77)
  Pallas kernels: 0 us -> 47.6 us
  matrix products: 40.7 us -> 1.3 us
  blocking collectives: 27.2 us -> 0 us
  waiting for transfers between devices: 47 us -> 21 us
  starting transfers between devices: 19.5 us -> 36.4 us
  local copies, waits for them, and re-layouts: 9.43 us -> 5 us
  other arithmetic: 9.2 us -> 6.04 us
    pallas_call x0 -> x7, Pallas kernels: none -> 47.6 us  [kernel_call(): pl.pallas_call(kernel, out_shape=[o for _, o in outs], in_specs=[specs[p]...]
    dot_general x19 -> x1, matrix products: 40.7 us -> 1.3 us  [dot(): return lax.dot_general(a, b, (dims, ((), ())), preferred_element_type=F32)]
    all_to_all x4 -> x3, waiting for transfers between devices: 44.7 us -> 7.86 us  [the longest x2 7.85 us: spread(): lax.all_to_all(jnp.broadcast_to(x[None], (n,) + x.shape), axes, 0, 0, til...]
    all_to_all x1 -> x0, blocking collectives: 27.2 us -> none  [body(): lax.all_to_all(jnp.broadcast_to(hidden[None], (n_peer, rows, width)), ('y...]
    ppermute x0 -> x9, starting transfers between devices: none -> 10.9 us  [the longest x6 6.71 us: ring_pass(): lax.ppermute(pick(x, (me + k) % 4), axis, ring[k])]
    ppermute x8 -> x9, waiting for transfers between devices: 2.3 us -> 10.3 us  [swap(): return lax.ppermute(x, axis, [(0, 1), (1, 0)])]
    unnamed x42 -> x16, local copies, waits for them, and re-layouts: 6.03 us -> 1.66 us
    all_to_all x4 -> x3, starting transfers between devices: 15.1 us -> 19.1 us  [the longest x2 15.3 us: spread(): lax.all_to_all(jnp.broadcast_to(x[None], (n,) + x.shape), axes, 0, 0, til...]
  transfers between devices with their start and end apart: 12 -> 21, of which waited for: 5 -> 6; matrix products, arithmetic and copies ran while one was open for 21% -> 6% of each run, Pallas kernels for 0% -> 33%
where the time goes in v2:
time: 120 us; the launch traced here: 118 us
  Pallas kernels  47.6 us (40%)
  starting transfers between devices  36.4 us (30%)
  waiting for transfers between devices  21 us (18%)
  other arithmetic  6.04 us (5%)
  local copies, waits for them, and re-layouts  5 us (4%)
  matrix products  1.3 us (1%)
    pallas_call x7, Pallas kernels, kernel_call(): pl.pallas_call(kernel, out_shape=[o for _, o in outs], in_specs=[specs[p]...  47.6 us
    all_to_all x2, starting transfers between devices, spread(): lax.all_to_all(jnp.broadcast_to(x[None], (n,) + x.shape), axes, 0, 0, til...  15.3 us
    ppermute x9, waiting for transfers between devices, swap(): return lax.ppermute(x, axis, [(0, 1), (1, 0)])  10.3 us
    all_to_all x2, waiting for transfers between devices, spread(): lax.all_to_all(jnp.broadcast_to(x[None], (n,) + x.shape), axes, 0, 0, til...  7.85 us
    ppermute x6, starting transfers between devices, ring_pass(): lax.ppermute(pick(x, (me + k) % 4), axis, ring[k])  6.71 us
    ppermute x9, starting transfers between devices, swap(): return lax.ppermute(x, axis, [(0, 1), (1, 0)])  6.44 us
    ppermute x3, starting transfers between devices, x_sum(): lax.ppermute(x, ('xl', 'xh'), [(i, i ^ k) for i in range(4)]).astype(F32)  4.19 us
    all_to_all x1, starting transfers between devices, body(): lax.all_to_all(enc.reshape(16, half // 16, width), PLANE, 0, 0, tiled=True)  3.76 us
  transfers between devices with their start and end apart: 21, of which 6 were waited for; matrix products, arithmetic and copies ran while one was open for 6% of the time, Pallas kernels for 33%

profile of v2, /device:TPU:0, one launch (start us, length us, event | category | flops | bytes accessed | tf_op | source)
XLA Modules:
  0.0 118.5 jit_solution(6406860385293214687)
XLA Ops:
  0.6 1.7 %broadcast_in_dim.46 = bf16[32,16,768]{2,1,0:T(8,128)(2,1)} broadcast(bf16[16,768]{1,0:T(8,128)(2,1)} %param.4), dimensions={1,2} | broadcast | bytes 811008 | tf_op jit(solution)/shard_map/broadcast_in_dim | solution.py:36
  2.3 10.9 %all-to-all-start = ((bf16[32,16,768]{2,1,0:T(8,128)(2,1)}), bf16[32,16,768]{2,1,0:T(8,128)(2,1)S(1)}, u32[]{:S(2)}, u32[]{:S(2)}) async-start(bf16[32,16,768]{2,1,0:T(8,128)(2,1)} %broadcast_in_dim.46), calls=%async_computation | async-start | bytes 1572864 | tf_op jit(solution)/shard_map/all_to_all | solution.py:36
  13.2 0.1 pad_add_fusion.at
  13.3 8.6 %shard_map.67 = bf16[64,16,3072]{2,1,0:T(8,128)(2,1)} custom-call(s32[2]{0:T(128)S(1)} %pad_add_fusion.at, s32[32,2,16,3072]{3,2,1,0:T(8,128)} %bitcast.48), custom_call_target="tpu_custom_call" | custom-call | flops 1024 | bytes 1024 | tf_op jit(solution)/shard_map/pallas_call | solution.py:66
  21.9 7.8 %all-to-all-done = bf16[32,16,768]{2,1,0:T(8,128)(2,1)S(1)} async-done(((bf16[32,16,768]{2,1,0:T(8,128)(2,1)}), bf16[32,16,768]{2,1,0:T(8,128)(2,1)S(1)}, u32[]{:S(2)}, u32[]{:S(2)}) %all-to-all-start) | async-done | bytes 786464 | tf_op jit(solution)/shard_map/all_to_all | solution.py:36
  29.7 2.3 %collective-permute-done = bf16[32,16,768]{2,1,0:T(8,128)(2,1)S(1)} collective-permute-done((bf16[32,16,768]{2,1,0:T(8,128)(2,1)S(1)}, bf16[32,16,768]{2,1,0:T(8,128)(2,1)S(1)}, u32[]{:S(2)}, u32[]{:S(2)}) %collective-permute-start) | collective-permute-done | bytes 786464 | tf_op jit(solution)/shard_map/ppermute | solution.py:28
  32.0 8.6 %shard_map.68 = (bf16[1024,768]{1,0:T(8,128)(2,1)S(1)}, bf16[1024,768]{1,0:T(8,128)(2,1)S(1)}, bf16[384,1024]{1,0:T(8,128)(2,1)S(1)}, f32[1024,768]{1,0:T(8,128)...) custom-call(s32[2]{0:T(128)S(1)} %pad_add_fusion.at, ...), custom_call_target="tpu_custom_call" | custom-call | flops 1024 | bytes 1024 | tf_op jit(solution)/shard_map/pallas_call | solution.py:66
  40.6 0.7 collective-permute-start.1
  41.3 16.8 %shard_map.69 = (bf16[384,768]{1,0:T(8,128)(2,1)S(1)}, f32[384,768]{1,0:T(8,128)S(1)}, bf16[384,1024]{1,0:T(8,128)(2,1)}, bf16[384,768]{1,0:T(8,128)(2,1)}, bf16...) custom-call(s32[2]{0:T(128)S(1)} %pad_add_fusion.at, ...), custom_call_target="tpu_custom_call" | custom-call | flops 1024 | bytes 1024 | tf_op jit(solution)/shard_map/pallas_call | solution.py:66
  58.2 0.1 collective-permute-start.2
  58.2 0.5 collective-permute-start.9
  58.7 1.4 %collective-permute-start.3 = (bf16[384,1024]{1,0:T(8,128)(2,1)}, bf16[384,1024]{1,0:T(8,128)(2,1)}, u32[]{:S(2)}, u32[]{:S(2)}) collective-permute-start(bf16[384,1024]{1,0:T(8,128)(2,1)} %get-tuple-element.55), channel_id=1, source_target_pairs={{0,64},{64,0},{1,65},{65,1},{2,66},{66,2},{3,67},{67,3},{4,68},{68... | collective-permute-start | bytes 2359304 | tf_op jit(solution)/shard_map/ppermute | solution.py:28
  60.2 0.1 collective-permute-done.2
  60.2 0.9 add_convert_fusion.1
  61.2 3.8 %all-to-all-start.1 = ((bf16[16,24,768]{2,1,0:T(8,128)(2,1)}), bf16[16,24,768]{2,1,0:T(8,128)(2,1)S(1)}, u32[]{:S(2)}, u32[]{:S(2)}) async-start(bf16[16,24,768]{2,1,0:T(8,128)(2,1)} %bitcast.6), calls=%async_computation.1 | async-start | bytes 1179648 | tf_op jit(solution)/shard_map/all_to_all | solution.py:368
  65.0 0.9 copy-done.3
  65.9 1.3 %add_convert_fusion = bf16[512,768]{1,0:T(8,128)(2,1)S(1)} fusion(bf16[512,768]{1,0:T(8,128)(2,1)} %copy-done.3, bf16[512,768]{1,0:T(8,128)(2,1)S(1)} %copy-done.2), kind=kLoop, calls=%fused_computation | loop fusion | flops 1572864 | bytes 2359296 | tf_op jit(solution)/shard_map/convert_element_type | solution.py:380
  67.2 3.4 %shard_map.70.refs_2_ = bf16[384,3072]{1,0:T(8,128)(2,1)} custom-call(bf16[384,1024]{1,0:T(8,128)(2,1)} %get-tuple-element.62.keep_t, bf16[1024,768]{1,0:T(8,128)(2,1)} %get-tuple-element.57.refs_0_, bf16[384,768]{1,0:T(8,128)(2,1)} %copy-done.4), custom_call_target="tpu_custom_call" | custom-call | flops 1024 | bytes 1024 | tf_op jit(solution)/shard_map/pallas_call | solution.py:66
  70.6 8.0 %collective-permute-done.3.refs_1_ = bf16[384,1024]{1,0:T(8,128)(2,1)} collective-permute-done((bf16[384,1024]{1,0:T(8,128)(2,1)}, bf16[384,1024]{1,0:T(8,128)(2,1)}, u32[]{:S(2)}, u32[]{:S(2)}) %collective-permute-start.3) | collective-permute-done | bytes 786464 | tf_op jit(solution)/shard_map/ppermute | solution.py:28
  78.6 0.1 reduce_sum.12
  78.7 1.2 %collective-permute-start.4 = (bf16[24,768]{1,0:T(8,128)(2,1)S(1)}, bf16[24,768]{1,0:T(8,128)(2,1)S(1)}, u32[]{:S(2)}, u32[]{:S(2)}) collective-permute-start(bf16[24,768]{1,0:T(8,128)(2,1)S(1)} %reduce_sum.12), channel_id=1, source_target_pairs={{0,2},{2,0},{64,66},{66,64},{1,3},{3,1},{65,67},{67,65},{4,6},{6,4... | collective-permute-start | bytes 110600 | tf_op jit(solution)/shard_map/ppermute | solution.py:55
  79.9 0.4 collective-permute-start.5
  80.3 2.6 %collective-permute-start.6 = (bf16[24,768]{1,0:T(8,128)(2,1)S(1)}, bf16[24,768]{1,0:T(8,128)(2,1)S(1)}, u32[]{:S(2)}, u32[]{:S(2)}) collective-permute-start(bf16[24,768]{1,0:T(8,128)(2,1)S(1)} %reduce_sum.12), channel_id=1, source_target_pairs={{0,66},{2,64},{64,2},{66,0},{1,67},{3,65},{65,3},{67,1},{4,70},{6,... | collective-permute-start | bytes 110600 | tf_op jit(solution)/shard_map/ppermute | solution.py:55
  82.9 0.1 dynamic-slice_bitcast_fusion.3
  82.9 0.1 collective-permute-start.10
  83.0 2.3 %collective-permute-start.11 = (bf16[128,768]{1,0:T(8,128)(2,1)S(1)}, bf16[128,768]{1,0:T(8,128)(2,1)S(1)}, u32[]{:S(2)}, u32[]{:S(2)}) collective-permute-start(bf16[128,768]{1,0:T(8,128)(2,1)S(1)} %get-tuple-element.77), channel_id=1, source_target_pairs={{0,32},{16,48},{32,0},{48,16},{1,33},{17,49},{33,1},{49,17},{2,34}... | collective-permute-start | bytes 589832 | tf_op jit(solution)/shard_map/ppermute | solution.py:46
  85.3 1.1 collective-permute-start.12
  86.5 1.5 %collective-permute-start.8 = (bf16[384,768]{1,0:T(8,128)(2,1)}, bf16[384,768]{1,0:T(8,128)(2,1)S(1)}, u32[]{:S(2)}, u32[]{:S(2)}) collective-permute-start(bf16[384,768]{1,0:T(8,128)(2,1)} %get-tuple-element.61), channel_id=1, source_target_pairs={{0,64},{64,0},{1,65},{65,1},{2,66},{66,2},{3,67},{67,3},{4,68},{68... | collective-permute-start | bytes 1769480 | tf_op jit(solution)/shard_map/ppermute | solution.py:28
  88.0 0.9 broadcast_in_dim.47
  88.8 4.5 %all-to-all-start.2 = ((bf16[16,24,768]{2,1,0:T(8,128)(2,1)}), bf16[16,24,768]{2,1,0:T(8,128)(2,1)S(1)}, u32[]{:S(2)}, u32[]{:S(2)}) async-start(bf16[16,24,768]{2,1,0:T(8,128)(2,1)} %broadcast_in_dim.47), calls=%async_computation.2 | async-start | bytes 1179648 | tf_op jit(solution)/shard_map/all_to_all | solution.py:36
  93.3 0.6 collective-permute-done.10
  94.0 2.2 %collective-permute-done.12 = bf16[128,768]{1,0:T(8,128)(2,1)} collective-permute-done((bf16[128,768]{1,0:T(8,128)(2,1)S(1)}, bf16[128,768]{1,0:T(8,128)(2,1)}, u32[]{:S(2)}, u32[]{:S(2)}) %collective-permute-start.12) | collective-permute-done | bytes 196640 | tf_op jit(solution)/shard_map/ppermute | solution.py:46
  96.2 1.0 add_convert_fusion.2
  97.2 0.7 dynamic-slice_bitcast_fusion.7
  97.9 1.7 %collective-permute-start.14 = (bf16[32,768]{1,0:T(8,128)(2,1)S(1)}, bf16[32,768]{1,0:T(8,128)(2,1)}, u32[]{:S(2)}, u32[]{:S(2)}) collective-permute-start(bf16[32,768]{1,0:T(8,128)(2,1)S(1)} %get-tuple-element.81), channel_id=1, source_target_pairs={{0,8},{4,12},{8,0},{12,4},{1,9},{5,13},{9,1},{13,5},{2,10},{6,14},... | collective-permute-start | bytes 147464 | tf_op jit(solution)/shard_map/ppermute | solution.py:46
  99.6 1.5 %collective-permute-start.15 = (bf16[32,768]{1,0:T(8,128)(2,1)S(1)}, bf16[32,768]{1,0:T(8,128)(2,1)}, u32[]{:S(2)}, u32[]{:S(2)}) collective-permute-start(bf16[32,768]{1,0:T(8,128)(2,1)S(1)} %get-tuple-element.80), channel_id=1, source_target_pairs={{0,12},{4,0},{8,4},{12,8},{1,13},{5,1},{9,5},{13,9},{2,14},{6,2},{... | collective-permute-start | bytes 147464 | tf_op jit(solution)/shard_map/ppermute | solution.py:46
  101.1 1.4 %collective-permute-start.7 = (bf16[384,512]{1,0:T(8,128)(2,1)}, bf16[384,512]{1,0:T(8,128)(2,1)S(1)}, u32[]{:S(2)}, u32[]{:S(2)}) collective-permute-start(bf16[384,512]{1,0:T(8,128)(2,1)} %get-tuple-element.59), channel_id=1, source_target_pairs={{0,64},{64,0},{1,65},{65,1},{2,66},{66,2},{3,67},{67,3},{4,68},{68... | collective-permute-start | bytes 1179656 | tf_op jit(solution)/shard_map/ppermute | solution.py:28
  102.5 3.9 %shard_map.71.refs_2_ = bf16[384,3072]{1,0:T(8,128)(2,1)} custom-call(bf16[384,1024]{1,0:T(8,128)(2,1)} %get-tuple-element.62.keep_t, bf16[1024,2304]{1,0:T(8,128)(2,1)} %get-tuple-element.49.refs_0_, bf16[384,1024]{1,0:T(8,128)(2,1)} %collective-permute-done.3.refs_1_, bf16[384,3072]{1,0:T(8,128)(2,1)} %shard_map.70.refs_2_), custom_call_target="tpu_custom_call", output_to_operand_aliasing={{}: (3, {})} | custom-call | flops 1024 | bytes 1024 | tf_op jit(solution)/shard_map/pallas_call | solution.py:66
  106.4 0.1 collective-permute-start.17
  106.6 0.9 convert_add_fusion
  107.5 0.8 collective-permute-start.16
  108.3 0.1 broadcast_in_dim.48
  108.4 3.4 %shard_map.72.refs_2_ = bf16[384,3072]{1,0:T(8,128)(2,1)} custom-call(bf16[384,1024]{1,0:T(8,128)(2,1)} %get-tuple-element.62.keep_t, bf16[1024,2304]{1,0:T(8,128)(2,1)} %get-tuple-element.49.refs_0_, bf16[384,768]{1,0:T(8,128)(2,1)} %copy-done.5, bf16[384,3072]{1,0:T(8,128)(2,1)} %shard_map.71.refs_2_), custom_call_target="tpu_custom_call", output_to_operand_aliasing={{}: (3, {})} | custom-call | flops 1024 | bytes 1024 | tf_op jit(solution)/shard_map/pallas_call | solution.py:66
  111.8 0.0 copy-start.7
  111.8 0.7 copy-done.6
  112.6 2.9 %shard_map.73 = bf16[384,3072]{1,0:T(8,128)(2,1)} custom-call(bf16[384,1024]{1,0:T(8,128)(2,1)} %get-tuple-element.62.keep_t, bf16[1024,2304]{1,0:T(8,128)(2,1)} %get-tuple-element.49.refs_0_, bf16[384,512]{1,0:T(8,128)(2,1)} %copy-done.6, bf16[384,3072]{1,0:T(8,128)(2,1)} %shard_map.72.refs_2_), custom_call_target="tpu_custom_call", output_to_operand_aliasing={{}: (3, {})} | custom-call | flops 1024 | bytes 1024 | tf_op jit(solution)/shard_map/pallas_call | solution.py:66
  115.5 1.3 %fusion.5 = bf16[16,768]{1,0:T(8,128)(2,1)} fusion(bf16[768,768]{1,0:T(8,128)(2,1)S(1)} %copy-done, bf16[16,768]{1,0:T(8,128)(2,1)S(1)} %copy-done.7, bf16[16,768]{1,0:T(8,128)(2,1)S(1)} %collective-permute-done.16, f32[2,16,768]{2,1,0:T(8,128)S(1)} %bitcast.55, s32[]{:T(128)S(6)} %select_n.79), kind=kOutput, calls=%fused_computation.10 | convolution fusion | flops 37871616 | bytes 2556928 | tf_op jit(solution)/shard_map/dot_general | solution.py:24
  116.8 1.6 %fusion = f32[768,768]{1,0:T(8,128)} fusion(pred[768]{0:T(1024)(128)(4,1)S(1)} %broadcast_in_dim.49, bf16[384,768]{1,0:T(8,128)(2,1)S(1)} %collective-permute-done.17, bf16[384,768]{1,0:T(8,128)(2,1)S(1)} %bitcast.52), kind=kLoop, calls=%fused_computation.2 | loop fusion | flops 1179648 | bytes 3539712 | tf_op jit(solution)/shard_map/convert_element_type | solution.py:377
  (34 shorter events, 0.1 us)
Async XLA Ops:
  2.3 27.4 %all-to-all-start = ((bf16[32,16,768]{2,1,0:T(8,128)(2,1)}), bf16[32,16,768]{2,1,0:T(8,128)(2,1)S(1)}, u32[]{:S(2)}, u32[]{:S(2)}) async-start(bf16[32,16,768]{2,1,0:T(8,128)(2,1)} %broadcast_in_dim.46), calls=%async_computation | async-start | bytes 1572864 | tf_op jit(solution)/shard_map/all_to_all | solution.py:36
  13.3 18.7 %copy-start = (bf16[768,768]{1,0:T(8,128)(2,1)S(1)}, bf16[768,768]{1,0:T(8,128)(2,1)}, u32[]{:S(2)}) copy-start(bf16[768,768]{1,0:T(8,128)(2,1)} %enc_w.1) | copy-start | bytes 3538948
  29.7 2.3 %copy-start.1 = (bf16[32,16,768]{2,1,0:T(8,128)(2,1)}, bf16[32,16,768]{2,1,0:T(8,128)(2,1)S(1)}, u32[]{:S(2)}) copy-start(bf16[32,16,768]{2,1,0:T(8,128)(2,1)S(1)} %all-to-all-done) | copy-start | bytes 2359300
  29.7 2.3 %collective-permute-start = (bf16[32,16,768]{2,1,0:T(8,128)(2,1)S(1)}, bf16[32,16,768]{2,1,0:T(8,128)(2,1)S(1)}, u32[]{:S(2)}, u32[]{:S(2)}) collective-permute-start(bf16[32,16,768]{2,1,0:T(8,128)(2,1)S(1)} %all-to-all-done), channel_id=1, source_target_pairs={{0,1},{1,0},{2,3},{3,2},{4,5},{5,4},{6,7},{7,6},{8,9},{9,8},{10,11... | collective-permute-start | bytes 2359304 | tf_op jit(solution)/shard_map/ppermute | solution.py:28
  40.6 17.5 %collective-permute-start.1 = (bf16[384,768]{1,0:T(8,128)(2,1)}, bf16[384,768]{1,0:T(8,128)(2,1)S(1)}, u32[]{:S(2)}, u32[]{:S(2)}) collective-permute-start(bf16[384,768]{1,0:T(8,128)(2,1)} %get-tuple-element.53), channel_id=1, source_target_pairs={{0,64},{64,0},{1,65},{65,1},{2,66},{66,2},{3,67},{67,3},{4,68},{68... | collective-permute-start | bytes 1769480 | tf_op jit(solution)/shard_map/ppermute | solution.py:28
  58.1 3.0 %copy-start.4 = (bf16[384,768]{1,0:T(8,128)(2,1)}, bf16[384,768]{1,0:T(8,128)(2,1)S(1)}, u32[]{:S(2)}) copy-start(bf16[384,768]{1,0:T(8,128)(2,1)S(1)} %collective-permute-done.1.refs_1_) | copy-start | bytes 1769476
  58.2 2.1 %collective-permute-start.2 = (bf16[384,768]{1,0:T(8,128)(2,1)S(1)}, bf16[384,768]{1,0:T(8,128)(2,1)S(1)}, u32[]{:S(2)}, u32[]{:S(2)}) collective-permute-start(bf16[384,768]{1,0:T(8,128)(2,1)S(1)} %get-tuple-element.54), channel_id=1, source_target_pairs={{0,1},{1,0},{2,3},{3,2},{4,5},{5,4},{6,7},{7,6},{8,9},{9,8},{10,11... | collective-permute-start | bytes 1769480 | tf_op jit(solution)/shard_map/ppermute | solution.py:28
  58.2 6.8 %collective-permute-start.9 = (bf16[512,768]{1,0:T(8,128)(2,1)}, bf16[512,768]{1,0:T(8,128)(2,1)S(1)}, u32[]{:S(2)}, u32[]{:S(2)}) collective-permute-start(bf16[512,768]{1,0:T(8,128)(2,1)} %get-tuple-element.64), channel_id=1, source_target_pairs={{0,1},{1,0},{2,3},{3,2},{4,5},{5,4},{6,7},{7,6},{8,9},{9,8},{10,11... | collective-permute-start | bytes 2359304 | tf_op jit(solution)/shard_map/ppermute | solution.py:28
  58.7 19.9 %collective-permute-start.3 = (bf16[384,1024]{1,0:T(8,128)(2,1)}, bf16[384,1024]{1,0:T(8,128)(2,1)}, u32[]{:S(2)}, u32[]{:S(2)}) collective-permute-start(bf16[384,1024]{1,0:T(8,128)(2,1)} %get-tuple-element.55), channel_id=1, source_target_pairs={{0,64},{64,0},{1,65},{65,1},{2,66},{66,2},{3,67},{67,3},{4,68},{68... | collective-permute-start | bytes 2359304 | tf_op jit(solution)/shard_map/ppermute | solution.py:28
  60.2 5.7 %copy-start.2 = (bf16[512,768]{1,0:T(8,128)(2,1)S(1)}, bf16[512,768]{1,0:T(8,128)(2,1)}, u32[]{:S(2)}) copy-start(bf16[512,768]{1,0:T(8,128)(2,1)} %get-tuple-element.63) | copy-start | bytes 2359300
  61.2 17.4 %all-to-all-start.1 = ((bf16[16,24,768]{2,1,0:T(8,128)(2,1)}), bf16[16,24,768]{2,1,0:T(8,128)(2,1)S(1)}, u32[]{:S(2)}, u32[]{:S(2)}) async-start(bf16[16,24,768]{2,1,0:T(8,128)(2,1)} %bitcast.6), calls=%async_computation.1 | async-start | bytes 1179648 | tf_op jit(solution)/shard_map/all_to_all | solution.py:368
  65.0 0.9 copy-start.3
  78.7 6.6 %collective-permute-start.4 = (bf16[24,768]{1,0:T(8,128)(2,1)S(1)}, bf16[24,768]{1,0:T(8,128)(2,1)S(1)}, u32[]{:S(2)}, u32[]{:S(2)}) collective-permute-start(bf16[24,768]{1,0:T(8,128)(2,1)S(1)} %reduce_sum.12), channel_id=1, source_target_pairs={{0,2},{2,0},{64,66},{66,64},{1,3},{3,1},{65,67},{67,65},{4,6},{6,4... | collective-permute-start | bytes 110600 | tf_op jit(solution)/shard_map/ppermute | solution.py:55
  79.9 6.5 %collective-permute-start.5 = (bf16[24,768]{1,0:T(8,128)(2,1)S(1)}, bf16[24,768]{1,0:T(8,128)(2,1)S(1)}, u32[]{:S(2)}, u32[]{:S(2)}) collective-permute-start(bf16[24,768]{1,0:T(8,128)(2,1)S(1)} %reduce_sum.12), channel_id=1, source_target_pairs={{0,64},{2,66},{64,0},{66,2},{1,65},{3,67},{65,1},{67,3},{4,68},{6,... | collective-permute-start | bytes 110600 | tf_op jit(solution)/shard_map/ppermute | solution.py:55
  80.3 6.1 %collective-permute-start.6 = (bf16[24,768]{1,0:T(8,128)(2,1)S(1)}, bf16[24,768]{1,0:T(8,128)(2,1)S(1)}, u32[]{:S(2)}, u32[]{:S(2)}) collective-permute-start(bf16[24,768]{1,0:T(8,128)(2,1)S(1)} %reduce_sum.12), channel_id=1, source_target_pairs={{0,66},{2,64},{64,2},{66,0},{1,67},{3,65},{65,3},{67,1},{4,70},{6,... | collective-permute-start | bytes 110600 | tf_op jit(solution)/shard_map/ppermute | solution.py:55
  82.9 11.0 %collective-permute-start.10 = (bf16[128,768]{1,0:T(8,128)(2,1)S(1)}, bf16[128,768]{1,0:T(8,128)(2,1)S(1)}, u32[]{:S(2)}, u32[]{:S(2)}) collective-permute-start(bf16[128,768]{1,0:T(8,128)(2,1)S(1)} %get-tuple-element.78), channel_id=1, source_target_pairs={{0,16},{16,32},{32,48},{48,0},{1,17},{17,33},{33,49},{49,1},{2,18}... | collective-permute-start | bytes 589832 | tf_op jit(solution)/shard_map/ppermute | solution.py:46
  83.0 10.9 %collective-permute-start.11 = (bf16[128,768]{1,0:T(8,128)(2,1)S(1)}, bf16[128,768]{1,0:T(8,128)(2,1)S(1)}, u32[]{:S(2)}, u32[]{:S(2)}) collective-permute-start(bf16[128,768]{1,0:T(8,128)(2,1)S(1)} %get-tuple-element.77), channel_id=1, source_target_pairs={{0,32},{16,48},{32,0},{48,16},{1,33},{17,49},{33,1},{49,17},{2,34}... | collective-permute-start | bytes 589832 | tf_op jit(solution)/shard_map/ppermute | solution.py:46
  85.3 10.9 %collective-permute-start.12 = (bf16[128,768]{1,0:T(8,128)(2,1)S(1)}, bf16[128,768]{1,0:T(8,128)(2,1)}, u32[]{:S(2)}, u32[]{:S(2)}) collective-permute-start(bf16[128,768]{1,0:T(8,128)(2,1)S(1)} %get-tuple-element.76), channel_id=1, source_target_pairs={{0,48},{16,0},{32,16},{48,32},{1,49},{17,1},{33,17},{49,33},{2,50}... | collective-permute-start | bytes 589832 | tf_op jit(solution)/shard_map/ppermute | solution.py:46
  86.5 19.9 %collective-permute-start.8 = (bf16[384,768]{1,0:T(8,128)(2,1)}, bf16[384,768]{1,0:T(8,128)(2,1)S(1)}, u32[]{:S(2)}, u32[]{:S(2)}) collective-permute-start(bf16[384,768]{1,0:T(8,128)(2,1)} %get-tuple-element.61), channel_id=1, source_target_pairs={{0,64},{64,0},{1,65},{65,1},{2,66},{66,2},{3,67},{67,3},{4,68},{68... | collective-permute-start | bytes 1769480 | tf_op jit(solution)/shard_map/ppermute | solution.py:28
  88.8 17.6 %all-to-all-start.2 = ((bf16[16,24,768]{2,1,0:T(8,128)(2,1)}), bf16[16,24,768]{2,1,0:T(8,128)(2,1)S(1)}, u32[]{:S(2)}, u32[]{:S(2)}) async-start(bf16[16,24,768]{2,1,0:T(8,128)(2,1)} %broadcast_in_dim.47), calls=%async_computation.2 | async-start | bytes 1179648 | tf_op jit(solution)/shard_map/all_to_all | solution.py:36
  97.9 8.7 %collective-permute-start.13 = (bf16[32,768]{1,0:T(8,128)(2,1)}, bf16[32,768]{1,0:T(8,128)(2,1)S(1)}, u32[]{:S(2)}, u32[]{:S(2)}) collective-permute-start(bf16[32,768]{1,0:T(8,128)(2,1)} %get-tuple-element.82), channel_id=1, source_target_pairs={{0,4},{4,8},{8,12},{12,0},{1,5},{5,9},{9,13},{13,1},{2,6},{6,10},{... | collective-permute-start | bytes 147464 | tf_op jit(solution)/shard_map/ppermute | solution.py:46
  97.9 8.7 %collective-permute-start.14 = (bf16[32,768]{1,0:T(8,128)(2,1)S(1)}, bf16[32,768]{1,0:T(8,128)(2,1)}, u32[]{:S(2)}, u32[]{:S(2)}) collective-permute-start(bf16[32,768]{1,0:T(8,128)(2,1)S(1)} %get-tuple-element.81), channel_id=1, source_target_pairs={{0,8},{4,12},{8,0},{12,4},{1,9},{5,13},{9,1},{13,5},{2,10},{6,14},... | collective-permute-start | bytes 147464 | tf_op jit(solution)/shard_map/ppermute | solution.py:46
  99.6 7.0 %collective-permute-start.15 = (bf16[32,768]{1,0:T(8,128)(2,1)S(1)}, bf16[32,768]{1,0:T(8,128)(2,1)}, u32[]{:S(2)}, u32[]{:S(2)}) collective-permute-start(bf16[32,768]{1,0:T(8,128)(2,1)S(1)} %get-tuple-element.80), channel_id=1, source_target_pairs={{0,12},{4,0},{8,4},{12,8},{1,13},{5,1},{9,5},{13,9},{2,14},{6,2},{... | collective-permute-start | bytes 147464 | tf_op jit(solution)/shard_map/ppermute | solution.py:46
  101.1 10.7 %collective-permute-start.7 = (bf16[384,512]{1,0:T(8,128)(2,1)}, bf16[384,512]{1,0:T(8,128)(2,1)S(1)}, u32[]{:S(2)}, u32[]{:S(2)}) collective-permute-start(bf16[384,512]{1,0:T(8,128)(2,1)} %get-tuple-element.59), channel_id=1, source_target_pairs={{0,64},{64,0},{1,65},{65,1},{2,66},{66,2},{3,67},{67,3},{4,68},{68... | collective-permute-start | bytes 1179656 | tf_op jit(solution)/shard_map/ppermute | solution.py:28
  106.4 2.0 %copy-start.5 = (bf16[384,768]{1,0:T(8,128)(2,1)}, bf16[384,768]{1,0:T(8,128)(2,1)S(1)}, u32[]{:S(2)}) copy-start(bf16[384,768]{1,0:T(8,128)(2,1)S(1)} %collective-permute-done.8.refs_1_) | copy-start | bytes 1769476
  106.4 10.4 %collective-permute-start.17 = (bf16[384,768]{1,0:T(8,128)(2,1)S(1)}, bf16[384,768]{1,0:T(8,128)(2,1)S(1)}, u32[]{:S(2)}, u32[]{:S(2)}) collective-permute-start(bf16[384,768]{1,0:T(8,128)(2,1)S(1)} %bitcast.51), channel_id=1, source_target_pairs={{0,1},{1,0},{2,3},{3,2},{4,5},{5,4},{6,7},{7,6},{8,9},{9,8},{10,11... | collective-permute-start | bytes 1769480 | tf_op jit(solution)/shard_map/ppermute | solution.py:28
  107.5 8.0 %collective-permute-start.16 = (bf16[16,768]{1,0:T(8,128)(2,1)S(1)}, bf16[16,768]{1,0:T(8,128)(2,1)S(1)}, u32[]{:S(2)}, u32[]{:S(2)}) collective-permute-start(bf16[16,768]{1,0:T(8,128)(2,1)S(1)} %fusion.8), channel_id=1, source_target_pairs={{0,2},{2,0},{1,3},{3,1},{4,6},{6,4},{5,7},{7,5},{8,10},{10,8},{9,1... | collective-permute-start | bytes 73736 | tf_op jit(solution)/shard_map/ppermute | solution.py:28
  111.8 3.7 %copy-start.7 = (bf16[16,768]{1,0:T(8,128)(2,1)S(1)}, bf16[16,768]{1,0:T(8,128)(2,1)}, u32[]{:S(2)}) copy-start(bf16[16,768]{1,0:T(8,128)(2,1)} %param.4) | copy-start | bytes 73732
  111.8 0.7 copy-start.6

commit v3 on v2

v3 whole, which is shorter than its diff:
```python
import functools

import jax
import jax.numpy as jnp
from jax import lax
from jax.experimental import pallas as pl
from jax.experimental.pallas import tpu as pltpu
from jax.sharding import Mesh, PartitionSpec as P

F32 = jnp.float32
BF16 = jnp.bfloat16
AXES = ("xl", "y", "z", "xh", "c")
PLANE = ("y", "z")
CHUNKS = (768, 1024, 768, 512)
TILE = 256
MIB = 2**20
LIGHT = 1024
IN_VMEM = pl.BlockSpec(memory_space=pltpu.VMEM)
IN_SMEM = pl.BlockSpec(memory_space=pltpu.SMEM)
IN_HBM = pl.BlockSpec(memory_space=pl.ANY)


def dot(a, b, dims=((1,), (0,))):
    return lax.dot_general(a, b, (dims, ((), ())), preferred_element_type=F32)


def swap(x, axis):
    return lax.ppermute(x, axis, [(0, 1), (1, 0)])


def after(x, *earlier):
    return lax.optimization_barrier((x,) + earlier)[0]


def spread(x, axes, n):
    return lax.all_to_all(jnp.broadcast_to(x[None], (n,) + x.shape), axes, 0, 0, tiled=True)


def pick(x, i, dim=0):
    return lax.dynamic_index_in_dim(x, i, dim, keepdims=False)


def ring_pass(x, axis):
    me = lax.axis_index(axis)
    ring = [[(i, (i + k) % 4) for i in range(4)] for k in range(4)]
    return [pick(x, me)] + [lax.ppermute(pick(x, (me + k) % 4), axis, ring[k]) for k in (1, 2, 3)]


def add_up(blocks):
    return sum(b.astype(F32) for b in blocks)


def x_sum(x, *earlier):
    there = [lax.ppermute(x, ("xl", "xh"), [(i, i ^ k) for i in range(4)]) for k in (1, 2, 3)]
    there = [after(b, *earlier).astype(F32) for b in there]
    return (x.astype(F32) + there[0]) + (there[1] + there[2])


def kernel_call(kernel, ins, places, outs, scratch=(), flops=0, moved=0, limit=20, **more):
    specs = {"s": IN_SMEM, "v": IN_VMEM, "h": IN_HBM}
    given = [
        pltpu.with_memory_space_constraint(x, pltpu.HBM) if p == "h" else x
        for x, p in zip(ins, places)
    ]
    return pl.pallas_call(
        kernel,
        out_shape=[o for _, o in outs],
        in_specs=[specs[p] for p in places],
        out_specs=[specs[p] for p, _ in outs],
        scratch_shapes=scratch,
        cost_estimate=pl.CostEstimate(flops=LIGHT, bytes_accessed=LIGHT, transcendentals=0),
        compiler_params=pltpu.CompilerParams(vmem_limit_bytes=limit * MIB),
        **more,
    )(*given)


def vmem(shape, dtype=BF16):
    return ("v", jax.ShapeDtypeStruct(shape, dtype))


def hbm(shape, dtype=BF16):
    return ("h", pltpu.HBM(shape, dtype))


def start_all(copies):
    for c in copies:
        c.start()
    return copies


def wait_all(copies):
    for c in copies:
        c.wait()


def cast_kernel(at, t_hbm, out, slots, done, in_sems, out_sems):
    n_slot, piece = slots.shape[0], slots.shape[1]
    per_core = t_hbm.shape[0] // piece
    steps = 2 * per_core

    def read(s):
        core = at[0] if s < per_core else 1 - at[0]
        src = t_hbm.at[pl.ds((s % per_core) * piece, piece), core]
        return pltpu.make_async_copy(src, slots.at[s % n_slot], in_sems.at[s % n_slot])

    def write(s):
        dst = out.at[pl.ds(s * piece, piece)]
        return pltpu.make_async_copy(done.at[s % n_slot], dst, out_sems.at[s % n_slot])

    for s in range(n_slot):
        read(s).start()
    for s in range(steps):
        read(s).wait()
        if s >= n_slot:
            write(s - n_slot).wait()
        done[s % n_slot] = slots[s % n_slot].astype(F32).astype(BF16)
        write(s).start()
        if s + n_slot < steps:
            read(s + n_slot).start()
    for s in range(steps - n_slot, steps):
        write(s).wait()


def cast_targets(at, targets, rows):
    labels = targets.shape[1]
    tall = targets.reshape(32, 2, rows, labels)
    (out,) = kernel_call(
        cast_kernel,
        (at, tall),
        "sh",
        [hbm((64, rows, labels))],
        scratch=[
            pltpu.VMEM((4, 4, rows, labels), jnp.int32),
            pltpu.VMEM((4, 4, rows, labels), BF16),
            pltpu.SemaphoreType.DMA((4,)),
            pltpu.SemaphoreType.DMA((4,)),
        ],
        flops=10**9,
        moved=6 * targets.size,
    )
    return out.reshape(64 * rows, labels)


def err_of(logits, t, scale):
    return ((jax.nn.sigmoid(logits) - t.astype(F32)) * scale).astype(BF16)


def emb_rows(rows, hid, enc_w, emb, slope):
    for d in range(0, hid.shape[1], TILE):
        cut = pl.ds(d, TILE)
        act = jnp.tanh(dot(hid[...], enc_w[:, cut]))
        emb[rows, cut] = (hid[:, cut].astype(F32) + act).astype(BF16)
        slope[rows, cut] = (1.0 - act * act).astype(BF16)


def turn(rows, x, x_t):
    for d in range(0, x.shape[1], TILE):
        x_t[pl.ds(d, TILE), rows] = x[:, pl.ds(d, TILE)].T


def own_kernel(first, mine, enc_w, w_hbm, t_hbm, emb, slope, hid_t, emb_t, w, t, sems):
    n = mine.shape[0]
    now, rows = pl.ds(0, first), pl.ds(0, n)
    chunk = start_all([
        pltpu.make_async_copy(w_hbm.at[:, now], w.at[:, now], sems.at[0]),
        pltpu.make_async_copy(t_hbm.at[:, now], t.at[:, now], sems.at[1]),
    ])
    emb_rows(rows, mine, enc_w, emb, slope)
    turn(rows, mine, hid_t)
    turn(rows, emb.at[rows], emb_t)
    wait_all(chunk)


def both_halves(at, emb_t, err, lo, size, product):
    half = emb_t.shape[0] // 2
    for d in range(lo, lo + size, TILE):
        cut = pl.ds(d, TILE)
        product[:, cut] = dot(emb_t[...], err[:, cut]).astype(BF16)
    send = pl.ds(pl.multiple_of((1 - at[1]) * half, half), half)
    keep = pl.ds(pl.multiple_of(at[1] * half, half), half)
    return product.at[send, pl.ds(lo, size)], product.at[keep, pl.ds(lo, size)]


def front_kernel(
    scale, at, other, enc_w, w_hbm, t_hbm, emb0, slope0, hid_t0, emb_t0, w0, t0,
    emb, slope, hid_t, emb_t, w, t, err, gone, kept, product, sems,
):
    n = other.shape[0]
    first = err.shape[1]
    rows, later = pl.ds(n, n), pl.ds(first, w.shape[1] - first)
    copies = start_all([
        pltpu.make_async_copy(w_hbm.at[:, later], w.at[:, later], sems.at[0]),
        pltpu.make_async_copy(t_hbm.at[:, later], t.at[:, later], sems.at[1]),
    ])
    emb_rows(rows, other, enc_w, emb, slope)
    turn(rows, emb.at[rows], emb_t)
    for d in range(0, first, TILE):
        cut = pl.ds(d, TILE)
        err[:, cut] = err_of(dot(emb[...], w[:, cut]), t[:, cut], scale)
    send, keep = both_halves(at, emb_t, err, 0, first, product)
    copies += start_all([
        pltpu.make_async_copy(send, gone, sems.at[2]),
        pltpu.make_async_copy(keep, kept.at[:, pl.ds(0, first)], sems.at[3]),
    ])
    turn(rows, other, hid_t)
    wait_all(copies)


def main_kernel(scale, at, emb, slope, hid_t, emb_t, w, t, err0, kept0, *refs):
    enc_send, enc_keep, kept, part_own, part_other, *refs = refs
    *gone, err, product, parts_v, steep, sems = refs
    n_all, width = emb.shape
    half, n = width // 2, n_all // 2
    start, rest = err0.shape[1], err.shape[1]
    copies = []
    lo = 0
    for k, g in enumerate(gone):
        size = g.shape[1]
        for d in range(lo, lo + size, TILE):
            cut, wide = pl.ds(d, TILE), pl.ds(d + start, TILE)
            err[:, cut] = err_of(dot(emb[...], w[:, wide]), t[:, wide], scale)
        send, keep = both_halves(at, emb_t, err, lo, size, product)
        copies += start_all([
            pltpu.make_async_copy(send, g, sems.at[2 + 2 * k]),
            pltpu.make_async_copy(keep, kept.at[:, pl.ds(start + lo, size)], sems.at[3 + 2 * k]),
        ])
        lo += size
    transposed = ((1,), (1,))
    for i, part in ((1, part_other), (0, part_own)):
        rows = pl.ds(i * n, n)
        for d in range(0, width, TILE):
            cut = pl.ds(d, TILE)
            p = dot(err0[rows, :], w[cut, pl.ds(0, start)], transposed)
            p = p + dot(err[rows, :], w[cut, pl.ds(start, rest)], transposed)
            parts_v[rows, cut] = p.astype(BF16)
            steep[rows, cut] = (p * slope[rows, cut].astype(F32)).astype(BF16)
        copies += start_all([pltpu.make_async_copy(parts_v.at[rows], part, sems.at[i])])
    for lo, out in ((1 - at[0], enc_send), (at[0], enc_keep)):
        turned = pl.ds(pl.multiple_of(lo * half, half), half)
        for d in range(0, width, TILE):
            cut = pl.ds(d, TILE)
            out[:, cut] = dot(hid_t[turned, :], steep[:, cut]).astype(BF16)
    wait_all(copies)


def sum_kernel(a, b, out, total, sem):
    total[...] = (a[...].astype(F32) + b[...].astype(F32)).astype(BF16)
    copy = pltpu.make_async_copy(total, out, sem)
    copy.start()
    copy.wait()


def add_kernel(start, sizes, direct, kept, *refs):
    n = len(sizes)
    come, (out, mine, theirs, sems) = refs[:n], refs[n:]
    cuts = [pl.ds(sum(sizes[:i]), size) for i, size in enumerate(sizes)]
    places = [pl.ds(start + sum(sizes[:i]), size) for i, size in enumerate(sizes)]
    reads = []
    for i, (cut, place) in enumerate(zip(cuts, places)):
        reads.append(start_all([pltpu.make_async_copy(kept.at[:, place], mine.at[:, cut], sems.at[3 * i])]))
        if not direct:
            reads[i] += start_all([pltpu.make_async_copy(come[i], theirs.at[:, cut], sems.at[3 * i + 1])])
    writes = []
    for i, (cut, place) in enumerate(zip(cuts, places)):
        wait_all(reads[i])
        more = come[i][...] if direct else theirs[:, cut]
        mine[:, cut] = (mine[:, cut].astype(F32) + more.astype(F32)).astype(BF16)
        writes += start_all([pltpu.make_async_copy(mine.at[:, cut], out.at[:, place], sems.at[3 * i + 2])])
    wait_all(writes)


def add_in_place(kept, start, come, direct=False):
    half = kept.shape[0]
    sizes = [c.shape[1] for c in come]
    size = 0 if direct else sum(sizes)
    (out,) = kernel_call(
        functools.partial(add_kernel, start, sizes, direct),
        (kept, *come),
        "h" + ("v" if direct else "h") * len(come),
        [hbm(kept.shape)],
        scratch=[
            pltpu.VMEM((half, sum(sizes)), BF16),
            pltpu.VMEM((half, max(size, 128)), BF16),
            pltpu.SemaphoreType.DMA((3 * len(come),)),
        ],
        input_output_aliases={0: 0},
    )
    return out


def body(hidden, enc_weight, cls_weight, targets):
    core = lax.axis_index("c")
    dp = lax.axis_index("xl")
    far = lax.axis_index("xh")
    at = jnp.stack([core, dp]).astype(jnp.int32)
    rows, width = hidden.shape
    labels = cls_weight.shape[1]
    half = width // 2
    n_all = 64 * rows
    n_own = n_all // 2
    scale = float(1.0 / (2048.0**0.5))

    mine = spread(hidden, ("y", "z", "xh"), 32)
    t = cast_targets(at, targets, rows)
    mine, t = lax.optimization_barrier((mine, t))
    other = swap(mine, "c").reshape(n_own, width)
    mine = mine.reshape(n_own, width)

    first, rest = CHUNKS[0], labels - CHUNKS[0]
    starts = [sum(CHUNKS[:j]) for j in range(len(CHUNKS))]
    shared = [vmem((n_all, width))] * 2 + [vmem((width, n_all))] * 2
    shared += [vmem((width, labels)), vmem((n_all, labels))]
    half_done = kernel_call(
        functools.partial(own_kernel, first),
        (mine, enc_weight, cls_weight, t),
        "vvhh",
        shared,
        scratch=[pltpu.SemaphoreType.DMA((2,))],
    )
    *shared, err0, gone0, kept = kernel_call(
        functools.partial(front_kernel, scale),
        (at, other, enc_weight, cls_weight, t, *half_done),
        "svvhhvvvvvv",
        shared + [vmem((n_all, first)), hbm((half, first)), hbm((half, labels))],
        scratch=[pltpu.VMEM((width, first), BF16), pltpu.SemaphoreType.DMA((4,))],
        input_output_aliases={5 + i: i for i in range(6)},
    )
    gone0_in = swap(gone0, "xl")
    enc_send, enc_keep, kept, part_own, part_other, gone1, gone2, gone3 = kernel_call(
        functools.partial(main_kernel, scale),
        (at, *shared, err0, kept),
        "svvvvvvvh",
        [vmem((half, width))] * 2
        + [hbm((half, labels))]
        + [hbm((n_own, width))] * 2
        + [hbm((half, c)) for c in CHUNKS[1:]],
        scratch=[
            pltpu.VMEM((n_all, rest), BF16),
            pltpu.VMEM((width, rest), BF16),
            pltpu.VMEM((n_all, width), BF16),
            pltpu.VMEM((n_all, width), BF16),
            pltpu.SemaphoreType.DMA((2 * len(CHUNKS),)),
        ],
        input_output_aliases={8: 2},
    )
    enc_in = swap(after(enc_send, gone0_in), "c")
    gone1_in = swap(gone1, "xl")

    (enc_sent,) = kernel_call(
        sum_kernel,
        (enc_keep, enc_in),
        "vv",
        [hbm((half, width))],
        scratch=[pltpu.VMEM((half, width), BF16), pltpu.SemaphoreType.DMA],
    )
    enc = enc_sent
    enc = lax.all_to_all(enc.reshape(16, half // 16, width), PLANE, 0, 0, tiled=True)
    cls_grad = add_in_place(after(kept, enc_sent), 0, (gone0_in,))
    enc_part = jnp.sum(after(enc, gone1_in, cls_grad).astype(F32), 0).astype(BF16)

    sums_in = swap(part_other, "c")
    sums = after((part_own.astype(F32) + sums_in.astype(F32)).astype(BF16), enc_sent)
    sums = ring_pass(sums.reshape(4, 4 * 2 * rows, width), "y")

    enc = x_sum(enc_part, *sums[1:]).astype(BF16)
    gone2_in, gone3_in = swap(after(gone2, enc), "xl"), swap(after(gone3, enc), "xl")
    enc_half = after(spread(enc, PLANE, 16), gone2_in).reshape(half, width)
    enc_rest = swap(enc_half, "c")
    is_mine = (jnp.arange(2) == core)[:, None, None]
    enc_grad = jnp.where(is_mine, enc_half[None], enc_rest[None]).astype(F32).reshape(width, width)

    sums = [after(b, enc) for b in sums]
    sums = add_up(sums).astype(BF16).reshape(4, 2 * rows, width)
    sums = [after(b, enc_half) for b in ring_pass(sums, "z")]
    sums = add_up(sums).reshape(2, rows, width)
    emb_grad = pick(sums, far) + swap(pick(sums, 1 - far).astype(BF16), "xh").astype(F32)
    act_own = jnp.tanh(dot(hidden, enc_weight))
    pre_grad = (emb_grad * (1.0 - act_own * act_own)).astype(BF16)
    input_grad = (emb_grad + dot(pre_grad, enc_weight, ((1,), (1,)))).astype(BF16)

    cls_grad = add_in_place(after(cls_grad, enc_half), starts[1], (gone1_in, gone2_in))
    cls_grad = add_in_place(after(cls_grad, input_grad, enc_grad), starts[3], (gone3_in,), direct=True)
    return (cls_grad, input_grad, enc_grad)


def solution(mesh):
    grid = Mesh(mesh.devices.reshape(2, 4, 4, 2, 2), AXES)
    label = AXES[1:]
    placed = (P(AXES, None), P(), P(None, label), P("xl", label))
    return jax.shard_map(
        body,
        mesh=grid,
        in_specs=placed,
        out_specs=(P("xl", label), P(AXES, None), P()),
        check_vma=False,
    )
```

time: 120 us -> 113 us (0.942)
  Pallas kernels: 47.6 us -> 38.1 us
  starting transfers between devices: 36.4 us -> 43.7 us
  other arithmetic: 6.04 us -> 4.09 us
  waiting for transfers between devices: 21 us -> 19.2 us
  local copies, waits for them, and re-layouts: 5 us -> 3.36 us
    pallas_call x7 -> x8, Pallas kernels: 47.6 us -> 38.1 us  [kernel_call(): pl.pallas_call(kernel, out_shape=[o for _, o in outs], in_specs=[specs[p]...]
    ppermute x6, starting transfers between devices: 6.71 us -> 12.1 us  [ring_pass(): lax.ppermute(pick(x, (me + k) % 4), axis, ring[k])]
    ppermute x9, waiting for transfers between devices: 10.3 us -> 5.46 us  [swap(): return lax.ppermute(x, axis, [(0, 1), (1, 0)])]
    all_to_all x2, waiting for transfers between devices: 7.85 us -> 10.3 us  [spread(): lax.all_to_all(jnp.broadcast_to(x[None], (n,) + x.shape), axes, 0, 0, til...]
    unnamed x16 -> x10, local copies, waits for them, and re-layouts: 1.66 us -> 0.02 us
    all_to_all x2, starting transfers between devices: 15.3 us -> 16.8 us  [spread(): lax.all_to_all(jnp.broadcast_to(x[None], (n,) + x.shape), axes, 0, 0, til...]
    ppermute x3, waiting for transfers between devices: 0.01 us -> 1.28 us  [x_sum(): lax.ppermute(x, ('xl', 'xh'), [(i, i ^ k) for i in range(4)])]
  transfers between devices with their start and end apart: 21 -> 21, of which waited for: 6 -> 10; matrix products, arithmetic and copies ran while one was open for 6% -> 6% of each run, Pallas kernels for 33% -> 28%
where the time goes in v3:
time: 113 us; the launch traced here: 111 us
  starting transfers between devices  43.7 us (39%)
  Pallas kernels  38.1 us (34%)
  waiting for transfers between devices  19.2 us (17%)
  other arithmetic  4.09 us (4%)
  local copies, waits for them, and re-layouts  3.36 us (3%)
  matrix products  1.3 us (1%)
    pallas_call x8, Pallas kernels, kernel_call(): pl.pallas_call(kernel, out_shape=[o for _, o in outs], in_specs=[specs[p]...  38.1 us
    all_to_all x2, starting transfers between devices, spread(): lax.all_to_all(jnp.broadcast_to(x[None], (n,) + x.shape), axes, 0, 0, til...  16.8 us
    ppermute x6, starting transfers between devices, ring_pass(): lax.ppermute(pick(x, (me + k) % 4), axis, ring[k])  12.1 us
    all_to_all x2, waiting for transfers between devices, spread(): lax.all_to_all(jnp.broadcast_to(x[None], (n,) + x.shape), axes, 0, 0, til...  10.3 us
    ppermute x9, starting transfers between devices, swap(): return lax.ppermute(x, axis, [(0, 1), (1, 0)])  7.01 us
    ppermute x9, waiting for transfers between devices, swap(): return lax.ppermute(x, axis, [(0, 1), (1, 0)])  5.46 us
    ppermute x3, starting transfers between devices, x_sum(): lax.ppermute(x, ('xl', 'xh'), [(i, i ^ k) for i in range(4)])  4.18 us
    all_to_all x1, starting transfers between devices, body(): lax.all_to_all(enc.reshape(16, half // 16, width), PLANE, 0, 0, tiled=True)  3.73 us
  transfers between devices with their start and end apart: 21, of which 10 were waited for; matrix products, arithmetic and copies ran while one was open for 6% of the time, Pallas kernels for 28%

profile of v3, /device:TPU:0, one launch (start us, length us, event | category | flops | bytes accessed | tf_op | source)
XLA Modules:
  0.0 110.9 jit_solution(9706787770694759698)
XLA Ops:
  0.6 1.7 %broadcast_in_dim.46 = bf16[32,16,768]{2,1,0:T(8,128)(2,1)} broadcast(bf16[16,768]{1,0:T(8,128)(2,1)} %param.4), dimensions={1,2} | broadcast | bytes 811008 | tf_op jit(solution)/shard_map/broadcast_in_dim | solution.py:36
  2.3 10.9 %all-to-all-start = ((bf16[32,16,768]{2,1,0:T(8,128)(2,1)}), bf16[32,16,768]{2,1,0:T(8,128)(2,1)S(1)}, u32[]{:S(2)}, u32[]{:S(2)}) async-start(bf16[32,16,768]{2,1,0:T(8,128)(2,1)} %broadcast_in_dim.46), calls=%async_computation | async-start | bytes 1572864 | tf_op jit(solution)/shard_map/all_to_all | solution.py:36
  13.2 0.1 pad_add_fusion.at
  13.3 8.6 %shard_map.67 = bf16[64,16,3072]{2,1,0:T(8,128)(2,1)} custom-call(s32[2]{0:T(128)S(1)} %pad_add_fusion.at, s32[32,2,16,3072]{3,2,1,0:T(8,128)} %bitcast.50), custom_call_target="tpu_custom_call" | custom-call | flops 1024 | bytes 1024 | tf_op jit(solution)/shard_map/pallas_call | solution.py:65
  21.9 7.9 %all-to-all-done = bf16[32,16,768]{2,1,0:T(8,128)(2,1)S(1)} async-done(((bf16[32,16,768]{2,1,0:T(8,128)(2,1)}), bf16[32,16,768]{2,1,0:T(8,128)(2,1)S(1)}, u32[]{:S(2)}, u32[]{:S(2)}) %all-to-all-start) | async-done | bytes 786464 | tf_op jit(solution)/shard_map/all_to_all | solution.py:36
  29.7 2.4 %shard_map.68 = (bf16[1024,768]{1,0:T(8,128)(2,1)S(1)}, bf16[1024,768]{1,0:T(8,128)(2,1)S(1)}, bf16[768,1024]{1,0:T(8,128)(2,1)S(1)}, bf16[768,1024]{1,0:T(8,128...) custom-call(bf16[512,768]{1,0:T(8,128)(2,1)S(1)} %bitcast.46, bf16[768,768]{1,0:T(8,128)(2,1)S(1)} %copy-done, ...), custom_call_target="tpu_custom_call" | custom-call | flops 1024 | bytes 1024 | tf_op jit(solution)/shard_map/pallas_call | solution.py:65
  32.2 4.9 %shard_map.69 = (bf16[1024,768]{1,0:T(8,128)(2,1)S(1)}, bf16[1024,768]{1,0:T(8,128)(2,1)S(1)}, bf16[768,1024]{1,0:T(8,128)(2,1)S(1)}, bf16[768,1024]{1,0:T(8,128...) custom-call(s32[2]{0:T(128)S(1)} %pad_add_fusion.at, ...), custom_call_target="tpu_custom_call", output_to_operand_aliasing={{0}: (5, {}), {1}: (6, {}), {2}: (7, {}), {3}: (8, {}), {4}... | custom-call | flops 1024 | bytes 1024 | tf_op jit(solution)/shard_map/pallas_call | solution.py:65
  37.1 0.9 collective-permute-start.1
  38.0 14.4 %shard_map.70 = (bf16[384,768]{1,0:T(8,128)(2,1)S(1)}, bf16[384,768]{1,0:T(8,128)(2,1)S(1)}, bf16[384,3072]{1,0:T(8,128)(2,1)}, bf16[512,768]{1,0:T(8,128)(2,1)}...) custom-call(s32[2]{0:T(128)S(1)} %pad_add_fusion.at, ...), custom_call_target="tpu_custom_call", output_to_operand_aliasing={{2}: (8, {})} | custom-call | flops 1024 | bytes 1024 | tf_op jit(solution)/shard_map/pallas_call | solution.py:65
  52.4 0.3 collective-permute-start.5
  52.6 0.7 collective-permute-done.1.refs_0_
  53.3 1.1 collective-permute-start.3
  54.4 1.2 %collective-permute-done.2.b = bf16[384,768]{1,0:T(8,128)(2,1)S(1)} collective-permute-done((bf16[384,768]{1,0:T(8,128)(2,1)S(1)}, bf16[384,768]{1,0:T(8,128)(2,1)S(1)}, u32[]{:S(2)}, u32[]{:S(2)}) %collective-permute-start.2) | collective-permute-done | bytes 589856 | tf_op jit(solution)/shard_map/ppermute | solution.py:28
  55.6 1.0 shard_map.71
  56.6 3.7 %all-to-all-start.1 = ((bf16[16,24,768]{2,1,0:T(8,128)(2,1)}), bf16[16,24,768]{2,1,0:T(8,128)(2,1)S(1)}, u32[]{:S(2)}, u32[]{:S(2)}) async-start(bf16[16,24,768]{2,1,0:T(8,128)(2,1)} %bitcast.52), calls=%async_computation.1 | async-start | bytes 1179648 | tf_op jit(solution)/shard_map/all_to_all | solution.py:357
  60.3 1.3 %add_convert_fusion = bf16[512,768]{1,0:T(8,128)(2,1)S(1)} fusion(bf16[512,768]{1,0:T(8,128)(2,1)} %collective-permute-done.5, bf16[512,768]{1,0:T(8,128)(2,1)S(1)} %copy-done.1), kind=kLoop, calls=%fused_computation | loop fusion | flops 1572864 | bytes 2359296 | tf_op jit(solution)/shard_map/convert_element_type | solution.py:362
  61.6 0.1 dynamic-slice_bitcast_fusion
  61.7 1.9 %collective-permute-start.6 = (bf16[128,768]{1,0:T(8,128)(2,1)S(1)}, bf16[128,768]{1,0:T(8,128)(2,1)S(1)}, u32[]{:S(2)}, u32[]{:S(2)}) collective-permute-start(bf16[128,768]{1,0:T(8,128)(2,1)S(1)} %get-tuple-element.96), channel_id=1, source_target_pairs={{0,16},{16,32},{32,48},{48,0},{1,17},{17,33},{33,49},{49,1},{2,18}... | collective-permute-start | bytes 589832 | tf_op jit(solution)/shard_map/ppermute | solution.py:46
  63.6 2.7 %collective-permute-start.7 = (bf16[128,768]{1,0:T(8,128)(2,1)S(1)}, bf16[128,768]{1,0:T(8,128)(2,1)S(1)}, u32[]{:S(2)}, u32[]{:S(2)}) collective-permute-start(bf16[128,768]{1,0:T(8,128)(2,1)S(1)} %get-tuple-element.95), channel_id=1, source_target_pairs={{0,32},{16,48},{32,0},{48,16},{1,33},{17,49},{33,1},{49,17},{2,34}... | collective-permute-start | bytes 589832 | tf_op jit(solution)/shard_map/ppermute | solution.py:46
  66.3 1.4 %collective-permute-start.8 = (bf16[128,768]{1,0:T(8,128)(2,1)S(1)}, bf16[128,768]{1,0:T(8,128)(2,1)S(1)}, u32[]{:S(2)}, u32[]{:S(2)}) collective-permute-start(bf16[128,768]{1,0:T(8,128)(2,1)S(1)} %get-tuple-element.94), channel_id=1, source_target_pairs={{0,48},{16,0},{32,16},{48,32},{1,49},{17,1},{33,17},{49,33},{2,50}... | collective-permute-start | bytes 589832 | tf_op jit(solution)/shard_map/ppermute | solution.py:46
  67.8 2.2 %shard_map.72.kept = bf16[384,3072]{1,0:T(8,128)(2,1)} custom-call(bf16[384,3072]{1,0:T(8,128)(2,1)} %get-tuple-element.69.kept, bf16[384,768]{1,0:T(8,128)(2,1)} %copy-done.3), custom_call_target="tpu_custom_call", output_to_operand_aliasing={{}: (0, {})} | custom-call | flops 1024 | bytes 1024 | tf_op jit(solution)/shard_map/pallas_call | solution.py:65
  70.0 3.6 %collective-permute-done.3.refs_0_ = bf16[384,1024]{1,0:T(8,128)(2,1)} collective-permute-done((bf16[384,1024]{1,0:T(8,128)(2,1)}, bf16[384,1024]{1,0:T(8,128)(2,1)}, u32[]{:S(2)}, u32[]{:S(2)}) %collective-permute-start.3) | collective-permute-done | bytes 786464 | tf_op jit(solution)/shard_map/ppermute | solution.py:28
  73.6 0.2 all-to-all-done.1
  73.8 0.1 reduce_sum.12
  73.9 1.2 %collective-permute-start.4 = (bf16[24,768]{1,0:T(8,128)(2,1)S(1)}, bf16[24,768]{1,0:T(8,128)(2,1)S(1)}, u32[]{:S(2)}, u32[]{:S(2)}) collective-permute-start(bf16[24,768]{1,0:T(8,128)(2,1)S(1)} %reduce_sum.12), channel_id=1, source_target_pairs={{0,2},{2,0},{64,66},{66,64},{1,3},{3,1},{65,67},{67,65},{4,6},{6,4... | collective-permute-start | bytes 110600 | tf_op jit(solution)/shard_map/ppermute | solution.py:54
  75.1 0.4 collective-permute-start.9
  75.5 2.6 %collective-permute-start.10 = (bf16[24,768]{1,0:T(8,128)(2,1)S(1)}, bf16[24,768]{1,0:T(8,128)(2,1)S(1)}, u32[]{:S(2)}, u32[]{:S(2)}) collective-permute-start(bf16[24,768]{1,0:T(8,128)(2,1)S(1)} %reduce_sum.12), channel_id=1, source_target_pairs={{0,66},{2,64},{64,2},{66,0},{1,67},{3,65},{65,3},{67,1},{4,70},{6,... | collective-permute-start | bytes 110600 | tf_op jit(solution)/shard_map/ppermute | solution.py:54
  78.1 1.3 %collective-permute-done.7 = bf16[128,768]{1,0:T(8,128)(2,1)S(1)} collective-permute-done((bf16[128,768]{1,0:T(8,128)(2,1)S(1)}, bf16[128,768]{1,0:T(8,128)(2,1)S(1)}, u32[]{:S(2)}, u32[]{:S(2)}) %collective-permute-start.7) | collective-permute-done | bytes 196640 | tf_op jit(solution)/shard_map/ppermute | solution.py:46
  79.4 0.1 collective-permute-done.4
  79.4 1.2 %collective-permute-done.10 = bf16[24,768]{1,0:T(8,128)(2,1)S(1)} collective-permute-done((bf16[24,768]{1,0:T(8,128)(2,1)S(1)}, bf16[24,768]{1,0:T(8,128)(2,1)S(1)}, u32[]{:S(2)}, u32[]{:S(2)}) %collective-permute-start.10) | collective-permute-done | bytes 36896 | tf_op jit(solution)/shard_map/ppermute | solution.py:54
  80.7 0.8 collective-permute-start.11
  81.5 0.9 broadcast_in_dim.47
  82.4 5.9 %all-to-all-start.2 = ((bf16[16,24,768]{2,1,0:T(8,128)(2,1)}), bf16[16,24,768]{2,1,0:T(8,128)(2,1)S(1)}, u32[]{:S(2)}, u32[]{:S(2)}) async-start(bf16[16,24,768]{2,1,0:T(8,128)(2,1)} %broadcast_in_dim.47), calls=%async_computation.2 | async-start | bytes 1179648 | tf_op jit(solution)/shard_map/all_to_all | solution.py:36
  88.3 0.1 add_convert_fusion.1
  88.4 0.6 dynamic-slice_bitcast_fusion.7
  89.1 1.9 %collective-permute-start.12 = (bf16[32,768]{1,0:T(8,128)(2,1)}, bf16[32,768]{1,0:T(8,128)(2,1)S(1)}, u32[]{:S(2)}, u32[]{:S(2)}) collective-permute-start(bf16[32,768]{1,0:T(8,128)(2,1)} %get-tuple-element.100), channel_id=1, source_target_pairs={{0,4},{4,8},{8,12},{12,0},{1,5},{5,9},{9,13},{13,1},{2,6},{6,10},{... | collective-permute-start | bytes 147464 | tf_op jit(solution)/shard_map/ppermute | solution.py:46
  91.0 2.7 %collective-permute-start.13 = (bf16[32,768]{1,0:T(8,128)(2,1)S(1)}, bf16[32,768]{1,0:T(8,128)(2,1)}, u32[]{:S(2)}, u32[]{:S(2)}) collective-permute-start(bf16[32,768]{1,0:T(8,128)(2,1)S(1)} %get-tuple-element.99), channel_id=1, source_target_pairs={{0,8},{4,12},{8,0},{12,4},{1,9},{5,13},{9,1},{13,5},{2,10},{6,14},... | collective-permute-start | bytes 147464 | tf_op jit(solution)/shard_map/ppermute | solution.py:46
  93.6 1.5 %collective-permute-start.14 = (bf16[32,768]{1,0:T(8,128)(2,1)S(1)}, bf16[32,768]{1,0:T(8,128)(2,1)}, u32[]{:S(2)}, u32[]{:S(2)}) collective-permute-start(bf16[32,768]{1,0:T(8,128)(2,1)S(1)} %get-tuple-element.98), channel_id=1, source_target_pairs={{0,12},{4,0},{8,4},{12,8},{1,13},{5,1},{9,5},{13,9},{2,14},{6,2},{... | collective-permute-start | bytes 147464 | tf_op jit(solution)/shard_map/ppermute | solution.py:46
  95.1 1.2 %collective-permute-start.17 = (bf16[384,512]{1,0:T(8,128)(2,1)}, bf16[384,512]{1,0:T(8,128)(2,1)S(1)}, u32[]{:S(2)}, u32[]{:S(2)}) collective-permute-start(bf16[384,512]{1,0:T(8,128)(2,1)} %get-tuple-element.92), channel_id=1, source_target_pairs={{0,64},{64,0},{1,65},{65,1},{2,66},{66,2},{3,67},{67,3},{4,68},{68... | collective-permute-start | bytes 1179656 | tf_op jit(solution)/shard_map/ppermute | solution.py:28
  96.3 2.5 %all-to-all-done.2 = bf16[16,24,768]{2,1,0:T(8,128)(2,1)S(1)} async-done(((bf16[16,24,768]{2,1,0:T(8,128)(2,1)}), bf16[16,24,768]{2,1,0:T(8,128)(2,1)S(1)}, u32[]{:S(2)}, u32[]{:S(2)}) %all-to-all-start.2) | async-done | bytes 589856 | tf_op jit(solution)/shard_map/all_to_all | solution.py:36
  98.8 0.6 collective-permute-done.13
  99.4 0.8 convert_add_fusion
  100.2 2.8 %collective-permute-start.15 = (bf16[16,768]{1,0:T(8,128)(2,1)S(1)}, bf16[16,768]{1,0:T(8,128)(2,1)S(1)}, u32[]{:S(2)}, u32[]{:S(2)}) collective-permute-start(bf16[16,768]{1,0:T(8,128)(2,1)S(1)} %fusion.8), channel_id=1, source_target_pairs={{0,2},{2,0},{1,3},{3,1},{4,6},{6,4},{5,7},{7,5},{8,10},{10,8},{9,1... | collective-permute-start | bytes 73736 | tf_op jit(solution)/shard_map/ppermute | solution.py:28
  103.0 0.1 broadcast_in_dim.48
  103.1 2.7 %shard_map.73.kept = bf16[384,3072]{1,0:T(8,128)(2,1)} custom-call(bf16[384,3072]{1,0:T(8,128)(2,1)} %shard_map.72.kept, bf16[384,1024]{1,0:T(8,128)(2,1)} %collective-permute-done.3.refs_0_, bf16[384,768]{1,0:T(8,128)(2,1)} %copy-done.2), custom_call_target="tpu_custom_call", output_to_operand_aliasing={{}: (0, {})} | custom-call | flops 1024 | bytes 1024 | tf_op jit(solution)/shard_map/pallas_call | solution.py:65
  105.9 1.3 %fusion.5 = bf16[16,768]{1,0:T(8,128)(2,1)} fusion(bf16[768,768]{1,0:T(8,128)(2,1)S(1)} %copy-done, bf16[16,768]{1,0:T(8,128)(2,1)S(1)} %copy-done.4, bf16[16,768]{1,0:T(8,128)(2,1)S(1)} %collective-permute-done.15, f32[2,16,768]{2,1,0:T(8,128)S(1)} %bitcast.57, s32[]{:T(128)S(6)} %select_n.79), kind=kOutput, calls=%fused_computation.9 | convolution fusion | flops 37871616 | bytes 2556928 | tf_op jit(solution)/shard_map/dot_general | solution.py:24
  107.2 1.6 %fusion = f32[768,768]{1,0:T(8,128)} fusion(pred[768]{0:T(1024)(128)(4,1)S(1)} %broadcast_in_dim.49, bf16[384,768]{1,0:T(8,128)(2,1)S(1)} %collective-permute-done.16, bf16[384,768]{1,0:T(8,128)(2,1)S(1)} %bitcast.54), kind=kLoop, calls=%fused_computation.2 | loop fusion | flops 1179648 | bytes 3539712 | tf_op jit(solution)/shard_map/convert_element_type | solution.py:370
  108.8 1.9 %shard_map.74 = bf16[384,3072]{1,0:T(8,128)(2,1)} custom-call(bf16[384,3072]{1,0:T(8,128)(2,1)} %shard_map.73.kept, bf16[384,512]{1,0:T(8,128)(2,1)S(1)} %collective-permute-done.17.refs_0_), custom_call_target="tpu_custom_call", output_to_operand_aliasing={{}: (0, {})} | custom-call | flops 1024 | bytes 1024 | tf_op jit(solution)/shard_map/pallas_call | solution.py:65
  (28 shorter events, 0.1 us)
Async XLA Ops:
  2.3 27.4 %all-to-all-start = ((bf16[32,16,768]{2,1,0:T(8,128)(2,1)}), bf16[32,16,768]{2,1,0:T(8,128)(2,1)S(1)}, u32[]{:S(2)}, u32[]{:S(2)}) async-start(bf16[32,16,768]{2,1,0:T(8,128)(2,1)} %broadcast_in_dim.46), calls=%async_computation | async-start | bytes 1572864 | tf_op jit(solution)/shard_map/all_to_all | solution.py:36
  13.3 16.5 %copy-start = (bf16[768,768]{1,0:T(8,128)(2,1)S(1)}, bf16[768,768]{1,0:T(8,128)(2,1)}, u32[]{:S(2)}) copy-start(bf16[768,768]{1,0:T(8,128)(2,1)} %enc_w.3) | copy-start | bytes 3538948
  29.7 2.5 %collective-permute-start = (bf16[32,16,768]{2,1,0:T(8,128)(2,1)S(1)}, bf16[32,16,768]{2,1,0:T(8,128)(2,1)S(1)}, u32[]{:S(2)}, u32[]{:S(2)}) collective-permute-start(bf16[32,16,768]{2,1,0:T(8,128)(2,1)S(1)} %all-to-all-done), channel_id=1, source_target_pairs={{0,1},{1,0},{2,3},{3,2},{4,5},{5,4},{6,7},{7,6},{8,9},{9,8},{10,11... | collective-permute-start | bytes 2359304 | tf_op jit(solution)/shard_map/ppermute | solution.py:28
  37.1 16.2 %collective-permute-start.1 = (bf16[384,768]{1,0:T(8,128)(2,1)}, bf16[384,768]{1,0:T(8,128)(2,1)S(1)}, u32[]{:S(2)}, u32[]{:S(2)}) collective-permute-start(bf16[384,768]{1,0:T(8,128)(2,1)} %get-tuple-element.67), channel_id=1, source_target_pairs={{0,64},{64,0},{1,65},{65,1},{2,66},{66,2},{3,67},{67,3},{4,68},{68... | collective-permute-start | bytes 1769480 | tf_op jit(solution)/shard_map/ppermute | solution.py:28
  52.4 7.9 %collective-permute-start.5 = (bf16[512,768]{1,0:T(8,128)(2,1)}, bf16[512,768]{1,0:T(8,128)(2,1)}, u32[]{:S(2)}, u32[]{:S(2)}) collective-permute-start(bf16[512,768]{1,0:T(8,128)(2,1)} %get-tuple-element.73), channel_id=1, source_target_pairs={{0,1},{1,0},{2,3},{3,2},{4,5},{5,4},{6,7},{7,6},{8,9},{9,8},{10,11... | collective-permute-start | bytes 2359304 | tf_op jit(solution)/shard_map/ppermute | solution.py:28
  53.3 8.3 %copy-start.3 = (bf16[384,768]{1,0:T(8,128)(2,1)}, bf16[384,768]{1,0:T(8,128)(2,1)S(1)}, u32[]{:S(2)}) copy-start(bf16[384,768]{1,0:T(8,128)(2,1)S(1)} %collective-permute-done.1.refs_0_) | copy-start | bytes 1769476
  53.3 2.2 %collective-permute-start.2 = (bf16[384,768]{1,0:T(8,128)(2,1)S(1)}, bf16[384,768]{1,0:T(8,128)(2,1)S(1)}, u32[]{:S(2)}, u32[]{:S(2)}) collective-permute-start(bf16[384,768]{1,0:T(8,128)(2,1)S(1)} %get-tuple-element.68), channel_id=1, source_target_pairs={{0,1},{1,0},{2,3},{3,2},{4,5},{5,4},{6,7},{7,6},{8,9},{9,8},{10,11... | collective-permute-start | bytes 1769480 | tf_op jit(solution)/shard_map/ppermute | solution.py:28
  53.3 20.3 %collective-permute-start.3 = (bf16[384,1024]{1,0:T(8,128)(2,1)}, bf16[384,1024]{1,0:T(8,128)(2,1)}, u32[]{:S(2)}, u32[]{:S(2)}) collective-permute-start(bf16[384,1024]{1,0:T(8,128)(2,1)} %get-tuple-element.70), channel_id=1, source_target_pairs={{0,64},{64,0},{1,65},{65,1},{2,66},{66,2},{3,67},{67,3},{4,68},{68... | collective-permute-start | bytes 2359304 | tf_op jit(solution)/shard_map/ppermute | solution.py:28
  56.5 3.8 %copy-start.1 = (bf16[512,768]{1,0:T(8,128)(2,1)S(1)}, bf16[512,768]{1,0:T(8,128)(2,1)}, u32[]{:S(2)}) copy-start(bf16[512,768]{1,0:T(8,128)(2,1)} %get-tuple-element.72) | copy-start | bytes 2359300
  56.6 17.2 %all-to-all-start.1 = ((bf16[16,24,768]{2,1,0:T(8,128)(2,1)}), bf16[16,24,768]{2,1,0:T(8,128)(2,1)S(1)}, u32[]{:S(2)}, u32[]{:S(2)}) async-start(bf16[16,24,768]{2,1,0:T(8,128)(2,1)} %bitcast.52), calls=%async_computation.1 | async-start | bytes 1179648 | tf_op jit(solution)/shard_map/all_to_all | solution.py:357
  61.7 13.8 %collective-permute-start.6 = (bf16[128,768]{1,0:T(8,128)(2,1)S(1)}, bf16[128,768]{1,0:T(8,128)(2,1)S(1)}, u32[]{:S(2)}, u32[]{:S(2)}) collective-permute-start(bf16[128,768]{1,0:T(8,128)(2,1)S(1)} %get-tuple-element.96), channel_id=1, source_target_pairs={{0,16},{16,32},{32,48},{48,0},{1,17},{17,33},{33,49},{49,1},{2,18}... | collective-permute-start | bytes 589832 | tf_op jit(solution)/shard_map/ppermute | solution.py:46
  63.6 15.8 %collective-permute-start.7 = (bf16[128,768]{1,0:T(8,128)(2,1)S(1)}, bf16[128,768]{1,0:T(8,128)(2,1)S(1)}, u32[]{:S(2)}, u32[]{:S(2)}) collective-permute-start(bf16[128,768]{1,0:T(8,128)(2,1)S(1)} %get-tuple-element.95), channel_id=1, source_target_pairs={{0,32},{16,48},{32,0},{48,16},{1,33},{17,49},{33,1},{49,17},{2,34}... | collective-permute-start | bytes 589832 | tf_op jit(solution)/shard_map/ppermute | solution.py:46
  66.3 13.1 %collective-permute-start.8 = (bf16[128,768]{1,0:T(8,128)(2,1)S(1)}, bf16[128,768]{1,0:T(8,128)(2,1)S(1)}, u32[]{:S(2)}, u32[]{:S(2)}) collective-permute-start(bf16[128,768]{1,0:T(8,128)(2,1)S(1)} %get-tuple-element.94), channel_id=1, source_target_pairs={{0,48},{16,0},{32,16},{48,32},{1,49},{17,1},{33,17},{49,33},{2,50}... | collective-permute-start | bytes 589832 | tf_op jit(solution)/shard_map/ppermute | solution.py:46
  73.9 5.5 %collective-permute-start.4 = (bf16[24,768]{1,0:T(8,128)(2,1)S(1)}, bf16[24,768]{1,0:T(8,128)(2,1)S(1)}, u32[]{:S(2)}, u32[]{:S(2)}) collective-permute-start(bf16[24,768]{1,0:T(8,128)(2,1)S(1)} %reduce_sum.12), channel_id=1, source_target_pairs={{0,2},{2,0},{64,66},{66,64},{1,3},{3,1},{65,67},{67,65},{4,6},{6,4... | collective-permute-start | bytes 110600 | tf_op jit(solution)/shard_map/ppermute | solution.py:54
  75.1 4.3 %collective-permute-start.9 = (bf16[24,768]{1,0:T(8,128)(2,1)S(1)}, bf16[24,768]{1,0:T(8,128)(2,1)S(1)}, u32[]{:S(2)}, u32[]{:S(2)}) collective-permute-start(bf16[24,768]{1,0:T(8,128)(2,1)S(1)} %reduce_sum.12), channel_id=1, source_target_pairs={{0,64},{2,66},{64,0},{66,2},{1,65},{3,67},{65,1},{67,3},{4,68},{6,... | collective-permute-start | bytes 110600 | tf_op jit(solution)/shard_map/ppermute | solution.py:54
  75.5 5.2 %collective-permute-start.10 = (bf16[24,768]{1,0:T(8,128)(2,1)S(1)}, bf16[24,768]{1,0:T(8,128)(2,1)S(1)}, u32[]{:S(2)}, u32[]{:S(2)}) collective-permute-start(bf16[24,768]{1,0:T(8,128)(2,1)S(1)} %reduce_sum.12), channel_id=1, source_target_pairs={{0,66},{2,64},{64,2},{66,0},{1,67},{3,65},{65,3},{67,1},{4,70},{6,... | collective-permute-start | bytes 110600 | tf_op jit(solution)/shard_map/ppermute | solution.py:54
  80.7 18.1 %collective-permute-start.11 = (bf16[384,768]{1,0:T(8,128)(2,1)}, bf16[384,768]{1,0:T(8,128)(2,1)S(1)}, u32[]{:S(2)}, u32[]{:S(2)}) collective-permute-start(bf16[384,768]{1,0:T(8,128)(2,1)} %get-tuple-element.79), channel_id=1, source_target_pairs={{0,64},{64,0},{1,65},{65,1},{2,66},{66,2},{3,67},{67,3},{4,68},{68... | collective-permute-start | bytes 1769480 | tf_op jit(solution)/shard_map/ppermute | solution.py:28
  82.4 16.3 %all-to-all-start.2 = ((bf16[16,24,768]{2,1,0:T(8,128)(2,1)}), bf16[16,24,768]{2,1,0:T(8,128)(2,1)S(1)}, u32[]{:S(2)}, u32[]{:S(2)}) async-start(bf16[16,24,768]{2,1,0:T(8,128)(2,1)} %broadcast_in_dim.47), calls=%async_computation.2 | async-start | bytes 1179648 | tf_op jit(solution)/shard_map/all_to_all | solution.py:36
  89.1 9.7 %collective-permute-start.12 = (bf16[32,768]{1,0:T(8,128)(2,1)}, bf16[32,768]{1,0:T(8,128)(2,1)S(1)}, u32[]{:S(2)}, u32[]{:S(2)}) collective-permute-start(bf16[32,768]{1,0:T(8,128)(2,1)} %get-tuple-element.100), channel_id=1, source_target_pairs={{0,4},{4,8},{8,12},{12,0},{1,5},{5,9},{9,13},{13,1},{2,6},{6,10},{... | collective-permute-start | bytes 147464 | tf_op jit(solution)/shard_map/ppermute | solution.py:46
  91.0 8.4 %collective-permute-start.13 = (bf16[32,768]{1,0:T(8,128)(2,1)S(1)}, bf16[32,768]{1,0:T(8,128)(2,1)}, u32[]{:S(2)}, u32[]{:S(2)}) collective-permute-start(bf16[32,768]{1,0:T(8,128)(2,1)S(1)} %get-tuple-element.99), channel_id=1, source_target_pairs={{0,8},{4,12},{8,0},{12,4},{1,9},{5,13},{9,1},{13,5},{2,10},{6,14},... | collective-permute-start | bytes 147464 | tf_op jit(solution)/shard_map/ppermute | solution.py:46
  93.6 5.7 %collective-permute-start.14 = (bf16[32,768]{1,0:T(8,128)(2,1)S(1)}, bf16[32,768]{1,0:T(8,128)(2,1)}, u32[]{:S(2)}, u32[]{:S(2)}) collective-permute-start(bf16[32,768]{1,0:T(8,128)(2,1)S(1)} %get-tuple-element.98), channel_id=1, source_target_pairs={{0,12},{4,0},{8,4},{12,8},{1,13},{5,1},{9,5},{13,9},{2,14},{6,2},{... | collective-permute-start | bytes 147464 | tf_op jit(solution)/shard_map/ppermute | solution.py:46
  95.1 13.7 %collective-permute-start.17 = (bf16[384,512]{1,0:T(8,128)(2,1)}, bf16[384,512]{1,0:T(8,128)(2,1)S(1)}, u32[]{:S(2)}, u32[]{:S(2)}) collective-permute-start(bf16[384,512]{1,0:T(8,128)(2,1)} %get-tuple-element.92), channel_id=1, source_target_pairs={{0,64},{64,0},{1,65},{65,1},{2,66},{66,2},{3,67},{67,3},{4,68},{68... | collective-permute-start | bytes 1179656 | tf_op jit(solution)/shard_map/ppermute | solution.py:28
  98.7 4.4 %copy-start.2 = (bf16[384,768]{1,0:T(8,128)(2,1)}, bf16[384,768]{1,0:T(8,128)(2,1)S(1)}, u32[]{:S(2)}) copy-start(bf16[384,768]{1,0:T(8,128)(2,1)S(1)} %collective-permute-done.11.refs_1_) | copy-start | bytes 1769476
  98.7 8.5 %collective-permute-start.16 = (bf16[384,768]{1,0:T(8,128)(2,1)S(1)}, bf16[384,768]{1,0:T(8,128)(2,1)S(1)}, u32[]{:S(2)}, u32[]{:S(2)}) collective-permute-start(bf16[384,768]{1,0:T(8,128)(2,1)S(1)} %bitcast.53), channel_id=1, source_target_pairs={{0,1},{1,0},{2,3},{3,2},{4,5},{5,4},{6,7},{7,6},{8,9},{9,8},{10,11... | collective-permute-start | bytes 1769480 | tf_op jit(solution)/shard_map/ppermute | solution.py:28
  100.2 5.6 %collective-permute-start.15 = (bf16[16,768]{1,0:T(8,128)(2,1)S(1)}, bf16[16,768]{1,0:T(8,128)(2,1)S(1)}, u32[]{:S(2)}, u32[]{:S(2)}) collective-permute-start(bf16[16,768]{1,0:T(8,128)(2,1)S(1)} %fusion.8), channel_id=1, source_target_pairs={{0,2},{2,0},{1,3},{3,1},{4,6},{6,4},{5,7},{7,5},{8,10},{10,8},{9,1... | collective-permute-start | bytes 73736 | tf_op jit(solution)/shard_map/ppermute | solution.py:28
  103.1 2.8 %copy-start.4 = (bf16[16,768]{1,0:T(8,128)(2,1)S(1)}, bf16[16,768]{1,0:T(8,128)(2,1)}, u32[]{:S(2)}) copy-start(bf16[16,768]{1,0:T(8,128)(2,1)} %param.4) | copy-start | bytes 73732

commit v4 on v3

--- a/solution.py
+++ b/solution.py
@@ -142,7 +142,8 @@
 
 
 def err_of(logits, t, scale):
-    return ((jax.nn.sigmoid(logits) - t.astype(F32)) * scale).astype(BF16)
+    sigmoid = pl.reciprocal(1.0 + jnp.exp(-logits))
+    return ((sigmoid - t.astype(F32)) * scale).astype(BF16)
 
 
 def emb_rows(rows, hid, enc_w, emb, slope):

time: 113 us -> 114 us (level)
    ppermute x9, waiting for transfers between devices: 5.46 us -> 3.93 us  [swap(): return lax.ppermute(x, axis, [(0, 1), (1, 0)])]
  transfers between devices with their start and end apart: 21 -> 21, of which waited for: 10 -> 8; matrix products, arithmetic and copies ran while one was open for 6% -> 6% of each run, Pallas kernels for 28% -> 29%
where the time goes in v4:
time: 114 us; the launch traced here: 112 us
  starting transfers between devices  44.7 us (39%)
  Pallas kernels  39.1 us (34%)
  waiting for transfers between devices  18.3 us (16%)
  other arithmetic  4.09 us (4%)
  local copies, waits for them, and re-layouts  3.36 us (3%)
  matrix products  1.3 us (1%)
    pallas_call x8, Pallas kernels, kernel_call(): pl.pallas_call(kernel, out_shape=[o for _, o in outs], in_specs=[specs[p]...  39.1 us
    all_to_all x2, starting transfers between devices, spread(): lax.all_to_all(jnp.broadcast_to(x[None], (n,) + x.shape), axes, 0, 0, til...  16.8 us
    ppermute x6, starting transfers between devices, ring_pass(): lax.ppermute(pick(x, (me + k) % 4), axis, ring[k])  12.3 us
    all_to_all x2, waiting for transfers between devices, spread(): lax.all_to_all(jnp.broadcast_to(x[None], (n,) + x.shape), axes, 0, 0, til...  10.3 us
    ppermute x9, starting transfers between devices, swap(): return lax.ppermute(x, axis, [(0, 1), (1, 0)])  7.71 us
    ppermute x3, starting transfers between devices, x_sum(): lax.ppermute(x, ('xl', 'xh'), [(i, i ^ k) for i in range(4)])  4.2 us
    ppermute x9, waiting for transfers between devices, swap(): return lax.ppermute(x, axis, [(0, 1), (1, 0)])  3.93 us
    all_to_all x1, starting transfers between devices, body(): lax.all_to_all(enc.reshape(16, half // 16, width), PLANE, 0, 0, tiled=True)  3.73 us
  transfers between devices with their start and end apart: 21, of which 8 were waited for; matrix products, arithmetic and copies ran while one was open for 6% of the time, Pallas kernels for 29%

profile of v4, /device:TPU:0, one launch (start us, length us, event | category | flops | bytes accessed | tf_op | source)
XLA Modules:
  0.0 111.9 jit_solution(12881674864841179236)
XLA Ops:
  0.6 1.7 %broadcast_in_dim.46 = bf16[32,16,768]{2,1,0:T(8,128)(2,1)} broadcast(bf16[16,768]{1,0:T(8,128)(2,1)} %param.4), dimensions={1,2} | broadcast | bytes 811008 | tf_op jit(solution)/shard_map/broadcast_in_dim | solution.py:36
  2.3 10.9 %all-to-all-start = ((bf16[32,16,768]{2,1,0:T(8,128)(2,1)}), bf16[32,16,768]{2,1,0:T(8,128)(2,1)S(1)}, u32[]{:S(2)}, u32[]{:S(2)}) async-start(bf16[32,16,768]{2,1,0:T(8,128)(2,1)} %broadcast_in_dim.46), calls=%async_computation | async-start | bytes 1572864 | tf_op jit(solution)/shard_map/all_to_all | solution.py:36
  13.2 0.1 pad_add_fusion.at
  13.3 8.6 %shard_map.67 = bf16[64,16,3072]{2,1,0:T(8,128)(2,1)} custom-call(s32[2]{0:T(128)S(1)} %pad_add_fusion.at, s32[32,2,16,3072]{3,2,1,0:T(8,128)} %bitcast.50), custom_call_target="tpu_custom_call" | custom-call | flops 1024 | bytes 1024 | tf_op jit(solution)/shard_map/pallas_call | solution.py:65
  21.9 7.9 %all-to-all-done = bf16[32,16,768]{2,1,0:T(8,128)(2,1)S(1)} async-done(((bf16[32,16,768]{2,1,0:T(8,128)(2,1)}), bf16[32,16,768]{2,1,0:T(8,128)(2,1)S(1)}, u32[]{:S(2)}, u32[]{:S(2)}) %all-to-all-start) | async-done | bytes 786464 | tf_op jit(solution)/shard_map/all_to_all | solution.py:36
  29.7 2.4 %shard_map.68 = (bf16[1024,768]{1,0:T(8,128)(2,1)S(1)}, bf16[1024,768]{1,0:T(8,128)(2,1)S(1)}, bf16[768,1024]{1,0:T(8,128)(2,1)S(1)}, bf16[768,1024]{1,0:T(8,128...) custom-call(bf16[512,768]{1,0:T(8,128)(2,1)S(1)} %bitcast.46, bf16[768,768]{1,0:T(8,128)(2,1)S(1)} %copy-done, ...), custom_call_target="tpu_custom_call" | custom-call | flops 1024 | bytes 1024 | tf_op jit(solution)/shard_map/pallas_call | solution.py:65
  32.2 5.1 %shard_map.69 = (bf16[1024,768]{1,0:T(8,128)(2,1)S(1)}, bf16[1024,768]{1,0:T(8,128)(2,1)S(1)}, bf16[768,1024]{1,0:T(8,128)(2,1)S(1)}, bf16[768,1024]{1,0:T(8,128...) custom-call(s32[2]{0:T(128)S(1)} %pad_add_fusion.at, ...), custom_call_target="tpu_custom_call", output_to_operand_aliasing={{0}: (5, {}), {1}: (6, {}), {2}: (7, {}), {3}: (8, {}), {4}... | custom-call | flops 1024 | bytes 1024 | tf_op jit(solution)/shard_map/pallas_call | solution.py:65
  37.3 0.9 collective-permute-start.1
  38.1 15.2 %shard_map.70 = (bf16[384,768]{1,0:T(8,128)(2,1)S(1)}, bf16[384,768]{1,0:T(8,128)(2,1)S(1)}, bf16[384,3072]{1,0:T(8,128)(2,1)}, bf16[512,768]{1,0:T(8,128)(2,1)}...) custom-call(s32[2]{0:T(128)S(1)} %pad_add_fusion.at, ...), custom_call_target="tpu_custom_call", output_to_operand_aliasing={{2}: (8, {})} | custom-call | flops 1024 | bytes 1024 | tf_op jit(solution)/shard_map/pallas_call | solution.py:65
  53.3 0.3 collective-permute-start.5
  53.7 0.3 collective-permute-start.2
  53.9 1.4 %collective-permute-start.3 = (bf16[384,1024]{1,0:T(8,128)(2,1)}, bf16[384,1024]{1,0:T(8,128)(2,1)}, u32[]{:S(2)}, u32[]{:S(2)}) collective-permute-start(bf16[384,1024]{1,0:T(8,128)(2,1)} %get-tuple-element.70), channel_id=1, source_target_pairs={{0,64},{64,0},{1,65},{65,1},{2,66},{66,2},{3,67},{67,3},{4,68},{68... | collective-permute-start | bytes 2359304 | tf_op jit(solution)/shard_map/ppermute | solution.py:28
  55.4 1.2 %collective-permute-done.2.b = bf16[384,768]{1,0:T(8,128)(2,1)S(1)} collective-permute-done((bf16[384,768]{1,0:T(8,128)(2,1)S(1)}, bf16[384,768]{1,0:T(8,128)(2,1)S(1)}, u32[]{:S(2)}, u32[]{:S(2)}) %collective-permute-start.2) | collective-permute-done | bytes 589856 | tf_op jit(solution)/shard_map/ppermute | solution.py:28
  56.6 1.0 shard_map.71
  57.6 3.7 %all-to-all-start.1 = ((bf16[16,24,768]{2,1,0:T(8,128)(2,1)}), bf16[16,24,768]{2,1,0:T(8,128)(2,1)S(1)}, u32[]{:S(2)}, u32[]{:S(2)}) async-start(bf16[16,24,768]{2,1,0:T(8,128)(2,1)} %bitcast.52), calls=%async_computation.1 | async-start | bytes 1179648 | tf_op jit(solution)/shard_map/all_to_all | solution.py:358
  61.3 1.3 %add_convert_fusion = bf16[512,768]{1,0:T(8,128)(2,1)S(1)} fusion(bf16[512,768]{1,0:T(8,128)(2,1)} %collective-permute-done.5, bf16[512,768]{1,0:T(8,128)(2,1)S(1)} %copy-done.1), kind=kLoop, calls=%fused_computation | loop fusion | flops 1572864 | bytes 2359296 | tf_op jit(solution)/shard_map/convert_element_type | solution.py:363
  62.6 0.1 dynamic-slice_bitcast_fusion
  62.7 2.1 %collective-permute-start.6 = (bf16[128,768]{1,0:T(8,128)(2,1)S(1)}, bf16[128,768]{1,0:T(8,128)(2,1)S(1)}, u32[]{:S(2)}, u32[]{:S(2)}) collective-permute-start(bf16[128,768]{1,0:T(8,128)(2,1)S(1)} %get-tuple-element.96), channel_id=1, source_target_pairs={{0,16},{16,32},{32,48},{48,0},{1,17},{17,33},{33,49},{49,1},{2,18}... | collective-permute-start | bytes 589832 | tf_op jit(solution)/shard_map/ppermute | solution.py:46
  64.8 2.7 %collective-permute-start.7 = (bf16[128,768]{1,0:T(8,128)(2,1)S(1)}, bf16[128,768]{1,0:T(8,128)(2,1)S(1)}, u32[]{:S(2)}, u32[]{:S(2)}) collective-permute-start(bf16[128,768]{1,0:T(8,128)(2,1)S(1)} %get-tuple-element.95), channel_id=1, source_target_pairs={{0,32},{16,48},{32,0},{48,16},{1,33},{17,49},{33,1},{49,17},{2,34}... | collective-permute-start | bytes 589832 | tf_op jit(solution)/shard_map/ppermute | solution.py:46
  67.5 1.4 %collective-permute-start.8 = (bf16[128,768]{1,0:T(8,128)(2,1)S(1)}, bf16[128,768]{1,0:T(8,128)(2,1)S(1)}, u32[]{:S(2)}, u32[]{:S(2)}) collective-permute-start(bf16[128,768]{1,0:T(8,128)(2,1)S(1)} %get-tuple-element.94), channel_id=1, source_target_pairs={{0,48},{16,0},{32,16},{48,32},{1,49},{17,1},{33,17},{49,33},{2,50}... | collective-permute-start | bytes 589832 | tf_op jit(solution)/shard_map/ppermute | solution.py:46
  69.0 2.2 %shard_map.72.kept = bf16[384,3072]{1,0:T(8,128)(2,1)} custom-call(bf16[384,3072]{1,0:T(8,128)(2,1)} %get-tuple-element.69.kept, bf16[384,768]{1,0:T(8,128)(2,1)} %copy-done.3), custom_call_target="tpu_custom_call", output_to_operand_aliasing={{}: (0, {})} | custom-call | flops 1024 | bytes 1024 | tf_op jit(solution)/shard_map/pallas_call | solution.py:65
  71.2 2.7 %collective-permute-done.3.refs_0_ = bf16[384,1024]{1,0:T(8,128)(2,1)} collective-permute-done((bf16[384,1024]{1,0:T(8,128)(2,1)}, bf16[384,1024]{1,0:T(8,128)(2,1)}, u32[]{:S(2)}, u32[]{:S(2)}) %collective-permute-start.3) | collective-permute-done | bytes 786464 | tf_op jit(solution)/shard_map/ppermute | solution.py:28
  74.0 0.8 all-to-all-done.1
  74.8 0.1 reduce_sum.12
  74.9 1.3 %collective-permute-start.4 = (bf16[24,768]{1,0:T(8,128)(2,1)S(1)}, bf16[24,768]{1,0:T(8,128)(2,1)S(1)}, u32[]{:S(2)}, u32[]{:S(2)}) collective-permute-start(bf16[24,768]{1,0:T(8,128)(2,1)S(1)} %reduce_sum.12), channel_id=1, source_target_pairs={{0,2},{2,0},{64,66},{66,64},{1,3},{3,1},{65,67},{67,65},{4,6},{6,4... | collective-permute-start | bytes 110600 | tf_op jit(solution)/shard_map/ppermute | solution.py:54
  76.1 0.4 collective-permute-start.9
  76.5 2.6 %collective-permute-start.10 = (bf16[24,768]{1,0:T(8,128)(2,1)S(1)}, bf16[24,768]{1,0:T(8,128)(2,1)S(1)}, u32[]{:S(2)}, u32[]{:S(2)}) collective-permute-start(bf16[24,768]{1,0:T(8,128)(2,1)S(1)} %reduce_sum.12), channel_id=1, source_target_pairs={{0,66},{2,64},{64,2},{66,0},{1,67},{3,65},{65,3},{67,1},{4,70},{6,... | collective-permute-start | bytes 110600 | tf_op jit(solution)/shard_map/ppermute | solution.py:54
  79.1 1.3 %collective-permute-done.7 = bf16[128,768]{1,0:T(8,128)(2,1)S(1)} collective-permute-done((bf16[128,768]{1,0:T(8,128)(2,1)S(1)}, bf16[128,768]{1,0:T(8,128)(2,1)S(1)}, u32[]{:S(2)}, u32[]{:S(2)}) %collective-permute-start.7) | collective-permute-done | bytes 196640 | tf_op jit(solution)/shard_map/ppermute | solution.py:46
  80.4 0.0 collective-permute-done.4
  80.4 1.2 %collective-permute-done.10 = bf16[24,768]{1,0:T(8,128)(2,1)S(1)} collective-permute-done((bf16[24,768]{1,0:T(8,128)(2,1)S(1)}, bf16[24,768]{1,0:T(8,128)(2,1)S(1)}, u32[]{:S(2)}, u32[]{:S(2)}) %collective-permute-start.10) | collective-permute-done | bytes 36896 | tf_op jit(solution)/shard_map/ppermute | solution.py:54
  81.7 0.8 collective-permute-start.11
  82.5 0.9 broadcast_in_dim.47
  83.4 5.9 %all-to-all-start.2 = ((bf16[16,24,768]{2,1,0:T(8,128)(2,1)}), bf16[16,24,768]{2,1,0:T(8,128)(2,1)S(1)}, u32[]{:S(2)}, u32[]{:S(2)}) async-start(bf16[16,24,768]{2,1,0:T(8,128)(2,1)} %broadcast_in_dim.47), calls=%async_computation.2 | async-start | bytes 1179648 | tf_op jit(solution)/shard_map/all_to_all | solution.py:36
  89.3 0.1 add_convert_fusion.1
  89.5 0.6 dynamic-slice_bitcast_fusion.7
  90.1 1.9 %collective-permute-start.12 = (bf16[32,768]{1,0:T(8,128)(2,1)}, bf16[32,768]{1,0:T(8,128)(2,1)S(1)}, u32[]{:S(2)}, u32[]{:S(2)}) collective-permute-start(bf16[32,768]{1,0:T(8,128)(2,1)} %get-tuple-element.100), channel_id=1, source_target_pairs={{0,4},{4,8},{8,12},{12,0},{1,5},{5,9},{9,13},{13,1},{2,6},{6,10},{... | collective-permute-start | bytes 147464 | tf_op jit(solution)/shard_map/ppermute | solution.py:46
  92.0 2.7 %collective-permute-start.13 = (bf16[32,768]{1,0:T(8,128)(2,1)S(1)}, bf16[32,768]{1,0:T(8,128)(2,1)}, u32[]{:S(2)}, u32[]{:S(2)}) collective-permute-start(bf16[32,768]{1,0:T(8,128)(2,1)S(1)} %get-tuple-element.99), channel_id=1, source_target_pairs={{0,8},{4,12},{8,0},{12,4},{1,9},{5,13},{9,1},{13,5},{2,10},{6,14},... | collective-permute-start | bytes 147464 | tf_op jit(solution)/shard_map/ppermute | solution.py:46
  94.6 1.5 %collective-permute-start.14 = (bf16[32,768]{1,0:T(8,128)(2,1)S(1)}, bf16[32,768]{1,0:T(8,128)(2,1)}, u32[]{:S(2)}, u32[]{:S(2)}) collective-permute-start(bf16[32,768]{1,0:T(8,128)(2,1)S(1)} %get-tuple-element.98), channel_id=1, source_target_pairs={{0,12},{4,0},{8,4},{12,8},{1,13},{5,1},{9,5},{13,9},{2,14},{6,2},{... | collective-permute-start | bytes 147464 | tf_op jit(solution)/shard_map/ppermute | solution.py:46
  96.1 1.2 %collective-permute-start.17 = (bf16[384,512]{1,0:T(8,128)(2,1)}, bf16[384,512]{1,0:T(8,128)(2,1)S(1)}, u32[]{:S(2)}, u32[]{:S(2)}) collective-permute-start(bf16[384,512]{1,0:T(8,128)(2,1)} %get-tuple-element.92), channel_id=1, source_target_pairs={{0,64},{64,0},{1,65},{65,1},{2,66},{66,2},{3,67},{67,3},{4,68},{68... | collective-permute-start | bytes 1179656 | tf_op jit(solution)/shard_map/ppermute | solution.py:28
  97.3 2.5 %all-to-all-done.2 = bf16[16,24,768]{2,1,0:T(8,128)(2,1)S(1)} async-done(((bf16[16,24,768]{2,1,0:T(8,128)(2,1)}), bf16[16,24,768]{2,1,0:T(8,128)(2,1)S(1)}, u32[]{:S(2)}, u32[]{:S(2)}) %all-to-all-start.2) | async-done | bytes 589856 | tf_op jit(solution)/shard_map/all_to_all | solution.py:36
  99.8 0.6 collective-permute-done.13
  100.4 0.8 convert_add_fusion
  101.2 2.8 %collective-permute-start.15 = (bf16[16,768]{1,0:T(8,128)(2,1)S(1)}, bf16[16,768]{1,0:T(8,128)(2,1)S(1)}, u32[]{:S(2)}, u32[]{:S(2)}) collective-permute-start(bf16[16,768]{1,0:T(8,128)(2,1)S(1)} %fusion.8), channel_id=1, source_target_pairs={{0,2},{2,0},{1,3},{3,1},{4,6},{6,4},{5,7},{7,5},{8,10},{10,8},{9,1... | collective-permute-start | bytes 73736 | tf_op jit(solution)/shard_map/ppermute | solution.py:28
  104.0 0.1 broadcast_in_dim.48
  104.2 2.7 %shard_map.73.kept = bf16[384,3072]{1,0:T(8,128)(2,1)} custom-call(bf16[384,3072]{1,0:T(8,128)(2,1)} %shard_map.72.kept, bf16[384,1024]{1,0:T(8,128)(2,1)} %collective-permute-done.3.refs_0_, bf16[384,768]{1,0:T(8,128)(2,1)} %copy-done.2), custom_call_target="tpu_custom_call", output_to_operand_aliasing={{}: (0, {})} | custom-call | flops 1024 | bytes 1024 | tf_op jit(solution)/shard_map/pallas_call | solution.py:65
  106.9 1.3 %fusion.5 = bf16[16,768]{1,0:T(8,128)(2,1)} fusion(bf16[768,768]{1,0:T(8,128)(2,1)S(1)} %copy-done, bf16[16,768]{1,0:T(8,128)(2,1)S(1)} %copy-done.4, bf16[16,768]{1,0:T(8,128)(2,1)S(1)} %collective-permute-done.15, f32[2,16,768]{2,1,0:T(8,128)S(1)} %bitcast.57, s32[]{:T(128)S(6)} %select_n.79), kind=kOutput, calls=%fused_computation.9 | convolution fusion | flops 37871616 | bytes 2556928 | tf_op jit(solution)/shard_map/dot_general | solution.py:24
  108.2 1.6 %fusion = f32[768,768]{1,0:T(8,128)} fusion(pred[768]{0:T(1024)(128)(4,1)S(1)} %broadcast_in_dim.49, bf16[384,768]{1,0:T(8,128)(2,1)S(1)} %collective-permute-done.16, bf16[384,768]{1,0:T(8,128)(2,1)S(1)} %bitcast.54), kind=kLoop, calls=%fused_computation.2 | loop fusion | flops 1179648 | bytes 3539712 | tf_op jit(solution)/shard_map/convert_element_type | solution.py:371
  109.8 1.9 %shard_map.74 = bf16[384,3072]{1,0:T(8,128)(2,1)} custom-call(bf16[384,3072]{1,0:T(8,128)(2,1)} %shard_map.73.kept, bf16[384,512]{1,0:T(8,128)(2,1)S(1)} %collective-permute-done.17.refs_0_), custom_call_target="tpu_custom_call", output_to_operand_aliasing={{}: (0, {})} | custom-call | flops 1024 | bytes 1024 | tf_op jit(solution)/shard_map/pallas_call | solution.py:65
  (28 shorter events, 0.1 us)
Async XLA Ops:
  2.3 27.4 %all-to-all-start = ((bf16[32,16,768]{2,1,0:T(8,128)(2,1)}), bf16[32,16,768]{2,1,0:T(8,128)(2,1)S(1)}, u32[]{:S(2)}, u32[]{:S(2)}) async-start(bf16[32,16,768]{2,1,0:T(8,128)(2,1)} %broadcast_in_dim.46), calls=%async_computation | async-start | bytes 1572864 | tf_op jit(solution)/shard_map/all_to_all | solution.py:36
  13.3 16.5 %copy-start = (bf16[768,768]{1,0:T(8,128)(2,1)S(1)}, bf16[768,768]{1,0:T(8,128)(2,1)}, u32[]{:S(2)}) copy-start(bf16[768,768]{1,0:T(8,128)(2,1)} %enc_w.3) | copy-start | bytes 3538948
  29.7 2.5 %collective-permute-start = (bf16[32,16,768]{2,1,0:T(8,128)(2,1)S(1)}, bf16[32,16,768]{2,1,0:T(8,128)(2,1)S(1)}, u32[]{:S(2)}, u32[]{:S(2)}) collective-permute-start(bf16[32,16,768]{2,1,0:T(8,128)(2,1)S(1)} %all-to-all-done), channel_id=1, source_target_pairs={{0,1},{1,0},{2,3},{3,2},{4,5},{5,4},{6,7},{7,6},{8,9},{9,8},{10,11... | collective-permute-start | bytes 2359304 | tf_op jit(solution)/shard_map/ppermute | solution.py:28
  37.3 16.4 %collective-permute-start.1 = (bf16[384,768]{1,0:T(8,128)(2,1)}, bf16[384,768]{1,0:T(8,128)(2,1)S(1)}, u32[]{:S(2)}, u32[]{:S(2)}) collective-permute-start(bf16[384,768]{1,0:T(8,128)(2,1)} %get-tuple-element.67), channel_id=1, source_target_pairs={{0,64},{64,0},{1,65},{65,1},{2,66},{66,2},{3,67},{67,3},{4,68},{68... | collective-permute-start | bytes 1769480 | tf_op jit(solution)/shard_map/ppermute | solution.py:28
  53.3 7.9 %collective-permute-start.5 = (bf16[512,768]{1,0:T(8,128)(2,1)}, bf16[512,768]{1,0:T(8,128)(2,1)}, u32[]{:S(2)}, u32[]{:S(2)}) collective-permute-start(bf16[512,768]{1,0:T(8,128)(2,1)} %get-tuple-element.73), channel_id=1, source_target_pairs={{0,1},{1,0},{2,3},{3,2},{4,5},{5,4},{6,7},{7,6},{8,9},{9,8},{10,11... | collective-permute-start | bytes 2359304 | tf_op jit(solution)/shard_map/ppermute | solution.py:28
  53.7 8.9 %copy-start.3 = (bf16[384,768]{1,0:T(8,128)(2,1)}, bf16[384,768]{1,0:T(8,128)(2,1)S(1)}, u32[]{:S(2)}) copy-start(bf16[384,768]{1,0:T(8,128)(2,1)S(1)} %collective-permute-done.1.refs_0_) | copy-start | bytes 1769476
  53.7 2.9 %collective-permute-start.2 = (bf16[384,768]{1,0:T(8,128)(2,1)S(1)}, bf16[384,768]{1,0:T(8,128)(2,1)S(1)}, u32[]{:S(2)}, u32[]{:S(2)}) collective-permute-start(bf16[384,768]{1,0:T(8,128)(2,1)S(1)} %get-tuple-element.68), channel_id=1, source_target_pairs={{0,1},{1,0},{2,3},{3,2},{4,5},{5,4},{6,7},{7,6},{8,9},{9,8},{10,11... | collective-permute-start | bytes 1769480 | tf_op jit(solution)/shard_map/ppermute | solution.py:28
  53.9 20.0 %collective-permute-start.3 = (bf16[384,1024]{1,0:T(8,128)(2,1)}, bf16[384,1024]{1,0:T(8,128)(2,1)}, u32[]{:S(2)}, u32[]{:S(2)}) collective-permute-start(bf16[384,1024]{1,0:T(8,128)(2,1)} %get-tuple-element.70), channel_id=1, source_target_pairs={{0,64},{64,0},{1,65},{65,1},{2,66},{66,2},{3,67},{67,3},{4,68},{68... | collective-permute-start | bytes 2359304 | tf_op jit(solution)/shard_map/ppermute | solution.py:28
  57.5 3.8 %copy-start.1 = (bf16[512,768]{1,0:T(8,128)(2,1)S(1)}, bf16[512,768]{1,0:T(8,128)(2,1)}, u32[]{:S(2)}) copy-start(bf16[512,768]{1,0:T(8,128)(2,1)} %get-tuple-element.72) | copy-start | bytes 2359300
  57.6 17.2 %all-to-all-start.1 = ((bf16[16,24,768]{2,1,0:T(8,128)(2,1)}), bf16[16,24,768]{2,1,0:T(8,128)(2,1)S(1)}, u32[]{:S(2)}, u32[]{:S(2)}) async-start(bf16[16,24,768]{2,1,0:T(8,128)(2,1)} %bitcast.52), calls=%async_computation.1 | async-start | bytes 1179648 | tf_op jit(solution)/shard_map/all_to_all | solution.py:358
  62.7 13.8 %collective-permute-start.6 = (bf16[128,768]{1,0:T(8,128)(2,1)S(1)}, bf16[128,768]{1,0:T(8,128)(2,1)S(1)}, u32[]{:S(2)}, u32[]{:S(2)}) collective-permute-start(bf16[128,768]{1,0:T(8,128)(2,1)S(1)} %get-tuple-element.96), channel_id=1, source_target_pairs={{0,16},{16,32},{32,48},{48,0},{1,17},{17,33},{33,49},{49,1},{2,18}... | collective-permute-start | bytes 589832 | tf_op jit(solution)/shard_map/ppermute | solution.py:46
  64.8 15.6 %collective-permute-start.7 = (bf16[128,768]{1,0:T(8,128)(2,1)S(1)}, bf16[128,768]{1,0:T(8,128)(2,1)S(1)}, u32[]{:S(2)}, u32[]{:S(2)}) collective-permute-start(bf16[128,768]{1,0:T(8,128)(2,1)S(1)} %get-tuple-element.95), channel_id=1, source_target_pairs={{0,32},{16,48},{32,0},{48,16},{1,33},{17,49},{33,1},{49,17},{2,34}... | collective-permute-start | bytes 589832 | tf_op jit(solution)/shard_map/ppermute | solution.py:46
  67.5 12.9 %collective-permute-start.8 = (bf16[128,768]{1,0:T(8,128)(2,1)S(1)}, bf16[128,768]{1,0:T(8,128)(2,1)S(1)}, u32[]{:S(2)}, u32[]{:S(2)}) collective-permute-start(bf16[128,768]{1,0:T(8,128)(2,1)S(1)} %get-tuple-element.94), channel_id=1, source_target_pairs={{0,48},{16,0},{32,16},{48,32},{1,49},{17,1},{33,17},{49,33},{2,50}... | collective-permute-start | bytes 589832 | tf_op jit(solution)/shard_map/ppermute | solution.py:46
  74.9 5.5 %collective-permute-start.4 = (bf16[24,768]{1,0:T(8,128)(2,1)S(1)}, bf16[24,768]{1,0:T(8,128)(2,1)S(1)}, u32[]{:S(2)}, u32[]{:S(2)}) collective-permute-start(bf16[24,768]{1,0:T(8,128)(2,1)S(1)} %reduce_sum.12), channel_id=1, source_target_pairs={{0,2},{2,0},{64,66},{66,64},{1,3},{3,1},{65,67},{67,65},{4,6},{6,4... | collective-permute-start | bytes 110600 | tf_op jit(solution)/shard_map/ppermute | solution.py:54
  76.1 4.3 %collective-permute-start.9 = (bf16[24,768]{1,0:T(8,128)(2,1)S(1)}, bf16[24,768]{1,0:T(8,128)(2,1)S(1)}, u32[]{:S(2)}, u32[]{:S(2)}) collective-permute-start(bf16[24,768]{1,0:T(8,128)(2,1)S(1)} %reduce_sum.12), channel_id=1, source_target_pairs={{0,64},{2,66},{64,0},{66,2},{1,65},{3,67},{65,1},{67,3},{4,68},{6,... | collective-permute-start | bytes 110600 | tf_op jit(solution)/shard_map/ppermute | solution.py:54
  76.5 5.2 %collective-permute-start.10 = (bf16[24,768]{1,0:T(8,128)(2,1)S(1)}, bf16[24,768]{1,0:T(8,128)(2,1)S(1)}, u32[]{:S(2)}, u32[]{:S(2)}) collective-permute-start(bf16[24,768]{1,0:T(8,128)(2,1)S(1)} %reduce_sum.12), channel_id=1, source_target_pairs={{0,66},{2,64},{64,2},{66,0},{1,67},{3,65},{65,3},{67,1},{4,70},{6,... | collective-permute-start | bytes 110600 | tf_op jit(solution)/shard_map/ppermute | solution.py:54
  81.7 18.1 %collective-permute-start.11 = (bf16[384,768]{1,0:T(8,128)(2,1)}, bf16[384,768]{1,0:T(8,128)(2,1)S(1)}, u32[]{:S(2)}, u32[]{:S(2)}) collective-permute-start(bf16[384,768]{1,0:T(8,128)(2,1)} %get-tuple-element.79), channel_id=1, source_target_pairs={{0,64},{64,0},{1,65},{65,1},{2,66},{66,2},{3,67},{67,3},{4,68},{68... | collective-permute-start | bytes 1769480 | tf_op jit(solution)/shard_map/ppermute | solution.py:28
  83.4 16.3 %all-to-all-start.2 = ((bf16[16,24,768]{2,1,0:T(8,128)(2,1)}), bf16[16,24,768]{2,1,0:T(8,128)(2,1)S(1)}, u32[]{:S(2)}, u32[]{:S(2)}) async-start(bf16[16,24,768]{2,1,0:T(8,128)(2,1)} %broadcast_in_dim.47), calls=%async_computation.2 | async-start | bytes 1179648 | tf_op jit(solution)/shard_map/all_to_all | solution.py:36
  90.1 9.7 %collective-permute-start.12 = (bf16[32,768]{1,0:T(8,128)(2,1)}, bf16[32,768]{1,0:T(8,128)(2,1)S(1)}, u32[]{:S(2)}, u32[]{:S(2)}) collective-permute-start(bf16[32,768]{1,0:T(8,128)(2,1)} %get-tuple-element.100), channel_id=1, source_target_pairs={{0,4},{4,8},{8,12},{12,0},{1,5},{5,9},{9,13},{13,1},{2,6},{6,10},{... | collective-permute-start | bytes 147464 | tf_op jit(solution)/shard_map/ppermute | solution.py:46
  92.0 8.4 %collective-permute-start.13 = (bf16[32,768]{1,0:T(8,128)(2,1)S(1)}, bf16[32,768]{1,0:T(8,128)(2,1)}, u32[]{:S(2)}, u32[]{:S(2)}) collective-permute-start(bf16[32,768]{1,0:T(8,128)(2,1)S(1)} %get-tuple-element.99), channel_id=1, source_target_pairs={{0,8},{4,12},{8,0},{12,4},{1,9},{5,13},{9,1},{13,5},{2,10},{6,14},... | collective-permute-start | bytes 147464 | tf_op jit(solution)/shard_map/ppermute | solution.py:46
  94.6 5.7 %collective-permute-start.14 = (bf16[32,768]{1,0:T(8,128)(2,1)S(1)}, bf16[32,768]{1,0:T(8,128)(2,1)}, u32[]{:S(2)}, u32[]{:S(2)}) collective-permute-start(bf16[32,768]{1,0:T(8,128)(2,1)S(1)} %get-tuple-element.98), channel_id=1, source_target_pairs={{0,12},{4,0},{8,4},{12,8},{1,13},{5,1},{9,5},{13,9},{2,14},{6,2},{... | collective-permute-start | bytes 147464 | tf_op jit(solution)/shard_map/ppermute | solution.py:46
  96.1 13.7 %collective-permute-start.17 = (bf16[384,512]{1,0:T(8,128)(2,1)}, bf16[384,512]{1,0:T(8,128)(2,1)S(1)}, u32[]{:S(2)}, u32[]{:S(2)}) collective-permute-start(bf16[384,512]{1,0:T(8,128)(2,1)} %get-tuple-element.92), channel_id=1, source_target_pairs={{0,64},{64,0},{1,65},{65,1},{2,66},{66,2},{3,67},{67,3},{4,68},{68... | collective-permute-start | bytes 1179656 | tf_op jit(solution)/shard_map/ppermute | solution.py:28
  99.8 4.4 %copy-start.2 = (bf16[384,768]{1,0:T(8,128)(2,1)}, bf16[384,768]{1,0:T(8,128)(2,1)S(1)}, u32[]{:S(2)}) copy-start(bf16[384,768]{1,0:T(8,128)(2,1)S(1)} %collective-permute-done.11.refs_1_) | copy-start | bytes 1769476
  99.8 8.5 %collective-permute-start.16 = (bf16[384,768]{1,0:T(8,128)(2,1)S(1)}, bf16[384,768]{1,0:T(8,128)(2,1)S(1)}, u32[]{:S(2)}, u32[]{:S(2)}) collective-permute-start(bf16[384,768]{1,0:T(8,128)(2,1)S(1)} %bitcast.53), channel_id=1, source_target_pairs={{0,1},{1,0},{2,3},{3,2},{4,5},{5,4},{6,7},{7,6},{8,9},{9,8},{10,11... | collective-permute-start | bytes 1769480 | tf_op jit(solution)/shard_map/ppermute | solution.py:28
  101.2 5.6 %collective-permute-start.15 = (bf16[16,768]{1,0:T(8,128)(2,1)S(1)}, bf16[16,768]{1,0:T(8,128)(2,1)S(1)}, u32[]{:S(2)}, u32[]{:S(2)}) collective-permute-start(bf16[16,768]{1,0:T(8,128)(2,1)S(1)} %fusion.8), channel_id=1, source_target_pairs={{0,2},{2,0},{1,3},{3,1},{4,6},{6,4},{5,7},{7,5},{8,10},{10,8},{9,1... | collective-permute-start | bytes 73736 | tf_op jit(solution)/shard_map/ppermute | solution.py:28
  104.1 2.8 %copy-start.4 = (bf16[16,768]{1,0:T(8,128)(2,1)S(1)}, bf16[16,768]{1,0:T(8,128)(2,1)}, u32[]{:S(2)}) copy-start(bf16[16,768]{1,0:T(8,128)(2,1)} %param.4) | copy-start | bytes 73732

commit v5 on v4

--- a/solution.py
+++ b/solution.py
@@ -251,22 +251,32 @@
     copy.wait()
 
 
+def add_parts(sizes, direct):
+    step = TILE if direct else 2 * TILE
+    return [
+        (i, pl.ds(d, min(step, size - d)), pl.ds(sum(sizes[:i]) + d, min(step, size - d)))
+        for i, size in enumerate(sizes)
+        for d in range(0, size, step)
+    ]
+
+
 def add_kernel(start, sizes, direct, kept, *refs):
     n = len(sizes)
     come, (out, mine, theirs, sems) = refs[:n], refs[n:]
-    cuts = [pl.ds(sum(sizes[:i]), size) for i, size in enumerate(sizes)]
-    places = [pl.ds(start + sum(sizes[:i]), size) for i, size in enumerate(sizes)]
+    parts = add_parts(sizes, direct)
+    places = [pl.ds(start + cut.start, cut.size) for _, _, cut in parts]
     reads = []
-    for i, (cut, place) in enumerate(zip(cuts, places)):
-        reads.append(start_all([pltpu.make_async_copy(kept.at[:, place], mine.at[:, cut], sems.at[3 * i])]))
+    for k, (i, its, cut) in enumerate(parts):
+        reads.append(start_all([pltpu.make_async_copy(kept.at[:, places[k]], mine.at[:, cut], sems.at[3 * k])]))
         if not direct:
-            reads[i] += start_all([pltpu.make_async_copy(come[i], theirs.at[:, cut], sems.at[3 * i + 1])])
+            there = pltpu.make_async_copy(come[i].at[:, its], theirs.at[:, cut], sems.at[3 * k + 1])
+            reads[k] += start_all([there])
     writes = []
-    for i, (cut, place) in enumerate(zip(cuts, places)):
-        wait_all(reads[i])
-        more = come[i][...] if direct else theirs[:, cut]
+    for k, (i, its, cut) in enumerate(parts):
+        wait_all(reads[k])
+        more = come[i][:, its] if direct else theirs[:, cut]
         mine[:, cut] = (mine[:, cut].astype(F32) + more.astype(F32)).astype(BF16)
-        writes += start_all([pltpu.make_async_copy(mine.at[:, cut], out.at[:, place], sems.at[3 * i + 2])])
+        writes += start_all([pltpu.make_async_copy(mine.at[:, cut], out.at[:, places[k]], sems.at[3 * k + 2])])
     wait_all(writes)
 
 
@@ -282,7 +292,7 @@
         scratch=[
             pltpu.VMEM((half, sum(sizes)), BF16),
             pltpu.VMEM((half, max(size, 128)), BF16),
-            pltpu.SemaphoreType.DMA((3 * len(come),)),
+            pltpu.SemaphoreType.DMA((3 * len(add_parts(sizes, direct)),)),
         ],
         input_output_aliases={0: 0},
     )

time: 114 us -> 113 us (level)
  no operation moved by 1% of the time
where the time goes in v5:
time: 113 us; the launch traced here: 112 us
  starting transfers between devices  44.7 us (40%)
  Pallas kernels  38.8 us (34%)
  waiting for transfers between devices  18.4 us (16%)
  other arithmetic  4.09 us (4%)
  local copies, waits for them, and re-layouts  3.36 us (3%)
  matrix products  1.3 us (1%)
    pallas_call x8, Pallas kernels, kernel_call(): pl.pallas_call(kernel, out_shape=[o for _, o in outs], in_specs=[specs[p]...  38.8 us
    all_to_all x2, starting transfers between devices, spread(): lax.all_to_all(jnp.broadcast_to(x[None], (n,) + x.shape), axes, 0, 0, til...  16.8 us
    ppermute x6, starting transfers between devices, ring_pass(): lax.ppermute(pick(x, (me + k) % 4), axis, ring[k])  12.3 us
    all_to_all x2, waiting for transfers between devices, spread(): lax.all_to_all(jnp.broadcast_to(x[None], (n,) + x.shape), axes, 0, 0, til...  10.3 us
    ppermute x9, starting transfers between devices, swap(): return lax.ppermute(x, axis, [(0, 1), (1, 0)])  7.71 us
    ppermute x3, starting transfers between devices, x_sum(): lax.ppermute(x, ('xl', 'xh'), [(i, i ^ k) for i in range(4)])  4.2 us
    ppermute x9, waiting for transfers between devices, swap(): return lax.ppermute(x, axis, [(0, 1), (1, 0)])  4.09 us
    all_to_all x1, starting transfers between devices, body(): lax.all_to_all(enc.reshape(16, half // 16, width), PLANE, 0, 0, tiled=True)  3.73 us
  transfers between devices with their start and end apart: 21, of which 8 were waited for; matrix products, arithmetic and copies ran while one was open for 6% of the time, Pallas kernels for 29%

profile of v5, /device:TPU:0, one launch (start us, length us, event | category | flops | bytes accessed | tf_op | source)
XLA Modules:
  0.0 111.7 jit_solution(13562378973997392755)
XLA Ops:
  0.6 1.7 %broadcast_in_dim.46 = bf16[32,16,768]{2,1,0:T(8,128)(2,1)} broadcast(bf16[16,768]{1,0:T(8,128)(2,1)} %param.4), dimensions={1,2} | broadcast | bytes 811008 | tf_op jit(solution)/shard_map/broadcast_in_dim | solution.py:36
  2.3 10.9 %all-to-all-start = ((bf16[32,16,768]{2,1,0:T(8,128)(2,1)}), bf16[32,16,768]{2,1,0:T(8,128)(2,1)S(1)}, u32[]{:S(2)}, u32[]{:S(2)}) async-start(bf16[32,16,768]{2,1,0:T(8,128)(2,1)} %broadcast_in_dim.46), calls=%async_computation | async-start | bytes 1572864 | tf_op jit(solution)/shard_map/all_to_all | solution.py:36
  13.2 0.1 pad_add_fusion.at
  13.3 8.6 %shard_map.67 = bf16[64,16,3072]{2,1,0:T(8,128)(2,1)} custom-call(s32[2]{0:T(128)S(1)} %pad_add_fusion.at, s32[32,2,16,3072]{3,2,1,0:T(8,128)} %bitcast.50), custom_call_target="tpu_custom_call" | custom-call | flops 1024 | bytes 1024 | tf_op jit(solution)/shard_map/pallas_call | solution.py:65
  21.9 7.9 %all-to-all-done = bf16[32,16,768]{2,1,0:T(8,128)(2,1)S(1)} async-done(((bf16[32,16,768]{2,1,0:T(8,128)(2,1)}), bf16[32,16,768]{2,1,0:T(8,128)(2,1)S(1)}, u32[]{:S(2)}, u32[]{:S(2)}) %all-to-all-start) | async-done | bytes 786464 | tf_op jit(solution)/shard_map/all_to_all | solution.py:36
  29.7 2.4 %shard_map.68 = (bf16[1024,768]{1,0:T(8,128)(2,1)S(1)}, bf16[1024,768]{1,0:T(8,128)(2,1)S(1)}, bf16[768,1024]{1,0:T(8,128)(2,1)S(1)}, bf16[768,1024]{1,0:T(8,128...) custom-call(bf16[512,768]{1,0:T(8,128)(2,1)S(1)} %bitcast.46, bf16[768,768]{1,0:T(8,128)(2,1)S(1)} %copy-done, ...), custom_call_target="tpu_custom_call" | custom-call | flops 1024 | bytes 1024 | tf_op jit(solution)/shard_map/pallas_call | solution.py:65
  32.2 5.1 %shard_map.69 = (bf16[1024,768]{1,0:T(8,128)(2,1)S(1)}, bf16[1024,768]{1,0:T(8,128)(2,1)S(1)}, bf16[768,1024]{1,0:T(8,128)(2,1)S(1)}, bf16[768,1024]{1,0:T(8,128...) custom-call(s32[2]{0:T(128)S(1)} %pad_add_fusion.at, ...), custom_call_target="tpu_custom_call", output_to_operand_aliasing={{0}: (5, {}), {1}: (6, {}), {2}: (7, {}), {3}: (8, {}), {4}... | custom-call | flops 1024 | bytes 1024 | tf_op jit(solution)/shard_map/pallas_call | solution.py:65
  37.3 0.9 collective-permute-start.1
  38.1 15.2 %shard_map.70 = (bf16[384,768]{1,0:T(8,128)(2,1)S(1)}, bf16[384,768]{1,0:T(8,128)(2,1)S(1)}, bf16[384,3072]{1,0:T(8,128)(2,1)}, bf16[512,768]{1,0:T(8,128)(2,1)}...) custom-call(s32[2]{0:T(128)S(1)} %pad_add_fusion.at, ...), custom_call_target="tpu_custom_call", output_to_operand_aliasing={{2}: (8, {})} | custom-call | flops 1024 | bytes 1024 | tf_op jit(solution)/shard_map/pallas_call | solution.py:65
  53.3 0.3 collective-permute-start.5
  53.7 0.3 collective-permute-start.2
  53.9 1.4 %collective-permute-start.3 = (bf16[384,1024]{1,0:T(8,128)(2,1)}, bf16[384,1024]{1,0:T(8,128)(2,1)}, u32[]{:S(2)}, u32[]{:S(2)}) collective-permute-start(bf16[384,1024]{1,0:T(8,128)(2,1)} %get-tuple-element.70), channel_id=1, source_target_pairs={{0,64},{64,0},{1,65},{65,1},{2,66},{66,2},{3,67},{67,3},{4,68},{68... | collective-permute-start | bytes 2359304 | tf_op jit(solution)/shard_map/ppermute | solution.py:28
  55.4 1.2 %collective-permute-done.2.b = bf16[384,768]{1,0:T(8,128)(2,1)S(1)} collective-permute-done((bf16[384,768]{1,0:T(8,128)(2,1)S(1)}, bf16[384,768]{1,0:T(8,128)(2,1)S(1)}, u32[]{:S(2)}, u32[]{:S(2)}) %collective-permute-start.2) | collective-permute-done | bytes 589856 | tf_op jit(solution)/shard_map/ppermute | solution.py:28
  56.6 1.0 shard_map.71
  57.6 3.7 %all-to-all-start.1 = ((bf16[16,24,768]{2,1,0:T(8,128)(2,1)}), bf16[16,24,768]{2,1,0:T(8,128)(2,1)S(1)}, u32[]{:S(2)}, u32[]{:S(2)}) async-start(bf16[16,24,768]{2,1,0:T(8,128)(2,1)} %bitcast.52), calls=%async_computation.1 | async-start | bytes 1179648 | tf_op jit(solution)/shard_map/all_to_all | solution.py:368
  61.3 1.3 %add_convert_fusion = bf16[512,768]{1,0:T(8,128)(2,1)S(1)} fusion(bf16[512,768]{1,0:T(8,128)(2,1)} %collective-permute-done.5, bf16[512,768]{1,0:T(8,128)(2,1)S(1)} %copy-done.1), kind=kLoop, calls=%fused_computation | loop fusion | flops 1572864 | bytes 2359296 | tf_op jit(solution)/shard_map/convert_element_type | solution.py:373
  62.6 0.1 dynamic-slice_bitcast_fusion
  62.7 2.1 %collective-permute-start.6 = (bf16[128,768]{1,0:T(8,128)(2,1)S(1)}, bf16[128,768]{1,0:T(8,128)(2,1)S(1)}, u32[]{:S(2)}, u32[]{:S(2)}) collective-permute-start(bf16[128,768]{1,0:T(8,128)(2,1)S(1)} %get-tuple-element.96), channel_id=1, source_target_pairs={{0,16},{16,32},{32,48},{48,0},{1,17},{17,33},{33,49},{49,1},{2,18}... | collective-permute-start | bytes 589832 | tf_op jit(solution)/shard_map/ppermute | solution.py:46
  64.8 2.7 %collective-permute-start.7 = (bf16[128,768]{1,0:T(8,128)(2,1)S(1)}, bf16[128,768]{1,0:T(8,128)(2,1)S(1)}, u32[]{:S(2)}, u32[]{:S(2)}) collective-permute-start(bf16[128,768]{1,0:T(8,128)(2,1)S(1)} %get-tuple-element.95), channel_id=1, source_target_pairs={{0,32},{16,48},{32,0},{48,16},{1,33},{17,49},{33,1},{49,17},{2,34}... | collective-permute-start | bytes 589832 | tf_op jit(solution)/shard_map/ppermute | solution.py:46
  67.5 1.4 %collective-permute-start.8 = (bf16[128,768]{1,0:T(8,128)(2,1)S(1)}, bf16[128,768]{1,0:T(8,128)(2,1)S(1)}, u32[]{:S(2)}, u32[]{:S(2)}) collective-permute-start(bf16[128,768]{1,0:T(8,128)(2,1)S(1)} %get-tuple-element.94), channel_id=1, source_target_pairs={{0,48},{16,0},{32,16},{48,32},{1,49},{17,1},{33,17},{49,33},{2,50}... | collective-permute-start | bytes 589832 | tf_op jit(solution)/shard_map/ppermute | solution.py:46
  69.0 2.1 %shard_map.72.kept = bf16[384,3072]{1,0:T(8,128)(2,1)} custom-call(bf16[384,3072]{1,0:T(8,128)(2,1)} %get-tuple-element.69.kept, bf16[384,768]{1,0:T(8,128)(2,1)} %copy-done.3), custom_call_target="tpu_custom_call", output_to_operand_aliasing={{}: (0, {})} | custom-call | flops 1024 | bytes 1024 | tf_op jit(solution)/shard_map/pallas_call | solution.py:65
  71.1 2.9 %collective-permute-done.3.refs_0_ = bf16[384,1024]{1,0:T(8,128)(2,1)} collective-permute-done((bf16[384,1024]{1,0:T(8,128)(2,1)}, bf16[384,1024]{1,0:T(8,128)(2,1)}, u32[]{:S(2)}, u32[]{:S(2)}) %collective-permute-start.3) | collective-permute-done | bytes 786464 | tf_op jit(solution)/shard_map/ppermute | solution.py:28
  74.0 0.8 all-to-all-done.1
  74.8 0.1 reduce_sum.12
  74.9 1.3 %collective-permute-start.4 = (bf16[24,768]{1,0:T(8,128)(2,1)S(1)}, bf16[24,768]{1,0:T(8,128)(2,1)S(1)}, u32[]{:S(2)}, u32[]{:S(2)}) collective-permute-start(bf16[24,768]{1,0:T(8,128)(2,1)S(1)} %reduce_sum.12), channel_id=1, source_target_pairs={{0,2},{2,0},{64,66},{66,64},{1,3},{3,1},{65,67},{67,65},{4,6},{6,4... | collective-permute-start | bytes 110600 | tf_op jit(solution)/shard_map/ppermute | solution.py:54
  76.1 0.4 collective-permute-start.9
  76.5 2.6 %collective-permute-start.10 = (bf16[24,768]{1,0:T(8,128)(2,1)S(1)}, bf16[24,768]{1,0:T(8,128)(2,1)S(1)}, u32[]{:S(2)}, u32[]{:S(2)}) collective-permute-start(bf16[24,768]{1,0:T(8,128)(2,1)S(1)} %reduce_sum.12), channel_id=1, source_target_pairs={{0,66},{2,64},{64,2},{66,0},{1,67},{3,65},{65,3},{67,1},{4,70},{6,... | collective-permute-start | bytes 110600 | tf_op jit(solution)/shard_map/ppermute | solution.py:54
  79.1 1.3 %collective-permute-done.7 = bf16[128,768]{1,0:T(8,128)(2,1)S(1)} collective-permute-done((bf16[128,768]{1,0:T(8,128)(2,1)S(1)}, bf16[128,768]{1,0:T(8,128)(2,1)S(1)}, u32[]{:S(2)}, u32[]{:S(2)}) %collective-permute-start.7) | collective-permute-done | bytes 196640 | tf_op jit(solution)/shard_map/ppermute | solution.py:46
  80.4 0.0 collective-permute-done.4
  80.4 1.2 %collective-permute-done.10 = bf16[24,768]{1,0:T(8,128)(2,1)S(1)} collective-permute-done((bf16[24,768]{1,0:T(8,128)(2,1)S(1)}, bf16[24,768]{1,0:T(8,128)(2,1)S(1)}, u32[]{:S(2)}, u32[]{:S(2)}) %collective-permute-start.10) | collective-permute-done | bytes 36896 | tf_op jit(solution)/shard_map/ppermute | solution.py:54
  81.7 0.8 collective-permute-start.11
  82.5 0.9 broadcast_in_dim.47
  83.4 5.9 %all-to-all-start.2 = ((bf16[16,24,768]{2,1,0:T(8,128)(2,1)}), bf16[16,24,768]{2,1,0:T(8,128)(2,1)S(1)}, u32[]{:S(2)}, u32[]{:S(2)}) async-start(bf16[16,24,768]{2,1,0:T(8,128)(2,1)} %broadcast_in_dim.47), calls=%async_computation.2 | async-start | bytes 1179648 | tf_op jit(solution)/shard_map/all_to_all | solution.py:36
  89.3 0.1 add_convert_fusion.1
  89.5 0.6 dynamic-slice_bitcast_fusion.7
  90.1 1.9 %collective-permute-start.12 = (bf16[32,768]{1,0:T(8,128)(2,1)}, bf16[32,768]{1,0:T(8,128)(2,1)S(1)}, u32[]{:S(2)}, u32[]{:S(2)}) collective-permute-start(bf16[32,768]{1,0:T(8,128)(2,1)} %get-tuple-element.100), channel_id=1, source_target_pairs={{0,4},{4,8},{8,12},{12,0},{1,5},{5,9},{9,13},{13,1},{2,6},{6,10},{... | collective-permute-start | bytes 147464 | tf_op jit(solution)/shard_map/ppermute | solution.py:46
  92.0 2.7 %collective-permute-start.13 = (bf16[32,768]{1,0:T(8,128)(2,1)S(1)}, bf16[32,768]{1,0:T(8,128)(2,1)}, u32[]{:S(2)}, u32[]{:S(2)}) collective-permute-start(bf16[32,768]{1,0:T(8,128)(2,1)S(1)} %get-tuple-element.99), channel_id=1, source_target_pairs={{0,8},{4,12},{8,0},{12,4},{1,9},{5,13},{9,1},{13,5},{2,10},{6,14},... | collective-permute-start | bytes 147464 | tf_op jit(solution)/shard_map/ppermute | solution.py:46
  94.6 1.5 %collective-permute-start.14 = (bf16[32,768]{1,0:T(8,128)(2,1)S(1)}, bf16[32,768]{1,0:T(8,128)(2,1)}, u32[]{:S(2)}, u32[]{:S(2)}) collective-permute-start(bf16[32,768]{1,0:T(8,128)(2,1)S(1)} %get-tuple-element.98), channel_id=1, source_target_pairs={{0,12},{4,0},{8,4},{12,8},{1,13},{5,1},{9,5},{13,9},{2,14},{6,2},{... | collective-permute-start | bytes 147464 | tf_op jit(solution)/shard_map/ppermute | solution.py:46
  96.1 1.2 %collective-permute-start.17 = (bf16[384,512]{1,0:T(8,128)(2,1)}, bf16[384,512]{1,0:T(8,128)(2,1)S(1)}, u32[]{:S(2)}, u32[]{:S(2)}) collective-permute-start(bf16[384,512]{1,0:T(8,128)(2,1)} %get-tuple-element.92), channel_id=1, source_target_pairs={{0,64},{64,0},{1,65},{65,1},{2,66},{66,2},{3,67},{67,3},{4,68},{68... | collective-permute-start | bytes 1179656 | tf_op jit(solution)/shard_map/ppermute | solution.py:28
  97.3 2.5 %all-to-all-done.2 = bf16[16,24,768]{2,1,0:T(8,128)(2,1)S(1)} async-done(((bf16[16,24,768]{2,1,0:T(8,128)(2,1)}), bf16[16,24,768]{2,1,0:T(8,128)(2,1)S(1)}, u32[]{:S(2)}, u32[]{:S(2)}) %all-to-all-start.2) | async-done | bytes 589856 | tf_op jit(solution)/shard_map/all_to_all | solution.py:36
  99.8 0.6 collective-permute-done.13
  100.4 0.8 convert_add_fusion
  101.2 2.8 %collective-permute-start.15 = (bf16[16,768]{1,0:T(8,128)(2,1)S(1)}, bf16[16,768]{1,0:T(8,128)(2,1)S(1)}, u32[]{:S(2)}, u32[]{:S(2)}) collective-permute-start(bf16[16,768]{1,0:T(8,128)(2,1)S(1)} %fusion.8), channel_id=1, source_target_pairs={{0,2},{2,0},{1,3},{3,1},{4,6},{6,4},{5,7},{7,5},{8,10},{10,8},{9,1... | collective-permute-start | bytes 73736 | tf_op jit(solution)/shard_map/ppermute | solution.py:28
  104.0 0.1 broadcast_in_dim.48
  104.2 2.6 %shard_map.73.kept = bf16[384,3072]{1,0:T(8,128)(2,1)} custom-call(bf16[384,3072]{1,0:T(8,128)(2,1)} %shard_map.72.kept, bf16[384,1024]{1,0:T(8,128)(2,1)} %collective-permute-done.3.refs_0_, bf16[384,768]{1,0:T(8,128)(2,1)} %copy-done.2), custom_call_target="tpu_custom_call", output_to_operand_aliasing={{}: (0, {})} | custom-call | flops 1024 | bytes 1024 | tf_op jit(solution)/shard_map/pallas_call | solution.py:65
  106.8 1.3 %fusion.5 = bf16[16,768]{1,0:T(8,128)(2,1)} fusion(bf16[768,768]{1,0:T(8,128)(2,1)S(1)} %copy-done, bf16[16,768]{1,0:T(8,128)(2,1)S(1)} %copy-done.4, bf16[16,768]{1,0:T(8,128)(2,1)S(1)} %collective-permute-done.15, f32[2,16,768]{2,1,0:T(8,128)S(1)} %bitcast.57, s32[]{:T(128)S(6)} %select_n.79), kind=kOutput, calls=%fused_computation.9 | convolution fusion | flops 37871616 | bytes 2556928 | tf_op jit(solution)/shard_map/dot_general | solution.py:24
  108.1 1.6 %fusion = f32[768,768]{1,0:T(8,128)} fusion(pred[768]{0:T(1024)(128)(4,1)S(1)} %broadcast_in_dim.49, bf16[384,768]{1,0:T(8,128)(2,1)S(1)} %collective-permute-done.16, bf16[384,768]{1,0:T(8,128)(2,1)S(1)} %bitcast.54), kind=kLoop, calls=%fused_computation.2 | loop fusion | flops 1179648 | bytes 3539712 | tf_op jit(solution)/shard_map/convert_element_type | solution.py:381
  109.7 1.8 %shard_map.74 = bf16[384,3072]{1,0:T(8,128)(2,1)} custom-call(bf16[384,3072]{1,0:T(8,128)(2,1)} %shard_map.73.kept, bf16[384,512]{1,0:T(8,128)(2,1)S(1)} %collective-permute-done.17.refs_0_), custom_call_target="tpu_custom_call", output_to_operand_aliasing={{}: (0, {})} | custom-call | flops 1024 | bytes 1024 | tf_op jit(solution)/shard_map/pallas_call | solution.py:65
  (28 shorter events, 0.1 us)
Async XLA Ops:
  2.3 27.4 %all-to-all-start = ((bf16[32,16,768]{2,1,0:T(8,128)(2,1)}), bf16[32,16,768]{2,1,0:T(8,128)(2,1)S(1)}, u32[]{:S(2)}, u32[]{:S(2)}) async-start(bf16[32,16,768]{2,1,0:T(8,128)(2,1)} %broadcast_in_dim.46), calls=%async_computation | async-start | bytes 1572864 | tf_op jit(solution)/shard_map/all_to_all | solution.py:36
  13.3 16.5 %copy-start = (bf16[768,768]{1,0:T(8,128)(2,1)S(1)}, bf16[768,768]{1,0:T(8,128)(2,1)}, u32[]{:S(2)}) copy-start(bf16[768,768]{1,0:T(8,128)(2,1)} %enc_w.3) | copy-start | bytes 3538948
  29.7 2.5 %collective-permute-start = (bf16[32,16,768]{2,1,0:T(8,128)(2,1)S(1)}, bf16[32,16,768]{2,1,0:T(8,128)(2,1)S(1)}, u32[]{:S(2)}, u32[]{:S(2)}) collective-permute-start(bf16[32,16,768]{2,1,0:T(8,128)(2,1)S(1)} %all-to-all-done), channel_id=1, source_target_pairs={{0,1},{1,0},{2,3},{3,2},{4,5},{5,4},{6,7},{7,6},{8,9},{9,8},{10,11... | collective-permute-start | bytes 2359304 | tf_op jit(solution)/shard_map/ppermute | solution.py:28
  37.3 16.4 %collective-permute-start.1 = (bf16[384,768]{1,0:T(8,128)(2,1)}, bf16[384,768]{1,0:T(8,128)(2,1)S(1)}, u32[]{:S(2)}, u32[]{:S(2)}) collective-permute-start(bf16[384,768]{1,0:T(8,128)(2,1)} %get-tuple-element.67), channel_id=1, source_target_pairs={{0,64},{64,0},{1,65},{65,1},{2,66},{66,2},{3,67},{67,3},{4,68},{68... | collective-permute-start | bytes 1769480 | tf_op jit(solution)/shard_map/ppermute | solution.py:28
  53.3 7.9 %collective-permute-start.5 = (bf16[512,768]{1,0:T(8,128)(2,1)}, bf16[512,768]{1,0:T(8,128)(2,1)}, u32[]{:S(2)}, u32[]{:S(2)}) collective-permute-start(bf16[512,768]{1,0:T(8,128)(2,1)} %get-tuple-element.73), channel_id=1, source_target_pairs={{0,1},{1,0},{2,3},{3,2},{4,5},{5,4},{6,7},{7,6},{8,9},{9,8},{10,11... | collective-permute-start | bytes 2359304 | tf_op jit(solution)/shard_map/ppermute | solution.py:28
  53.7 8.9 %copy-start.3 = (bf16[384,768]{1,0:T(8,128)(2,1)}, bf16[384,768]{1,0:T(8,128)(2,1)S(1)}, u32[]{:S(2)}) copy-start(bf16[384,768]{1,0:T(8,128)(2,1)S(1)} %collective-permute-done.1.refs_0_) | copy-start | bytes 1769476
  53.7 2.9 %collective-permute-start.2 = (bf16[384,768]{1,0:T(8,128)(2,1)S(1)}, bf16[384,768]{1,0:T(8,128)(2,1)S(1)}, u32[]{:S(2)}, u32[]{:S(2)}) collective-permute-start(bf16[384,768]{1,0:T(8,128)(2,1)S(1)} %get-tuple-element.68), channel_id=1, source_target_pairs={{0,1},{1,0},{2,3},{3,2},{4,5},{5,4},{6,7},{7,6},{8,9},{9,8},{10,11... | collective-permute-start | bytes 1769480 | tf_op jit(solution)/shard_map/ppermute | solution.py:28
  53.9 20.0 %collective-permute-start.3 = (bf16[384,1024]{1,0:T(8,128)(2,1)}, bf16[384,1024]{1,0:T(8,128)(2,1)}, u32[]{:S(2)}, u32[]{:S(2)}) collective-permute-start(bf16[384,1024]{1,0:T(8,128)(2,1)} %get-tuple-element.70), channel_id=1, source_target_pairs={{0,64},{64,0},{1,65},{65,1},{2,66},{66,2},{3,67},{67,3},{4,68},{68... | collective-permute-start | bytes 2359304 | tf_op jit(solution)/shard_map/ppermute | solution.py:28
  57.5 3.8 %copy-start.1 = (bf16[512,768]{1,0:T(8,128)(2,1)S(1)}, bf16[512,768]{1,0:T(8,128)(2,1)}, u32[]{:S(2)}) copy-start(bf16[512,768]{1,0:T(8,128)(2,1)} %get-tuple-element.72) | copy-start | bytes 2359300
  57.6 17.2 %all-to-all-start.1 = ((bf16[16,24,768]{2,1,0:T(8,128)(2,1)}), bf16[16,24,768]{2,1,0:T(8,128)(2,1)S(1)}, u32[]{:S(2)}, u32[]{:S(2)}) async-start(bf16[16,24,768]{2,1,0:T(8,128)(2,1)} %bitcast.52), calls=%async_computation.1 | async-start | bytes 1179648 | tf_op jit(solution)/shard_map/all_to_all | solution.py:368
  62.7 13.8 %collective-permute-start.6 = (bf16[128,768]{1,0:T(8,128)(2,1)S(1)}, bf16[128,768]{1,0:T(8,128)(2,1)S(1)}, u32[]{:S(2)}, u32[]{:S(2)}) collective-permute-start(bf16[128,768]{1,0:T(8,128)(2,1)S(1)} %get-tuple-element.96), channel_id=1, source_target_pairs={{0,16},{16,32},{32,48},{48,0},{1,17},{17,33},{33,49},{49,1},{2,18}... | collective-permute-start | bytes 589832 | tf_op jit(solution)/shard_map/ppermute | solution.py:46
  64.8 15.6 %collective-permute-start.7 = (bf16[128,768]{1,0:T(8,128)(2,1)S(1)}, bf16[128,768]{1,0:T(8,128)(2,1)S(1)}, u32[]{:S(2)}, u32[]{:S(2)}) collective-permute-start(bf16[128,768]{1,0:T(8,128)(2,1)S(1)} %get-tuple-element.95), channel_id=1, source_target_pairs={{0,32},{16,48},{32,0},{48,16},{1,33},{17,49},{33,1},{49,17},{2,34}... | collective-permute-start | bytes 589832 | tf_op jit(solution)/shard_map/ppermute | solution.py:46
  67.5 12.9 %collective-permute-start.8 = (bf16[128,768]{1,0:T(8,128)(2,1)S(1)}, bf16[128,768]{1,0:T(8,128)(2,1)S(1)}, u32[]{:S(2)}, u32[]{:S(2)}) collective-permute-start(bf16[128,768]{1,0:T(8,128)(2,1)S(1)} %get-tuple-element.94), channel_id=1, source_target_pairs={{0,48},{16,0},{32,16},{48,32},{1,49},{17,1},{33,17},{49,33},{2,50}... | collective-permute-start | bytes 589832 | tf_op jit(solution)/shard_map/ppermute | solution.py:46
  74.9 5.5 %collective-permute-start.4 = (bf16[24,768]{1,0:T(8,128)(2,1)S(1)}, bf16[24,768]{1,0:T(8,128)(2,1)S(1)}, u32[]{:S(2)}, u32[]{:S(2)}) collective-permute-start(bf16[24,768]{1,0:T(8,128)(2,1)S(1)} %reduce_sum.12), channel_id=1, source_target_pairs={{0,2},{2,0},{64,66},{66,64},{1,3},{3,1},{65,67},{67,65},{4,6},{6,4... | collective-permute-start | bytes 110600 | tf_op jit(solution)/shard_map/ppermute | solution.py:54
  76.1 4.3 %collective-permute-start.9 = (bf16[24,768]{1,0:T(8,128)(2,1)S(1)}, bf16[24,768]{1,0:T(8,128)(2,1)S(1)}, u32[]{:S(2)}, u32[]{:S(2)}) collective-permute-start(bf16[24,768]{1,0:T(8,128)(2,1)S(1)} %reduce_sum.12), channel_id=1, source_target_pairs={{0,64},{2,66},{64,0},{66,2},{1,65},{3,67},{65,1},{67,3},{4,68},{6,... | collective-permute-start | bytes 110600 | tf_op jit(solution)/shard_map/ppermute | solution.py:54
  76.5 5.2 %collective-permute-start.10 = (bf16[24,768]{1,0:T(8,128)(2,1)S(1)}, bf16[24,768]{1,0:T(8,128)(2,1)S(1)}, u32[]{:S(2)}, u32[]{:S(2)}) collective-permute-start(bf16[24,768]{1,0:T(8,128)(2,1)S(1)} %reduce_sum.12), channel_id=1, source_target_pairs={{0,66},{2,64},{64,2},{66,0},{1,67},{3,65},{65,3},{67,1},{4,70},{6,... | collective-permute-start | bytes 110600 | tf_op jit(solution)/shard_map/ppermute | solution.py:54
  81.7 18.1 %collective-permute-start.11 = (bf16[384,768]{1,0:T(8,128)(2,1)}, bf16[384,768]{1,0:T(8,128)(2,1)S(1)}, u32[]{:S(2)}, u32[]{:S(2)}) collective-permute-start(bf16[384,768]{1,0:T(8,128)(2,1)} %get-tuple-element.79), channel_id=1, source_target_pairs={{0,64},{64,0},{1,65},{65,1},{2,66},{66,2},{3,67},{67,3},{4,68},{68... | collective-permute-start | bytes 1769480 | tf_op jit(solution)/shard_map/ppermute | solution.py:28
  83.4 16.3 %all-to-all-start.2 = ((bf16[16,24,768]{2,1,0:T(8,128)(2,1)}), bf16[16,24,768]{2,1,0:T(8,128)(2,1)S(1)}, u32[]{:S(2)}, u32[]{:S(2)}) async-start(bf16[16,24,768]{2,1,0:T(8,128)(2,1)} %broadcast_in_dim.47), calls=%async_computation.2 | async-start | bytes 1179648 | tf_op jit(solution)/shard_map/all_to_all | solution.py:36
  90.1 9.7 %collective-permute-start.12 = (bf16[32,768]{1,0:T(8,128)(2,1)}, bf16[32,768]{1,0:T(8,128)(2,1)S(1)}, u32[]{:S(2)}, u32[]{:S(2)}) collective-permute-start(bf16[32,768]{1,0:T(8,128)(2,1)} %get-tuple-element.100), channel_id=1, source_target_pairs={{0,4},{4,8},{8,12},{12,0},{1,5},{5,9},{9,13},{13,1},{2,6},{6,10},{... | collective-permute-start | bytes 147464 | tf_op jit(solution)/shard_map/ppermute | solution.py:46
  92.0 8.4 %collective-permute-start.13 = (bf16[32,768]{1,0:T(8,128)(2,1)S(1)}, bf16[32,768]{1,0:T(8,128)(2,1)}, u32[]{:S(2)}, u32[]{:S(2)}) collective-permute-start(bf16[32,768]{1,0:T(8,128)(2,1)S(1)} %get-tuple-element.99), channel_id=1, source_target_pairs={{0,8},{4,12},{8,0},{12,4},{1,9},{5,13},{9,1},{13,5},{2,10},{6,14},... | collective-permute-start | bytes 147464 | tf_op jit(solution)/shard_map/ppermute | solution.py:46
  94.6 5.7 %collective-permute-start.14 = (bf16[32,768]{1,0:T(8,128)(2,1)S(1)}, bf16[32,768]{1,0:T(8,128)(2,1)}, u32[]{:S(2)}, u32[]{:S(2)}) collective-permute-start(bf16[32,768]{1,0:T(8,128)(2,1)S(1)} %get-tuple-element.98), channel_id=1, source_target_pairs={{0,12},{4,0},{8,4},{12,8},{1,13},{5,1},{9,5},{13,9},{2,14},{6,2},{... | collective-permute-start | bytes 147464 | tf_op jit(solution)/shard_map/ppermute | solution.py:46
  96.1 13.6 %collective-permute-start.17 = (bf16[384,512]{1,0:T(8,128)(2,1)}, bf16[384,512]{1,0:T(8,128)(2,1)S(1)}, u32[]{:S(2)}, u32[]{:S(2)}) collective-permute-start(bf16[384,512]{1,0:T(8,128)(2,1)} %get-tuple-element.92), channel_id=1, source_target_pairs={{0,64},{64,0},{1,65},{65,1},{2,66},{66,2},{3,67},{67,3},{4,68},{68... | collective-permute-start | bytes 1179656 | tf_op jit(solution)/shard_map/ppermute | solution.py:28
  99.8 4.4 %copy-start.2 = (bf16[384,768]{1,0:T(8,128)(2,1)}, bf16[384,768]{1,0:T(8,128)(2,1)S(1)}, u32[]{:S(2)}) copy-start(bf16[384,768]{1,0:T(8,128)(2,1)S(1)} %collective-permute-done.11.refs_1_) | copy-start | bytes 1769476
  99.8 8.3 %collective-permute-start.16 = (bf16[384,768]{1,0:T(8,128)(2,1)S(1)}, bf16[384,768]{1,0:T(8,128)(2,1)S(1)}, u32[]{:S(2)}, u32[]{:S(2)}) collective-permute-start(bf16[384,768]{1,0:T(8,128)(2,1)S(1)} %bitcast.53), channel_id=1, source_target_pairs={{0,1},{1,0},{2,3},{3,2},{4,5},{5,4},{6,7},{7,6},{8,9},{9,8},{10,11... | collective-permute-start | bytes 1769480 | tf_op jit(solution)/shard_map/ppermute | solution.py:28
  101.2 5.5 %collective-permute-start.15 = (bf16[16,768]{1,0:T(8,128)(2,1)S(1)}, bf16[16,768]{1,0:T(8,128)(2,1)S(1)}, u32[]{:S(2)}, u32[]{:S(2)}) collective-permute-start(bf16[16,768]{1,0:T(8,128)(2,1)S(1)} %fusion.8), channel_id=1, source_target_pairs={{0,2},{2,0},{1,3},{3,1},{4,6},{6,4},{5,7},{7,5},{8,10},{10,8},{9,1... | collective-permute-start | bytes 73736 | tf_op jit(solution)/shard_map/ppermute | solution.py:28
  104.1 2.6 %copy-start.4 = (bf16[16,768]{1,0:T(8,128)(2,1)S(1)}, bf16[16,768]{1,0:T(8,128)(2,1)}, u32[]{:S(2)}) copy-start(bf16[16,768]{1,0:T(8,128)(2,1)} %param.4) | copy-start | bytes 73732
